TPU v7x, 32 devices: a whole 2x2x4 slice. The times are simulated.
32 devices in a mesh: shard: 8 (over y, x, core), context: 2 (over z_hi), tensor: 2 (over z_lo).
Axes of the slice: x: 2, y: 2, z: 4 (z_hi: 2, z_lo: 2; z = z_hi * 2 + z_lo), core: 2. Of those that a mesh axis runs over, the one named last changes fastest.
Arguments:
- hidden_in: bfloat16 [8192, 2048], P(('shard', 'context', 'tensor')), may hold values from -7 to 7
- cotangent: bfloat16 [8192, 2048], P(('shard', 'context', 'tensor')), may hold values from -6 to 6
- w_query: bfloat16 [2048, 2048], P('shard', ('context', 'tensor')), may hold values from -0.65 to 0.65
- w_key: bfloat16 [2048, 2048], P('shard', ('context', 'tensor')), may hold values from -0.9 to 0.9
- w_value: bfloat16 [2048, 2048], P('shard', ('context', 'tensor')), may hold values from -0.125 to 0.125
- w_out: bfloat16 [2048, 2048], P('shard', ('context', 'tensor')), may hold values from -1.42 to 1.42
- w_router: bfloat16 [2048, 16], P(('shard', 'context', 'tensor')), may hold values from -2.7 to 2.7
- norm_first: bfloat16 [2048], P(('shard', 'context', 'tensor')), may hold values from 0.25 to 1.75
- norm_second: bfloat16 [2048], P(('shard', 'context', 'tensor')), may hold values from 0.25 to 1.75
- query_gain: bfloat16 [2048], P(('shard', 'context', 'tensor')), may hold values from 0.45 to 6
- key_gain: bfloat16 [2048], P(('shard', 'context', 'tensor')), may hold values from 0.45 to 6
- w_gate: bfloat16 [16, 2048, 1024], P(('shard', 'context'), None, 'tensor'), may hold values from -0.125 to 0.125
- w_up: bfloat16 [16, 2048, 1024], P(('shard', 'context'), None, 'tensor'), may hold values from -0.125 to 0.125
- w_down: bfloat16 [16, 2048, 1024], P(('shard', 'context'), None, 'tensor'), may hold values from -2 to 2
- expert_ids: int32 [8192, 8], P(('shard', 'context', 'tensor')), may hold values from 0 to 15, all different within a row; in each aligned block of 256 rows (0 to 255, 256 to 511, ...) at most 160 rows name the same one
Outputs:
- block_output: bfloat16 [8192, 2048], P(('shard', 'context', 'tensor'))
- grad_input: float32 [8192, 2048], P(('shard', 'context', 'tensor'))
- grad_query: float32 [2048, 2048], P('shard', ('context', 'tensor'))
- grad_key: float32 [2048, 2048], P('shard', ('context', 'tensor'))
- grad_value: float32 [2048, 2048], P('shard', ('context', 'tensor'))
- grad_out: float32 [2048, 2048], P('shard', ('context', 'tensor'))
- grad_router: float32 [2048, 16], P(('shard', 'context', 'tensor'))
- grad_norm_first: float32 [2048], P(('shard', 'context', 'tensor'))
- grad_norm_second: float32 [2048], P(('shard', 'context', 'tensor'))
- grad_query_gain: float32 [2048], P(('shard', 'context', 'tensor'))
- grad_key_gain: float32 [2048], P(('shard', 'context', 'tensor'))
- grad_gate: float32 [16, 2048, 1024], P(('shard', 'context'), None, 'tensor')
- grad_up: float32 [16, 2048, 1024], P(('shard', 'context'), None, 'tensor')
- grad_down: float32 [16, 2048, 1024], P(('shard', 'context'), None, 'tensor')
Inputs may be any that keep to these rules, and one draw needn't show every extreme that they name: `expert_ids`: each row names 8 different experts. Within the rows of one device no expert is named by more than 160 rows, and in some device's rows one expert is named by exactly 160.
All inputs are finite; a program needn't handle non-finite values.
Results may differ from a plain program's by a relative error of at most 0.023.
Values may be sent and summed in bfloat16 or wider, within the bound.
No kernel may reach another device: no remote copies, remote signals or barrier semaphores. Data moves between devices by JAX's collectives and lax.ppermute only.
A program may use at most 256 MiB of HBM per device.

v0:
```python
import jax
import jax.numpy as jnp
from jax import lax
from jax.sharding import PartitionSpec as P

HDIM = 128
SEQ_LEN = 1024


EPSILON = 1e-05
MASKED = -1e30


def rms_scale(values, gain):
    factor = lax.rsqrt(jnp.mean(values * values, axis=-1, keepdims=True) + EPSILON)
    return (values * factor * gain, factor)


def rms_back(values, factor, gain, grad_out):
    scaled = grad_out * gain
    mean_term = jnp.mean(scaled * values, axis=-1, keepdims=True)
    grad_values = factor * scaled - values * (factor * factor * factor) * mean_term
    return (grad_values, jnp.sum(grad_out * values * factor, axis=0))


def rope_tables(positions, head_size):
    half_size = head_size // 2
    frequency = 10000.0 ** (-2.0 * jnp.arange(half_size, dtype=jnp.float32) / head_size)
    angles = positions.astype(jnp.float32)[:, None] * frequency[None, :]
    return (jnp.cos(angles)[:, None, :], jnp.sin(angles)[:, None, :])


def rotate(values, cosine_table, sine_table, direction):
    half_size = values.shape[-1] // 2
    first_half = values[..., :half_size]
    second_half = values[..., half_size:]
    return jnp.concatenate(
        [
            first_half * cosine_table - direction * second_half * sine_table,
            second_half * cosine_table + direction * first_half * sine_table,
        ],
        axis=-1,
    )


def contract_last(left, right):
    return lax.dot_general(
        left, right, (((1,), (1,)), ((), ())), preferred_element_type=jnp.float32
    )


def contract_first(left, right):
    return lax.dot_general(
        left, right, (((0,), (0,)), ((), ())), preferred_element_type=jnp.float32
    )


def block_scores(query_block, key_sequence, first_row):
    scores = jnp.einsum(
        "qhd,khd->hqk", query_block, key_sequence, preferred_element_type=jnp.float32
    ) * HDIM ** (-0.5)
    query_place = first_row + jnp.arange(query_block.shape[0], dtype=jnp.int32)
    key_place = jnp.arange(key_sequence.shape[0], dtype=jnp.int32)
    causal = query_place[:, None] >= key_place[None, :]
    return jnp.where(causal[None], scores, MASKED)


def block_place(block_index, block_rows):
    per_sequence = SEQ_LEN // block_rows
    return (block_index // per_sequence, block_index % per_sequence * block_rows)


def take_block(stacked, sequence, first_row, block_rows):
    return lax.dynamic_slice_in_dim(
        lax.dynamic_index_in_dim(stacked, sequence, 0, False), first_row, block_rows, 0
    )


def attend_forward(query_heads, key_heads, value_heads, block_rows):
    head_count = query_heads.shape[1] // HDIM
    sequences = query_heads.shape[0] // SEQ_LEN
    layout = (sequences, SEQ_LEN, head_count, HDIM)
    queries = query_heads.reshape(layout)
    key_vectors = key_heads.reshape(layout)
    value_vectors = value_heads.reshape(layout)

    def one_block(block_index):
        sequence, first_row = block_place(block_index, block_rows)
        query_block = take_block(queries, sequence, first_row, block_rows)
        key_sequence = lax.dynamic_index_in_dim(key_vectors, sequence, 0, False)
        value_sequence = lax.dynamic_index_in_dim(value_vectors, sequence, 0, False)
        scores = block_scores(query_block, key_sequence, first_row)
        maximum = jnp.max(scores, axis=-1, keepdims=True)
        weights = jnp.exp(scores - maximum)
        denominator = jnp.sum(weights, axis=-1, keepdims=True)
        attn_low = (weights / denominator).astype(jnp.bfloat16)
        output = jnp.einsum(
            "hqk,khd->qhd", attn_low, value_sequence, preferred_element_type=jnp.float32
        )
        return (output.astype(jnp.bfloat16), (maximum + jnp.log(denominator))[..., 0])

    block_total = sequences * (SEQ_LEN // block_rows)
    outputs, log_sums = lax.map(one_block, jnp.arange(block_total, dtype=jnp.int32))
    return (outputs.reshape(query_heads.shape), log_sums)


def attend_backward(query_heads, key_heads, value_heads, grad_heads, log_sums, block_rows):
    head_count = query_heads.shape[1] // HDIM
    sequences = query_heads.shape[0] // SEQ_LEN
    layout = (sequences, SEQ_LEN, head_count, HDIM)
    queries = query_heads.reshape(layout)
    key_vectors = key_heads.reshape(layout)
    value_vectors = value_heads.reshape(layout)
    grad_vectors = grad_heads.reshape(layout)
    score_scale = HDIM ** (-0.5)
    zero_grads = jnp.zeros(layout, jnp.float32)

    def one_block(grad_carry, inputs_pair):
        grad_keys, grad_values = grad_carry
        block_index, log_sum = inputs_pair
        sequence, first_row = block_place(block_index, block_rows)
        query_block = take_block(queries, sequence, first_row, block_rows)
        grad_block = take_block(grad_vectors, sequence, first_row, block_rows)
        key_sequence = lax.dynamic_index_in_dim(key_vectors, sequence, 0, False)
        value_sequence = lax.dynamic_index_in_dim(value_vectors, sequence, 0, False)
        scores = block_scores(query_block, key_sequence, first_row)
        attn_probs = jnp.exp(scores - log_sum[..., None])
        grad_probs = jnp.einsum(
            "qhd,khd->hqk", grad_block, value_sequence, preferred_element_type=jnp.float32
        )
        delta_term = jnp.sum(attn_probs * grad_probs, axis=-1, keepdims=True)
        grad_scores = (attn_probs * (grad_probs - delta_term)).astype(jnp.bfloat16)
        grad_query = (
            jnp.einsum(
                "hqk,khd->qhd", grad_scores, key_sequence, preferred_element_type=jnp.float32
            )
            * score_scale
        )
        key_part = (
            jnp.einsum("hqk,qhd->khd", grad_scores, query_block, preferred_element_type=jnp.float32)
            * score_scale
        )
        value_part = jnp.einsum(
            "hqk,qhd->khd",
            attn_probs.astype(jnp.bfloat16),
            grad_block,
            preferred_element_type=jnp.float32,
        )
        grad_keys = lax.dynamic_update_index_in_dim(
            grad_keys,
            lax.dynamic_index_in_dim(grad_keys, sequence, 0, False) + key_part,
            sequence,
            0,
        )
        grad_values = lax.dynamic_update_index_in_dim(
            grad_values,
            lax.dynamic_index_in_dim(grad_values, sequence, 0, False) + value_part,
            sequence,
            0,
        )
        return ((grad_keys, grad_values), grad_query.astype(jnp.bfloat16))

    block_total = sequences * (SEQ_LEN // block_rows)
    (grad_keys, grad_values), grad_queries = lax.scan(
        one_block, (zero_grads, zero_grads), (jnp.arange(block_total, dtype=jnp.int32), log_sums)
    )
    flat_shape = query_heads.shape
    return (
        grad_queries.reshape(flat_shape),
        grad_keys.astype(jnp.bfloat16).reshape(flat_shape),
        grad_values.astype(jnp.bfloat16).reshape(flat_shape),
    )


def move_slots(buffer):
    return lax.all_to_all(buffer, ("shard", "context"), split_axis=0, concat_axis=0, tiled=True)


def silu_parts(gate_act):
    sigmoid_value = jax.nn.sigmoid(gate_act)
    return (gate_act * sigmoid_value, sigmoid_value)


def expert_forward(arrived, w_gate, w_up, w_down):
    gate_full, up_full, down_full = (
        lax.all_gather(w_gate, "tensor", axis=2, tiled=True),
        lax.all_gather(w_up, "tensor", axis=2, tiled=True),
        lax.all_gather(w_down, "tensor", axis=2, tiled=True),
    )
    gate_weight, up_weight, down_weight = (gate_full[0], up_full[0], down_full[0])
    gate_act = jnp.dot(arrived, gate_weight, preferred_element_type=jnp.float32)
    up_act = jnp.dot(arrived, up_weight, preferred_element_type=jnp.float32)
    activated, sigmoid_value = silu_parts(gate_act)
    hidden_act = (activated * up_act).astype(jnp.bfloat16)
    produced = contract_last(hidden_act, down_weight)
    return (
        produced.astype(jnp.bfloat16),
        (arrived, gate_weight, up_weight, down_weight, gate_act, up_act, hidden_act),
    )


def expert_backward(arrived_grad, kept_state):
    rows_in, gate_weight, up_weight, down_weight, gate_act, up_act, hidden_act = kept_state
    grad_hidden = jnp.dot(arrived_grad, down_weight, preferred_element_type=jnp.float32)
    grad_down_weight = contract_first(arrived_grad, hidden_act)
    activated, sigmoid_value = silu_parts(gate_act)
    grad_gate_act = (
        grad_hidden * up_act * sigmoid_value * (1.0 + gate_act * (1.0 - sigmoid_value))
    ).astype(jnp.bfloat16)
    grad_up_act = (grad_hidden * activated).astype(jnp.bfloat16)
    grad_gate_weight = contract_first(rows_in, grad_gate_act)
    grad_up_weight = contract_first(rows_in, grad_up_act)
    grad_route = contract_last(grad_gate_act, gate_weight) + contract_last(grad_up_act, up_weight)
    owned_grads = (
        lax.psum_scatter(
            grad_gate_weight[None].astype(jnp.bfloat16), "tensor", scatter_dimension=2, tiled=True
        ).astype(jnp.float32),
        lax.psum_scatter(
            grad_up_weight[None].astype(jnp.bfloat16), "tensor", scatter_dimension=2, tiled=True
        ).astype(jnp.float32),
        lax.psum_scatter(
            grad_down_weight[None].astype(jnp.bfloat16), "tensor", scatter_dimension=2, tiled=True
        ).astype(jnp.float32),
    )
    return (grad_route.astype(jnp.bfloat16), owned_grads)


def unpack_small(router_part, first_part, second_part, query_part, key_part):
    return (
        router_part,
        first_part.astype(jnp.float32),
        second_part.astype(jnp.float32),
        query_part.astype(jnp.float32),
        key_part.astype(jnp.float32),
    )


def local(
    hidden_in,
    cotangent,
    w_query,
    w_key,
    w_value,
    w_out,
    w_router,
    norm_first,
    norm_second,
    query_gain,
    key_gain,
    w_gate,
    w_up,
    w_down,
    expert_ids,
):
    group_index = lax.axis_index(("context", "tensor"))
    inputs = hidden_in.astype(jnp.float32)
    row_count = inputs.shape[0]
    model_width = inputs.shape[1]
    column_span = w_query.shape[1]
    block_rows = min(512, SEQ_LEN)
    query_cols, key_cols, value_cols, out_cols = (
        lax.all_gather(w_query, "shard", axis=0, tiled=True),
        lax.all_gather(w_key, "shard", axis=0, tiled=True),
        lax.all_gather(w_value, "shard", axis=0, tiled=True),
        lax.all_gather(w_out, "shard", axis=0, tiled=True),
    )
    small_parts = (
        lax.all_gather(w_router, ("shard", "context", "tensor"), axis=0, tiled=True),
        lax.all_gather(norm_first, ("shard", "context", "tensor"), axis=0, tiled=True),
        lax.all_gather(norm_second, ("shard", "context", "tensor"), axis=0, tiled=True),
        lax.all_gather(query_gain, ("shard", "context", "tensor"), axis=0, tiled=True),
        lax.all_gather(key_gain, ("shard", "context", "tensor"), axis=0, tiled=True),
    )
    router_full, gain_first, gain_second, gain_query, gain_key = unpack_small(
        small_parts[0], small_parts[1], small_parts[2], small_parts[3], small_parts[4]
    )
    normed_first, factor_first = rms_scale(inputs, gain_first)
    low_first = normed_first.astype(jnp.bfloat16)
    low_group = lax.all_gather(low_first, ("context", "tensor"), axis=0, tiled=True)
    group_rows = low_group.shape[0]
    query_pre = jnp.dot(low_group, query_cols, preferred_element_type=jnp.float32)
    key_pre = jnp.dot(low_group, key_cols, preferred_element_type=jnp.float32)
    value_heads = jnp.dot(low_group, value_cols, preferred_element_type=jnp.float32).astype(
        jnp.bfloat16
    )
    query_square, key_square = lax.psum(
        (jnp.sum(query_pre * query_pre, axis=1), jnp.sum(key_pre * key_pre, axis=1)),
        ("context", "tensor"),
    )
    query_factor = lax.rsqrt(query_square / model_width + EPSILON)[:, None]
    key_factor = lax.rsqrt(key_square / model_width + EPSILON)[:, None]
    gain_query_cols = lax.dynamic_slice_in_dim(
        gain_query, group_index * column_span, column_span, 0
    )
    gain_key_cols = lax.dynamic_slice_in_dim(gain_key, group_index * column_span, column_span, 0)
    positions = jnp.arange(group_rows, dtype=jnp.int32) % SEQ_LEN
    cosine_table, sine_table = rope_tables(positions, HDIM)
    head_shape = (group_rows, column_span // HDIM, HDIM)
    query_heads = (
        rotate(
            (query_pre * query_factor * gain_query_cols).reshape(head_shape),
            cosine_table,
            sine_table,
            1.0,
        )
        .reshape(group_rows, column_span)
        .astype(jnp.bfloat16)
    )
    key_heads = (
        rotate(
            (key_pre * key_factor * gain_key_cols).reshape(head_shape),
            cosine_table,
            sine_table,
            1.0,
        )
        .reshape(group_rows, column_span)
        .astype(jnp.bfloat16)
    )
    attended_heads, log_sums = attend_forward(query_heads, key_heads, value_heads, block_rows)
    middle = inputs + lax.psum_scatter(
        contract_last(attended_heads, out_cols),
        ("context", "tensor"),
        scatter_dimension=0,
        tiled=True,
    )
    normed_second, factor_second = rms_scale(middle, gain_second)
    low_second = normed_second.astype(jnp.bfloat16)
    logits = jnp.dot(low_second, router_full, preferred_element_type=jnp.float32)
    maximum = jnp.max(logits, axis=-1, keepdims=True)
    weights = jnp.exp(logits - maximum)
    router_probs = weights / jnp.sum(weights, axis=-1, keepdims=True)
    expert_count = router_full.shape[1]
    top_count = expert_ids.shape[1]
    choose = expert_ids[:, :, None] == jnp.arange(expert_count, dtype=jnp.int32)[None, None, :]
    gate_probs = jnp.sum(jnp.where(choose, router_probs[:, None, :], 0.0), axis=2)
    capacity = max(2, row_count * top_count * 5 // (4 * expert_count))
    route_total = row_count * top_count
    flat_ids = expert_ids.reshape(-1)
    onehot = (flat_ids[:, None] == jnp.arange(expert_count, dtype=jnp.int32)[None, :]).astype(
        jnp.int32
    )
    before = jnp.cumsum(onehot, axis=0) - onehot
    route_slot = flat_ids * capacity + jnp.sum(before * onehot, axis=1)
    route_of_slot = (
        jnp.full((expert_count * capacity,), route_total, jnp.int32)
        .at[route_slot]
        .set(jnp.arange(route_total, dtype=jnp.int32))
    )
    filled = route_of_slot < route_total
    route_clipped = jnp.minimum(route_of_slot, route_total - 1)
    token_of_slot = route_clipped // top_count
    slot_shape = (expert_count, capacity, model_width)
    sending = jnp.where(filled[:, None], low_second[token_of_slot], jnp.zeros((), jnp.bfloat16))
    arrived = move_slots(sending.reshape(slot_shape)).reshape(expert_count * capacity, model_width)
    expert_out, kept_state = expert_forward(arrived, w_gate, w_up, w_down)
    returned = move_slots(expert_out.reshape(slot_shape)).reshape(
        expert_count * capacity, model_width
    )
    chosen = returned[route_slot].reshape(row_count, top_count, model_width).astype(jnp.float32)
    mixture = jnp.sum(gate_probs[:, :, None] * chosen, axis=1)
    block_output = (middle + mixture).astype(jnp.bfloat16)
    grad_top = cotangent.astype(jnp.float32)
    grad_gates = jnp.sum(chosen * grad_top[:, None, :], axis=2)
    slot_gate = jnp.where(filled, gate_probs.reshape(-1)[route_clipped], 0.0)
    sending_grad = (slot_gate[:, None] * grad_top[token_of_slot]).astype(jnp.bfloat16)
    arrived_grad = move_slots(sending_grad.reshape(slot_shape)).reshape(
        expert_count * capacity, model_width
    )
    grad_route, expert_grads = expert_backward(arrived_grad, kept_state)
    returned_grad = move_slots(grad_route.reshape(slot_shape)).reshape(
        expert_count * capacity, model_width
    )
    grad_from_experts = jnp.sum(
        returned_grad[route_slot].reshape(row_count, top_count, model_width).astype(jnp.float32),
        axis=1,
    )
    grad_router_probs = jnp.sum(jnp.where(choose, grad_gates[:, :, None], 0.0), axis=1)
    grad_logits = (
        router_probs
        * (grad_router_probs - jnp.sum(router_probs * grad_router_probs, axis=1, keepdims=True))
    ).astype(jnp.bfloat16)
    grad_router_weight = contract_first(low_second, grad_logits)
    grad_second = grad_from_experts + contract_last(grad_logits, router_full)
    grad_normed_second, grad_gain_second = rms_back(middle, factor_second, gain_second, grad_second)
    grad_middle = grad_top + grad_normed_second
    grad_branch = grad_middle.astype(jnp.bfloat16)
    piece = lax.all_gather(grad_branch, ("context", "tensor"), axis=0, tiled=True)
    out_total = contract_first(piece, attended_heads)
    grad_rows = jnp.dot(piece, out_cols, preferred_element_type=jnp.float32).astype(jnp.bfloat16)
    grad_query_heads, grad_key_heads, grad_value_heads = attend_backward(
        query_heads, key_heads, value_heads, grad_rows, log_sums, block_rows
    )
    grad_query_normed = rotate(
        grad_query_heads.astype(jnp.float32).reshape(head_shape), cosine_table, sine_table, -1.0
    ).reshape(group_rows, column_span)
    grad_key_normed = rotate(
        grad_key_heads.astype(jnp.float32).reshape(head_shape), cosine_table, sine_table, -1.0
    ).reshape(group_rows, column_span)
    query_scaled = grad_query_normed * gain_query_cols
    key_scaled = grad_key_normed * gain_key_cols
    query_total, key_total = lax.psum(
        (jnp.sum(query_scaled * query_pre, axis=1), jnp.sum(key_scaled * key_pre, axis=1)),
        ("context", "tensor"),
    )
    grad_query_low = (
        query_factor * query_scaled
        - query_pre
        * (query_factor * query_factor * query_factor)
        * (query_total / model_width)[:, None]
    ).astype(jnp.bfloat16)
    grad_key_low = (
        key_factor * key_scaled
        - key_pre * (key_factor * key_factor * key_factor) * (key_total / model_width)[:, None]
    ).astype(jnp.bfloat16)
    zero_gain = jnp.zeros((model_width,), jnp.float32)
    grad_gain_query = lax.dynamic_update_slice_in_dim(
        zero_gain,
        jnp.sum(grad_query_normed * query_pre * query_factor, axis=0),
        group_index * column_span,
        0,
    )
    grad_gain_key = lax.dynamic_update_slice_in_dim(
        zero_gain,
        jnp.sum(grad_key_normed * key_pre * key_factor, axis=0),
        group_index * column_span,
        0,
    )
    grad_query_cols = contract_first(low_group, grad_query_low)
    grad_key_cols = contract_first(low_group, grad_key_low)
    grad_value_cols = contract_first(low_group, grad_value_heads)
    grad_first = lax.psum_scatter(
        (
            contract_last(grad_query_low, query_cols)
            + contract_last(grad_key_low, key_cols)
            + contract_last(grad_value_heads, value_cols)
        ).astype(jnp.bfloat16),
        ("context", "tensor"),
        scatter_dimension=0,
        tiled=True,
    ).astype(jnp.float32)
    grad_normed_first, grad_gain_first = rms_back(inputs, factor_first, gain_first, grad_first)
    grad_input = grad_middle + grad_normed_first
    head_parts = (
        lax.psum_scatter(
            grad_query_cols.astype(jnp.bfloat16), "shard", scatter_dimension=0, tiled=True
        ).astype(jnp.float32),
        lax.psum_scatter(
            grad_key_cols.astype(jnp.bfloat16), "shard", scatter_dimension=0, tiled=True
        ).astype(jnp.float32),
        lax.psum_scatter(
            grad_value_cols.astype(jnp.bfloat16), "shard", scatter_dimension=0, tiled=True
        ).astype(jnp.float32),
        lax.psum_scatter(
            out_total.astype(jnp.bfloat16), "shard", scatter_dimension=0, tiled=True
        ).astype(jnp.float32),
    )
    small_grads = (
        lax.psum_scatter(
            grad_router_weight, ("shard", "context", "tensor"), scatter_dimension=0, tiled=True
        ),
        lax.psum_scatter(
            grad_gain_first, ("shard", "context", "tensor"), scatter_dimension=0, tiled=True
        ),
        lax.psum_scatter(
            grad_gain_second, ("shard", "context", "tensor"), scatter_dimension=0, tiled=True
        ),
        lax.psum_scatter(
            grad_gain_query, ("shard", "context", "tensor"), scatter_dimension=0, tiled=True
        ),
        lax.psum_scatter(
            grad_gain_key, ("shard", "context", "tensor"), scatter_dimension=0, tiled=True
        ),
    )
    finished = (
        head_parts[0],
        head_parts[1],
        head_parts[2],
        head_parts[3],
        small_grads[0],
        small_grads[1],
        small_grads[2],
        small_grads[3],
        small_grads[4],
    )
    return (
        block_output,
        grad_input,
        finished[0],
        finished[1],
        finished[2],
        finished[3],
        finished[4],
        finished[5],
        finished[6],
        finished[7],
        finished[8],
        expert_grads[0],
        expert_grads[1],
        expert_grads[2],
    )


def solution(mesh):
    placed = (
        P(("shard", "context", "tensor"), None),
        P(("shard", "context", "tensor"), None),
        P("shard", ("context", "tensor")),
        P("shard", ("context", "tensor")),
        P("shard", ("context", "tensor")),
        P("shard", ("context", "tensor")),
        P(("shard", "context", "tensor"), None),
        P(("shard", "context", "tensor")),
        P(("shard", "context", "tensor")),
        P(("shard", "context", "tensor")),
        P(("shard", "context", "tensor")),
        P(("shard", "context"), None, "tensor"),
        P(("shard", "context"), None, "tensor"),
        P(("shard", "context"), None, "tensor"),
        P(("shard", "context", "tensor"), None),
    )
    return jax.shard_map(
        local,
        mesh=mesh,
        in_specs=placed,
        out_specs=(
            P(("shard", "context", "tensor"), None),
            P(("shard", "context", "tensor"), None),
            P("shard", ("context", "tensor")),
            P("shard", ("context", "tensor")),
            P("shard", ("context", "tensor")),
            P("shard", ("context", "tensor")),
            P(("shard", "context", "tensor"), None),
            P(("shard", "context", "tensor")),
            P(("shard", "context", "tensor")),
            P(("shard", "context", "tensor")),
            P(("shard", "context", "tensor")),
            P(("shard", "context"), None, "tensor"),
            P(("shard", "context"), None, "tensor"),
            P(("shard", "context"), None, "tensor"),
        ),
        check_vma=False,
    )
```

profile of v0, /device:TPU:0, one launch (start us, length us, event | category | flops | bytes accessed | tf_op | source)
XLA Modules:
  0.0 2186.5 jit_solution(2722312540611688599)
XLA Ops:
  12.2 42.3 %all-reduce.11 = (bf16[2048]{0:T(1024)(128)(2,1)S(1)}, bf16[2048]{0:T(1024)(128)(2,1)S(1)}, bf16[2048]{0:T(1024)(128)(2,1)S(1)}, bf16[2048]{0:T(1024)(128)(2,1)S(1)}) all-reduce(bf16[2048]{0:T(1024)(128)(2,1)S(1)} %dynamic-update-slice, ...), channel_id=1, replica_groups=mesh['shard'=8,'context'=2,'tensor'=2] {'shard','context','tensor'}, use_global_device_ids=true, to_apply=%add | all-reduce | flops 8192 | bytes 32768
  63.6 75.7 %all-gather.11.cloned.1.call-done = bf16[1024,2048]{1,0:T(8,128)(2,1)} async-done(((bf16[256,2048]{1,0:T(8,128)(2,1)}), bf16[1024,2048]{1,0:T(8,128)(2,1)}) %all-gather.11.cloned.1.call-update) | async-done | bytes 4194320 | tf_op jit(solution)/shard_map/all_gather | solution.py:279
  144.6 23.1 %all-gather.15.cloned.1.call-done = bf16[2048,512]{1,0:T(8,128)(2,1)} async-done(((bf16[256,512]{1,0:T(8,128)(2,1)}), bf16[2048,512]{1,0:T(8,128)(2,1)}) %all-gather.15.cloned.1.call-update) | async-done | bytes 2097168 | tf_op jit(solution)/shard_map/all_gather | solution.py:263
  167.7 6.6 multiply_reduce_fusion.6
  174.2 12.0 all-reduce.10
  198.3 6.2 convolution_convert_fusion.6
  212.0 23.1 %while.30 = (s32[]{:T(128)}, bf16[2,512,4,128]{3,2,1,0:T(4,128)(2,1)}, f32[2,4,512]{2,1,0:T(4,128)S(1)}, s32[2]{0:T(128)S(1)}, bf16[1,1024,4,128]{3,1,2,0:T(8,12...) while((s32[]{:T(128)}, ...), condition=%wide.region_8.9_spmd, body=%wide.region_5.8_spmd.sunk | while | flops 1099692544 | bytes 35722052 | solution.py:103
  235.2 8.4 fusion.78
  244.7 72.1 %all-gather = bf16[32,64,16]{1,2,0:T(8,128)(2,1)S(1)} all-gather(bf16[1,64,16]{1,2,0:T(8,128)(2,1)S(1)} %bitcast.286), channel_id=1, replica_groups=mesh['shard'=8,'context'=2,'tensor'=2] {'shard','context','tensor'}, dimensions={0}, use_global_device_ids=true | all-gather | bytes 67584 | tf_op jit(solution)/shard_map/all_gather | solution.py:268
  322.7 8.5 scatter_custom_fusion
  331.3 58.7 %reduce-scatter.13.cloned.1.call-done = f32[256,2048]{1,0:T(8,128)} async-done(((f32[1024,2048]{1,0:T(8,128)}), f32[256,2048]{1,0:T(8,128)}) %reduce-scatter.13.cloned.1.call-update) | async-done | bytes 2097168 | tf_op jit(solution)/shard_map/reduce_scatter | solution.py:320
  394.7 13.6 gather_fusion.2
  408.4 10.7 gather_fusion
  419.2 10.0 broadcast_select_fusion
  429.2 6.4 all-to-all-start
  435.8 12.4 gather_fusion.3
  448.3 12.2 multiply_convert_fusion.1
  460.5 204.6 %all-to-all-done = bf16[16,160,2048]{2,1,0:T(8,128)(2,1)} async-done(((bf16[16,160,2048]{2,1,0:T(8,128)(2,1)}), bf16[16,160,2048]{2,1,0:T(8,128)(2,1)}, u32[]{:S(2)}, u32[]{:S(2)}) %all-to-all-start) | async-done | bytes 10485792 | tf_op jit(solution)/shard_map/all_to_all | solution.py:176
  671.7 100.0 %all-gather.23.cloned.1.call-done = bf16[1,2048,1024]{2,1,0:T(8,128)(2,1)} async-done(((bf16[1,2048,512]{2,1,0:T(8,128)(2,1)}), bf16[1,2048,1024]{2,1,0:T(8,128)(2,1)}) %all-gather.23.cloned.1.call-update) | async-done | bytes 4194320 | tf_op jit(solution)/shard_map/all_gather | solution.py:187
  771.7 16.4 fusion.53
  788.1 111.2 %all-gather.21.cloned.1.call-done = bf16[1,2048,1024]{2,1,0:T(8,128)(2,1)} async-done(((bf16[1,2048,512]{2,1,0:T(8,128)(2,1)}), bf16[1,2048,1024]{2,1,0:T(8,128)(2,1)}) %all-gather.21.cloned.1.call-update) | async-done | bytes 4194320 | tf_op jit(solution)/shard_map/all_gather | solution.py:186
  899.3 16.5 fusion.57
  915.8 39.7 %all-gather.25.cloned.1.call-done = bf16[1,2048,1024]{2,1,0:T(8,128)(2,1)} async-done(((bf16[1,2048,512]{2,1,0:T(8,128)(2,1)}), bf16[1,2048,1024]{2,1,0:T(8,128)(2,1)}) %all-gather.25.cloned.1.call-update) | async-done | bytes 4194320 | tf_op jit(solution)/shard_map/all_gather | solution.py:188
  955.5 26.9 %multiply_convert_fusion.2 = (bf16[2560,1024]{1,0:T(8,128)(2,1)}, bf16[2560,1024]{1,0:T(8,128)(2,1)}, bf16[2560,1024]{1,0:T(8,128)(2,1)}) fusion(f32[2560,1024]{1,0:T(8,128)} %fusion.57, f32[2560,1024]{1,0:T(8,128)} %fusion.53, bf16[2560,2048]{1,0:T(8,128)(2,1)} %bitcast.41, bf16[1,2048,1024]{2,1,0:T(8,128)(2,1)} %all-gather.25.cloned.1.call-done), kind=kOutput, calls=%fused_computation.73 | convolution fusion | flops 10776739840 | bytes 51380224 | tf_op jit(solution)/shard_map/dot_general | solution.py:204
  982.4 16.9 convolution_convert_fusion
  1005.3 18.3 fusion.55
  1023.6 19.8 add_convert_fusion
  1043.4 191.6 %all-to-all-done.1 = bf16[16,160,2048]{2,1,0:T(8,128)(2,1)} async-done(((bf16[16,160,2048]{2,1,0:T(8,128)(2,1)}), bf16[16,160,2048]{2,1,0:T(8,128)(2,1)}, u32[]{:S(2)}, u32[]{:S(2)}) %all-to-all-start.1) | async-done | bytes 10485792 | tf_op jit(solution)/shard_map/all_to_all | solution.py:176
  1240.1 22.0 %gather_fusion.1 = bf16[2048,2048]{1,0:T(8,128)(2,1)} fusion(bf16[2560,2048]{1,0:T(8,128)(2,1)} %bitcast.38, s32[2048]{0:T(1024)S(1)} %broadcast_clamp_fusion), kind=kCustom, calls=%fused_computation.1 | custom fusion | bytes 16785408 | tf_op jit(solution)/shard_map/gather | solution.py:359
  1262.1 9.5 fusion.47
  1271.8 196.2 %all-to-all-done.3 = bf16[16,160,2048]{2,1,0:T(8,128)(2,1)} async-done(((bf16[16,160,2048]{2,1,0:T(8,128)(2,1)}), bf16[16,160,2048]{2,1,0:T(8,128)(2,1)}, u32[]{:S(2)}, u32[]{:S(2)}) %all-to-all-start.3) | async-done | bytes 10485792 | tf_op jit(solution)/shard_map/all_to_all | solution.py:176
  1468.0 21.7 gather_fusion.4
  1489.7 11.4 convert_reduce_fusion
  1507.3 17.1 convert_bitcast_fusion
  1524.4 17.4 convert_bitcast_fusion.2
  1541.9 17.2 convert_bitcast_fusion.1
  1562.0 66.7 %all-gather.27.cloned.1.call-done = bf16[1024,2048]{1,0:T(8,128)(2,1)} async-done(((bf16[256,2048]{1,0:T(8,128)(2,1)}), bf16[1024,2048]{1,0:T(8,128)(2,1)}) %all-gather.27.cloned.1.call-update) | async-done | bytes 4194320 | tf_op jit(solution)/shard_map/all_gather | solution.py:387
  1628.6 6.2 convolution_convert_fusion.5
  1636.7 41.1 %while.31 = (s32[]{:T(128)}, f32[1,1024,4,128]{1,3,2,0:T(8,128)S(1)}, f32[1,1024,4,128]{1,3,2,0:T(8,128)}, bf16[2,512,4,128]{3,1,0,2:T(8,128)(2,1)}, s32[2]{0:T(...) while((s32[]{:T(128)}, ...), condition=%wide.region_26.27_spmd, body=%wide.region_24.26_spmd.sunk | while | flops 2718431744 | bytes 100200920 | solution.py:164
  1698.9 11.0 all-reduce.9
  1725.1 6.2 convolution_convert_fusion.1
  1764.7 111.2 %reduce-scatter.31.cloned.1.call-done = f32[64,16]{1,0:T(8,128)} async-done(((f32[2048,16]{1,0:T(8,128)}), f32[64,16]{1,0:T(8,128)}) %reduce-scatter.31.cloned.1.call-update) | async-done | bytes 4112
  1877.8 38.9 %reduce-scatter.19.cloned.1.call-done = bf16[256,512]{1,0:T(8,128)(2,1)} async-done(((bf16[2048,512]{1,0:T(8,128)(2,1)}), bf16[256,512]{1,0:T(8,128)(2,1)}) %reduce-scatter.19.cloned.1.call-update) | async-done | bytes 262160 | tf_op jit(solution)/shard_map/reduce_scatter | solution.py:447
  1918.6 43.4 %reduce-scatter.17.cloned.1.call-done = bf16[256,512]{1,0:T(8,128)(2,1)} async-done(((bf16[2048,512]{1,0:T(8,128)(2,1)}), bf16[256,512]{1,0:T(8,128)(2,1)}) %reduce-scatter.17.cloned.1.call-update) | async-done | bytes 262160 | tf_op jit(solution)/shard_map/reduce_scatter | solution.py:444
  1963.8 42.7 %reduce-scatter.23.cloned.1.call-done = bf16[256,512]{1,0:T(8,128)(2,1)} async-done(((bf16[2048,512]{1,0:T(8,128)(2,1)}), bf16[256,512]{1,0:T(8,128)(2,1)}) %reduce-scatter.23.cloned.1.call-update) | async-done | bytes 262160 | tf_op jit(solution)/shard_map/reduce_scatter | solution.py:453
  2008.2 42.8 %reduce-scatter.21.cloned.1.call-done = bf16[256,512]{1,0:T(8,128)(2,1)} async-done(((bf16[2048,512]{1,0:T(8,128)(2,1)}), bf16[256,512]{1,0:T(8,128)(2,1)}) %reduce-scatter.21.cloned.1.call-update) | async-done | bytes 262160 | tf_op jit(solution)/shard_map/reduce_scatter | solution.py:450
  2052.8 77.3 %reduce-scatter.15.cloned.1.call-done = bf16[256,2048]{1,0:T(8,128)(2,1)} async-done(((bf16[1024,2048]{1,0:T(8,128)(2,1)}), bf16[256,2048]{1,0:T(8,128)(2,1)}) %reduce-scatter.15.cloned.1.call-update) | async-done | bytes 1048592 | tf_op jit(solution)/shard_map/reduce_scatter | solution.py:431
  2132.0 41.1 %all-reduce.8 = (f32[2048]{0:T(1024)S(1)}, f32[2048]{0:T(1024)S(1)}, f32[2048]{0:T(1024)S(1)}, f32[2048]{0:T(1024)S(1)}) all-reduce(f32[2048]{0:T(1024)S(1)} %get-tuple-element.331, f32[2048]{0:T(1024)S(1)} %copy-done.57, ...), channel_id=9, replica_groups=mesh['shard'=8,'context'=2,'tensor'=2] {'shard','context','tensor'}, use_global_device_ids=true, to_apply=%region_39.40.clone | all-reduce | flops 8192 | bytes 65536
  (367 shorter events, 220.3 us)
Async XLA Ops:
  8.0 49.2 %copy-start.13 = (bf16[256,2048]{1,0:T(8,128)(2,1)S(1)}, bf16[256,2048]{1,0:T(8,128)(2,1)}, u32[]{:S(2)}) copy-start(bf16[256,2048]{1,0:T(8,128)(2,1)} %param.19) | copy-start | bytes 3145732
  8.0 55.6 %all-gather.13.cloned.1.call-start = ((), (), s32[]{:S(2)}) async-start(), calls=%async_computation.15 | async-start | bytes 2359296 | tf_op jit(solution)/shard_map/all_gather | solution.py:262
  8.8 130.5 %all-gather.11.cloned.1.call-start = ((), (), s32[]{:S(2)}) async-start(), calls=%async_computation.14 | async-start | bytes 5242880 | tf_op jit(solution)/shard_map/all_gather | solution.py:279
  58.5 109.2 %all-gather.15.cloned.1.call-start = ((), (), s32[]{:S(2)}) async-start(), calls=%async_computation.16 | async-start | bytes 2359296 | tf_op jit(solution)/shard_map/all_gather | solution.py:263
  59.2 139.0 %all-gather.17.cloned.1.call-start = ((), (), s32[]{:S(2)}) async-start(), calls=%async_computation.17 | async-start | bytes 2359296 | tf_op jit(solution)/shard_map/all_gather | solution.py:264
  59.8 175.4 %all-gather.19.cloned.1.call-start = ((), (), s32[]{:S(2)}) async-start(), calls=%async_computation.18 | async-start | bytes 2359296 | tf_op jit(solution)/shard_map/all_gather | solution.py:265
  60.4 329.5 %reduce-scatter.13.cloned.1.call-start = ((), (), s32[]{:S(2)}) async-start(), calls=%async_computation.19 | async-start | bytes 10485760 | tf_op jit(solution)/shard_map/reduce_scatter | solution.py:320
  60.6 126.3 %copy-start.53 = (f32[512]{0:T(512)}, f32[512]{0:T(512)S(1)}, u32[]{:S(2)}) copy-start(f32[512]{0:T(512)S(1)} %dynamic-slice_convert_fusion.1) | copy-start | bytes 6148
  60.7 133.2 %copy-start.55 = (f32[512]{0:T(512)}, f32[512]{0:T(512)S(1)}, u32[]{:S(2)}) copy-start(f32[512]{0:T(512)S(1)} %dynamic-slice_convert_fusion) | copy-start | bytes 6148
  63.6 143.3 %copy-start.25 = (f32[1024,64]{1,0:T(8,128)}, f32[1024,64]{1,0:T(8,128)S(1)}, u32[]{:S(2)}) copy-start(f32[1024,64]{1,0:T(8,128)S(1)} %get-tuple-element.413) | copy-start | bytes 786436
  144.6 42.3 %copy-start.16 = (f32[1024,512]{0,1:T(8,128)}, f32[1024,512]{0,1:T(8,128)S(1)}, u32[]{:S(2)}) copy-start(f32[1024,512]{0,1:T(8,128)S(1)} %get-tuple-element.423) | copy-start | bytes 6291460
  244.3 145.7 %copy-start.14 = (bf16[256,2048]{1,0:T(8,128)(2,1)S(1)}, bf16[256,2048]{1,0:T(8,128)(2,1)}, u32[]{:S(2)}) copy-start(bf16[256,2048]{1,0:T(8,128)(2,1)} %param.19) | copy-start | bytes 3145732
  244.7 147.9 %copy-start.45 = (f32[2048]{0:T(1024)}, f32[2048]{0:T(1024)S(1)}, u32[]{:S(2)}) copy-start(f32[2048]{0:T(1024)S(1)} %convert_element_type.260) | copy-start | bytes 24580
  317.0 75.8 %copy-start.37 = (bf16[2048,16]{0,1:T(8,128)(2,1)}, bf16[2048,16]{0,1:T(8,128)(2,1)S(1)}, u32[]{:S(2)}) copy-start(bf16[2048,16]{0,1:T(8,128)(2,1)S(1)} %reshape.512) | copy-start | bytes 196612
  322.7 69.2 %copy-start.58 = (s32[2048,1]{0,1:T(1,128)}, s32[2048,1]{0,1:T(1,128)S(1)}, u32[]{:S(2)}) copy-start(s32[2048,1]{0,1:T(1,128)S(1)} %compare_select_fusion) | copy-start | bytes 24580
  392.8 15.6 copy-start.2
  394.5 13.7 copy-start.30
  429.2 235.9 %all-to-all-start = ((bf16[16,160,2048]{2,1,0:T(8,128)(2,1)}), bf16[16,160,2048]{2,1,0:T(8,128)(2,1)}, u32[]{:S(2)}, u32[]{:S(2)}) async-start(bf16[16,160,2048]{2,1,0:T(8,128)(2,1)} %broadcast_select_fusion), calls=%async_computation.1 | async-start | bytes 20971520 | tf_op jit(solution)/shard_map/all_to_all | solution.py:176
  435.8 12.4 copy-start
  665.1 290.4 %all-to-all-start.2 = ((bf16[16,160,2048]{2,1,0:T(8,128)(2,1)}), bf16[16,160,2048]{2,1,0:T(8,128)(2,1)}, u32[]{:S(2)}, u32[]{:S(2)}) async-start(bf16[16,160,2048]{2,1,0:T(8,128)(2,1)} %multiply_convert_fusion.1), calls=%async_computation.3 | async-start | bytes 20971520 | tf_op jit(solution)/shard_map/all_to_all | solution.py:176
  669.9 101.8 %all-gather.23.cloned.1.call-start = ((), (), s32[]{:S(2)}) async-start(), calls=%async_computation.21 | async-start | bytes 6291456 | tf_op jit(solution)/shard_map/all_gather | solution.py:187
  670.5 228.8 %all-gather.21.cloned.1.call-start = ((), (), s32[]{:S(2)}) async-start(), calls=%async_computation.20 | async-start | bytes 6291456 | tf_op jit(solution)/shard_map/all_gather | solution.py:186
  671.1 284.4 %all-gather.25.cloned.1.call-start = ((), (), s32[]{:S(2)}) async-start(), calls=%async_computation.22 | async-start | bytes 6291456 | tf_op jit(solution)/shard_map/all_gather | solution.py:188
  999.3 235.7 %all-to-all-start.1 = ((bf16[16,160,2048]{2,1,0:T(8,128)(2,1)}), bf16[16,160,2048]{2,1,0:T(8,128)(2,1)}, u32[]{:S(2)}, u32[]{:S(2)}) async-start(bf16[16,160,2048]{2,1,0:T(8,128)(2,1)} %bitcast.275), calls=%async_computation.2 | async-start | bytes 20971520 | tf_op jit(solution)/shard_map/all_to_all | solution.py:176
  1235.0 233.0 %all-to-all-start.3 = ((bf16[16,160,2048]{2,1,0:T(8,128)(2,1)}), bf16[16,160,2048]{2,1,0:T(8,128)(2,1)}, u32[]{:S(2)}, u32[]{:S(2)}) async-start(bf16[16,160,2048]{2,1,0:T(8,128)(2,1)} %bitcast.274), calls=%async_computation.4 | async-start | bytes 20971520 | tf_op jit(solution)/shard_map/all_to_all | solution.py:176
  1240.0 388.6 %all-gather.27.cloned.1.call-start = ((), (), s32[]{:S(2)}) async-start(), calls=%async_computation.23 | async-start | bytes 5242880 | tf_op jit(solution)/shard_map/all_gather | solution.py:387
  1240.1 22.0 %copy-start.1 = (f32[256,2048]{1,0:T(8,128)S(1)}, f32[256,2048]{1,0:T(8,128)}, u32[]{:S(2)}) copy-start(f32[256,2048]{1,0:T(8,128)} %copy-done) | copy-start | bytes 6291460
  1240.1 22.0 %copy-start.31 = (f32[256,8]{1,0:T(8,128)S(1)}, f32[256,8]{1,0:T(8,128)}, u32[]{:S(2)}) copy-start(f32[256,8]{1,0:T(8,128)} %copy-done.30) | copy-start | bytes 24580
  1489.7 11.4 copy-start.11
  1489.7 11.4 copy-start.38
  1489.7 11.4 copy-start.46
  1489.7 11.4 copy-start.65
  1507.2 244.9 %reduce-scatter.29.cloned.1.call-start = ((), (), s32[]{:S(2)}) async-start(), calls=%async_computation.31 | async-start | bytes 6291456 | tf_op jit(solution)/shard_map/reduce_scatter | solution.py:221
  1524.3 232.0 %reduce-scatter.25.cloned.1.call-start = ((), (), s32[]{:S(2)}) async-start(), calls=%async_computation.29 | async-start | bytes 6291456 | tf_op jit(solution)/shard_map/reduce_scatter | solution.py:215
  1541.8 218.7 %reduce-scatter.27.cloned.1.call-start = ((), (), s32[]{:S(2)}) async-start(), calls=%async_computation.30 | async-start | bytes 6291456 | tf_op jit(solution)/shard_map/reduce_scatter | solution.py:218
  1559.1 316.8 %reduce-scatter.31.cloned.1.call-start = ((), (), s32[]{:S(2)}) async-start(), calls=%async_computation.32 | async-start | bytes 1081344
  1561.9 354.8 %reduce-scatter.19.cloned.1.call-start = ((), (), s32[]{:S(2)}) async-start(), calls=%async_computation.26 | async-start | bytes 2359296 | tf_op jit(solution)/shard_map/reduce_scatter | solution.py:447
  1696.7 13.2 copy-start.69
  1717.5 244.5 %reduce-scatter.17.cloned.1.call-start = ((), (), s32[]{:S(2)}) async-start(), calls=%async_computation.25 | async-start | bytes 2359296 | tf_op jit(solution)/shard_map/reduce_scatter | solution.py:444
  1725.1 281.4 %reduce-scatter.23.cloned.1.call-start = ((), (), s32[]{:S(2)}) async-start(), calls=%async_computation.28 | async-start | bytes 2359296 | tf_op jit(solution)/shard_map/reduce_scatter | solution.py:453
  1731.3 319.7 %reduce-scatter.21.cloned.1.call-start = ((), (), s32[]{:S(2)}) async-start(), calls=%async_computation.27 | async-start | bytes 2359296 | tf_op jit(solution)/shard_map/reduce_scatter | solution.py:450
  1739.1 391.1 %reduce-scatter.15.cloned.1.call-start = ((), (), s32[]{:S(2)}) async-start(), calls=%async_computation.24 | async-start | bytes 5242880 | tf_op jit(solution)/shard_map/reduce_scatter | solution.py:431
  1764.7 365.4 %copy-start.15 = (bf16[256,2048]{1,0:T(8,128)(2,1)S(1)}, bf16[256,2048]{1,0:T(8,128)(2,1)}, u32[]{:S(2)}) copy-start(bf16[256,2048]{1,0:T(8,128)(2,1)} %param.19) | copy-start | bytes 3145732
  1764.7 365.4 %copy-start.42 = (f32[2048]{0:T(1024)S(1)}, f32[2048]{0:T(1024)}, u32[]{:S(2)}) copy-start(f32[2048]{0:T(1024)} %copy-done.41) | copy-start | bytes 24580
  1764.7 365.4 %copy-start.63 = (f32[256]{0:T(256)S(1)}, f32[256]{0:T(256)}, u32[]{:S(2)}) copy-start(f32[256]{0:T(256)} %copy-done.62) | copy-start | bytes 3076
  1918.5 213.5 %copy-start.57 = (f32[2048]{0:T(1024)S(1)}, f32[2048]{0:T(1024)}, u32[]{:S(2)}) copy-start(f32[2048]{0:T(1024)} %get-tuple-element.329) | copy-start | bytes 24580
  1918.5 256.9 %copy-start.22 = (f32[256,2048]{1,0:T(8,128)S(1)}, f32[256,2048]{1,0:T(8,128)}, u32[]{:S(2)}) copy-start(f32[256,2048]{1,0:T(8,128)} %get-tuple-element.380) | copy-start | bytes 6291460
  1918.5 256.9 %copy-start.70 = (f32[256]{0:T(256)S(1)}, f32[256]{0:T(256)}, u32[]{:S(2)}) copy-start(f32[256]{0:T(256)} %get-tuple-element.418) | copy-start | bytes 3076
  (57 other events, 182.5 us)
Sparse Core Ops, SparseCore 0:
  10.7 30.7 all-gather.12
  58.6 80.6 all-gather.10
  141.2 26.4 all-gather.14
  169.4 27.8 all-gather.16
  199.1 27.8 all-gather.18
  243.8 146.1 reduce-scatter.12
  1507.3 121.2 all-gather.26
Sparse Core Ops, SparseCore 1:
  671.9 99.7 all-gather.22
  773.1 126.1 all-gather.20
  900.7 54.7 all-gather.24
  1524.4 99.7 reduce-scatter.28
  1627.2 54.2 reduce-scatter.24
  1683.7 54.7 reduce-scatter.26
  1740.7 135.2 reduce-scatter.30
  1879.1 37.6 reduce-scatter.18
  1920.8 41.1 reduce-scatter.16
  1965.3 41.1 reduce-scatter.22
  2009.9 41.1 reduce-scatter.20
  2053.4 76.7 reduce-scatter.14
where the time goes:
time: 2190 us
  waiting for transfers between devices  1430 us (65%)
  matrix products  275 us (13%)
  blocking collectives  178 us (8%)
  local copies, waits for them, and re-layouts  135 us (6%)
  other arithmetic  122 us (6%)
  starting transfers between devices  23.3 us (1%)
    all_to_all x4, waiting for transfers between devices, move_slots(): lax.all_to_all(buffer, ('shard', 'context'), split_axis=0, concat_axis=0,...  592 us
    unnamed x20, waiting for transfers between devices  115 us
    all_gather x1, waiting for transfers between devices, expert_forward(): lax.all_gather(w_gate, 'tensor', axis=2, tiled=True)  111 us
    all_gather x1, waiting for transfers between devices, expert_forward(): lax.all_gather(w_up, 'tensor', axis=2, tiled=True)  100 us
    unnamed x2, blocking collectives  83.4 us
    dot_general x8, matrix products, contract_last(): lax.dot_general(left, right, (((1,), (1,)), ((), ())), preferred_element_...  79 us
    reduce_scatter x1, waiting for transfers between devices, local(): lax.psum_scatter((contract_last(grad_query_low, query_cols) + contract_la...  77.3 us
    all_gather x1, waiting for transfers between devices, local(): lax.all_gather(low_first, ('context', 'tensor'), axis=0, tiled=True)  75.7 us
  transfers between devices with their start and end apart: 23, of which 16 were waited for; matrix products, arithmetic and copies ran while one was open for 18% of the time, Pallas kernels for 0%

commit v1 on v0

v1 whole, which is shorter than its diff:
```python
import jax
import jax.numpy as jnp
from jax import lax
from jax.sharding import PartitionSpec as P

HDIM = 128
SEQ_LEN = 1024


EPSILON = 1e-05
MASKED = -1e30
LOW = jnp.bfloat16
WIDE = jnp.float32
SWAP = ((0, 1), (1, 0))


def rms_scale(values, gain):
    factor = lax.rsqrt(jnp.mean(values * values, axis=-1, keepdims=True) + EPSILON)
    return (values * factor * gain, factor)


def rms_back(values, factor, gain, grad_out):
    scaled = grad_out * gain
    mean_term = jnp.mean(scaled * values, axis=-1, keepdims=True)
    grad_values = factor * scaled - values * (factor * factor * factor) * mean_term
    return (grad_values, jnp.sum(grad_out * values * factor, axis=0))


def rope_tables(positions, head_size):
    half_size = head_size // 2
    frequency = 10000.0 ** (-2.0 * jnp.arange(half_size, dtype=jnp.float32) / head_size)
    angles = positions.astype(jnp.float32)[:, None] * frequency[None, :]
    return (jnp.cos(angles)[:, None, :], jnp.sin(angles)[:, None, :])


def rotate(values, cosine_table, sine_table, direction):
    half_size = values.shape[-1] // 2
    first_half = values[..., :half_size]
    second_half = values[..., half_size:]
    return jnp.concatenate(
        [
            first_half * cosine_table - direction * second_half * sine_table,
            second_half * cosine_table + direction * first_half * sine_table,
        ],
        axis=-1,
    )


def contract_last(left, right):
    return lax.dot_general(
        left, right, (((1,), (1,)), ((), ())), preferred_element_type=jnp.float32
    )


def contract_first(left, right):
    return lax.dot_general(
        left, right, (((0,), (0,)), ((), ())), preferred_element_type=jnp.float32
    )


def plain(left, right):
    return jnp.dot(left, right, preferred_element_type=jnp.float32)


def swap(values, axis):
    return lax.ppermute(values, axis, SWAP)


def hop(values, distance):
    count = lax.axis_size("shard")
    return lax.ppermute(values, "shard", tuple((i, i ^ distance) for i in range(count)))


def gather_group(block):
    near = swap(block, "tensor")
    across = swap(block, "context")
    return [block, near, across, swap(across, "tensor")]


def scatter_group(parts):
    far = swap(parts[3].astype(LOW), "tensor")
    near = swap(parts[1].astype(LOW), "tensor")
    across = swap((parts[2] + far.astype(WIDE)).astype(LOW), "context")
    return parts[0] + near.astype(WIDE) + across.astype(WIDE)


def gather_chips(block):
    count = lax.axis_size("shard")
    return [block] + [hop(block, r) for r in range(2, count, 2)]


def gather_shard(block):
    even = gather_chips(block)
    return even + [hop(piece, 1) for piece in even]


def shard_order():
    count = lax.axis_size("shard")
    return jnp.array(list(range(0, count, 2)) + list(range(1, count, 2)), jnp.int32)


def bits_of(axes):
    return [(name, 1 << b) for name in axes for b in range(lax.axis_size(name).bit_length() - 1)]


SMALL_AXES = ("tensor", "context", "shard")


def step_to(values, name, bit):
    count = lax.axis_size(name)
    return lax.ppermute(values, name, tuple((i, i ^ bit) for i in range(count)))


def gather_small(row):
    for name, bit in bits_of(SMALL_AXES):
        other = step_to(row, name, bit)
        upper = (lax.axis_index(name) & bit) > 0
        row = jnp.where(
            upper, jnp.concatenate([other, row], axis=0), jnp.concatenate([row, other], axis=0)
        )
    return row


def scatter_small(rows):
    for name, bit in reversed(bits_of(SMALL_AXES)):
        half = rows.shape[0] // 2
        upper = (lax.axis_index(name) & bit) > 0
        mine = jnp.where(upper, rows[half:], rows[:half])
        theirs = jnp.where(upper, rows[:half], rows[half:])
        rows = mine + step_to(theirs, name, bit)
    return rows


def block_scores(query_block, key_sequence, query_place, key_place):
    scores = jnp.einsum(
        "qhd,khd->hqk", query_block, key_sequence, preferred_element_type=jnp.float32
    ) * HDIM ** (-0.5)
    causal = query_place[:, None] >= key_place[None, :]
    return jnp.where(causal[None], scores, MASKED)


def attend_forward(queries, key_vectors, value_vectors, place, block_rows):
    def one_block(block_index):
        first = block_index * block_rows
        query_block = lax.dynamic_slice_in_dim(queries, first, block_rows, 0)
        query_place = lax.dynamic_slice_in_dim(place, first, block_rows, 0)
        scores = block_scores(query_block, key_vectors, query_place, place)
        maximum = jnp.max(scores, axis=-1, keepdims=True)
        weights = jnp.exp(scores - maximum)
        denominator = jnp.sum(weights, axis=-1, keepdims=True)
        attn_low = (weights / denominator).astype(jnp.bfloat16)
        output = jnp.einsum(
            "hqk,khd->qhd", attn_low, value_vectors, preferred_element_type=jnp.float32
        )
        return (output.astype(jnp.bfloat16), (maximum + jnp.log(denominator))[..., 0])

    block_total = queries.shape[0] // block_rows
    outputs, log_sums = lax.map(one_block, jnp.arange(block_total, dtype=jnp.int32))
    return (outputs.reshape(queries.shape), log_sums)


def attend_backward(queries, key_vectors, value_vectors, grad_vectors, log_sums, place, block_rows):
    score_scale = HDIM ** (-0.5)
    zero_grads = jnp.zeros(queries.shape, jnp.float32)

    def one_block(grad_carry, inputs_pair):
        grad_keys, grad_values = grad_carry
        block_index, log_sum = inputs_pair
        first = block_index * block_rows
        query_block = lax.dynamic_slice_in_dim(queries, first, block_rows, 0)
        grad_block = lax.dynamic_slice_in_dim(grad_vectors, first, block_rows, 0)
        query_place = lax.dynamic_slice_in_dim(place, first, block_rows, 0)
        scores = block_scores(query_block, key_vectors, query_place, place)
        attn_probs = jnp.exp(scores - log_sum[..., None])
        grad_probs = jnp.einsum(
            "qhd,khd->hqk", grad_block, value_vectors, preferred_element_type=jnp.float32
        )
        delta_term = jnp.sum(attn_probs * grad_probs, axis=-1, keepdims=True)
        grad_scores = (attn_probs * (grad_probs - delta_term)).astype(jnp.bfloat16)
        grad_query = (
            jnp.einsum("hqk,khd->qhd", grad_scores, key_vectors, preferred_element_type=jnp.float32)
            * score_scale
        )
        key_part = (
            jnp.einsum("hqk,qhd->khd", grad_scores, query_block, preferred_element_type=jnp.float32)
            * score_scale
        )
        value_part = jnp.einsum(
            "hqk,qhd->khd",
            attn_probs.astype(jnp.bfloat16),
            grad_block,
            preferred_element_type=jnp.float32,
        )
        return ((grad_keys + key_part, grad_values + value_part), grad_query.astype(jnp.bfloat16))

    block_total = queries.shape[0] // block_rows
    (grad_keys, grad_values), grad_queries = lax.scan(
        one_block, (zero_grads, zero_grads), (jnp.arange(block_total, dtype=jnp.int32), log_sums)
    )
    return (
        grad_queries.reshape(queries.shape),
        grad_keys.astype(jnp.bfloat16),
        grad_values.astype(jnp.bfloat16),
    )


def silu_parts(gate_act):
    sigmoid_value = jax.nn.sigmoid(gate_act)
    return (gate_act * sigmoid_value, sigmoid_value)


def expert_forward(rows, weights):
    gate_weight, up_weight, down_weight = weights
    gate_act = plain(rows, gate_weight)
    up_act = plain(rows, up_weight)
    hidden_act = (silu_parts(gate_act)[0] * up_act).astype(LOW)
    produced = contract_last(hidden_act, down_weight).astype(LOW)
    return (produced, (gate_act, up_act, hidden_act))


def expert_backward(grad_rows, kept, weights):
    gate_weight, up_weight, down_weight = weights
    gate_act, up_act, hidden_act = kept
    grad_hidden = plain(grad_rows, down_weight)
    activated, sigmoid_value = silu_parts(gate_act)
    grad_gate_act = (
        grad_hidden * up_act * sigmoid_value * (1.0 + gate_act * (1.0 - sigmoid_value))
    ).astype(LOW)
    grad_up_act = (grad_hidden * activated).astype(LOW)
    grad_route = contract_last(grad_gate_act, gate_weight) + contract_last(grad_up_act, up_weight)
    return (grad_route, grad_gate_act, grad_up_act)


def owned_weight_grad(left, right):
    half = right.shape[1] // 2
    theirs = contract_first(left, right[:, half:]).astype(LOW)
    mine = contract_first(left, right[:, :half])
    return (mine + swap(theirs, "tensor").astype(WIDE))[None]


def softmax_rows(logits):
    weights = jnp.exp(logits - jnp.max(logits, axis=-1, keepdims=True))
    return weights / jnp.sum(weights, axis=-1, keepdims=True)


def pick_rows(pick, blocks):
    chosen = jnp.einsum(
        "bst,btd->bsd", pick, jnp.stack(blocks), preferred_element_type=jnp.float32
    ).astype(LOW)
    return chosen.reshape(-1, chosen.shape[-1])


def slot_picks(ids, expert, capacity):
    routed = jnp.any(ids == expert, axis=2)
    tokens = ids.shape[1]
    line = jnp.arange(tokens, dtype=jnp.int32)
    earlier = (line[:, None] < line[None, :]).astype(LOW)
    position = plain(routed.astype(LOW), earlier).astype(jnp.int32)
    position = jnp.where(routed, position, -1)
    slots = jnp.arange(capacity, dtype=jnp.int32)
    return (position[:, None, :] == slots[None, :, None]).astype(LOW)


def return_chips(rows, picks, other_picks, capacity):
    half = rows.shape[0] // 2
    width = rows.shape[1]
    chips = half // capacity
    arrived = hop(rows[half:], 1).reshape(chips, capacity, width)
    kept = rows[:half].reshape(chips, capacity, width)
    both = jnp.concatenate([kept, arrived], axis=1)
    pick = jnp.concatenate([picks[:chips], other_picks], axis=1)
    total = None
    parts = []
    for chip in range(chips):
        part = lax.dot_general(
            pick[chip], both[chip], (((0,), (0,)), ((), ())), preferred_element_type=jnp.float32
        )
        parts.append(part)
    total = parts[0]
    for chip in range(1, chips):
        total = total + hop(parts[chip].astype(LOW), 2 * chip).astype(WIDE)
    return total


def experts_by_blocks(low_second, cot_chunks, all_ids, router, weights, capacity):
    shard, context = lax.axis_index("shard"), lax.axis_index("context")
    contexts = lax.axis_size("context")
    expert = shard * contexts + context
    other_expert = (shard ^ 1) * contexts + context
    order = shard_order()
    token_count = low_second.shape[0]
    chips = order.shape[0] // 2
    across = swap(low_second, "context")
    chunks = [gather_shard(low_second), gather_shard(across)]
    mixtures, grads, gate_grads = [], [], []
    kept_rows, kept_grads, kept_hidden, kept_gate, kept_up = [], [], [], [], []
    for turn in range(2):
        sources = (shard ^ order) * contexts + (context ^ turn)
        ids = jnp.take(all_ids, sources, axis=0)
        picks = slot_picks(ids, expert, capacity)
        other_picks = slot_picks(ids[:chips], other_expert, capacity)
        rows = pick_rows(picks, chunks[turn])
        cot_rows = pick_rows(picks, cot_chunks[turn])
        probs = softmax_rows(plain(rows, router))
        mine = jnp.arange(probs.shape[1], dtype=jnp.int32)[None, :] == expert
        gate = jnp.sum(jnp.where(mine, probs, 0.0), axis=1, keepdims=True)
        produced, kept = expert_forward(rows, weights)
        cot_wide = cot_rows.astype(WIDE)
        produced_wide = produced.astype(WIDE)
        slot_grad = jnp.sum(produced_wide * cot_wide, axis=1)
        gate_grads.append(
            jnp.sum(
                picks.astype(WIDE) * slot_grad.reshape(picks.shape[0], capacity)[:, :, None], axis=1
            )
        )
        grad_rows = (gate * cot_wide).astype(LOW)
        mixtures.append(
            return_chips((gate * produced_wide).astype(LOW), picks, other_picks, capacity)
        )
        grad_route, grad_gate_act, grad_up_act = expert_backward(grad_rows, kept, weights)
        grads.append(return_chips(grad_route.astype(LOW), picks, other_picks, capacity))
        kept_rows.append(rows)
        kept_grads.append(grad_rows)
        kept_hidden.append(kept[2])
        kept_gate.append(grad_gate_act)
        kept_up.append(grad_up_act)
    mixture = mixtures[0] + swap(mixtures[1].astype(LOW), "context").astype(WIDE)
    grad = grads[0] + swap(grads[1].astype(LOW), "context").astype(WIDE)
    lines = jnp.stack(gate_grads, axis=1)
    lines = jnp.where(context == 0, lines, lines[:, ::-1])
    places = jnp.arange(order.shape[0], dtype=jnp.int32)
    slots = jnp.where((places & 1) == 0, places // 2, chips + places // 2)
    lines = jnp.take(lines, jnp.take(slots, shard ^ places), axis=0)
    lines = lines.reshape(-1, token_count)
    by_expert = lax.all_to_all(lines, ("shard", "context"), split_axis=0, concat_axis=0, tiled=True)
    all_rows = jnp.concatenate(kept_rows, axis=0)
    weight_grads = (
        owned_weight_grad(all_rows, jnp.concatenate(kept_gate, axis=0)),
        owned_weight_grad(all_rows, jnp.concatenate(kept_up, axis=0)),
        owned_weight_grad(
            jnp.concatenate(kept_grads, axis=0), jnp.concatenate(kept_hidden, axis=0)
        ),
    )
    return (mixture, grad, by_expert.T, weight_grads)


def move_slots(buffer):
    return lax.all_to_all(buffer, ("shard", "context"), split_axis=0, concat_axis=0, tiled=True)


def experts_by_slots(low_second, cotangent, expert_ids, router_probs, weights, capacity):
    row_count, model_width = low_second.shape
    expert_count = router_probs.shape[1]
    top_count = expert_ids.shape[1]
    choose = expert_ids[:, :, None] == jnp.arange(expert_count, dtype=jnp.int32)[None, None, :]
    gate_probs = jnp.sum(jnp.where(choose, router_probs[:, None, :], 0.0), axis=2)
    route_total = row_count * top_count
    flat_ids = expert_ids.reshape(-1)
    onehot = (flat_ids[:, None] == jnp.arange(expert_count, dtype=jnp.int32)[None, :]).astype(
        jnp.int32
    )
    before = jnp.cumsum(onehot, axis=0) - onehot
    route_slot = flat_ids * capacity + jnp.sum(before * onehot, axis=1)
    route_of_slot = (
        jnp.full((expert_count * capacity,), route_total, jnp.int32)
        .at[route_slot]
        .set(jnp.arange(route_total, dtype=jnp.int32))
    )
    filled = route_of_slot < route_total
    route_clipped = jnp.minimum(route_of_slot, route_total - 1)
    token_of_slot = route_clipped // top_count
    slot_shape = (expert_count, capacity, model_width)
    flat_shape = (expert_count * capacity, model_width)
    sending = jnp.where(filled[:, None], low_second[token_of_slot], jnp.zeros((), LOW))
    rows = move_slots(sending.reshape(slot_shape)).reshape(flat_shape)
    produced, kept = expert_forward(rows, weights)
    returned = move_slots(produced.reshape(slot_shape)).reshape(flat_shape)
    chosen = returned[route_slot].reshape(row_count, top_count, model_width).astype(WIDE)
    mixture = jnp.sum(gate_probs[:, :, None] * chosen, axis=1)
    grad_top = cotangent.astype(WIDE)
    grad_gates = jnp.sum(chosen * grad_top[:, None, :], axis=2)
    slot_gate = jnp.where(filled, gate_probs.reshape(-1)[route_clipped], 0.0)
    sending_grad = (slot_gate[:, None] * grad_top[token_of_slot]).astype(LOW)
    grad_rows = move_slots(sending_grad.reshape(slot_shape)).reshape(flat_shape)
    grad_route, grad_gate_act, grad_up_act = expert_backward(grad_rows, kept, weights)
    returned_grad = move_slots(grad_route.astype(LOW).reshape(slot_shape)).reshape(flat_shape)
    grad = jnp.sum(
        returned_grad[route_slot].reshape(row_count, top_count, model_width).astype(WIDE), axis=1
    )
    by_expert = jnp.sum(jnp.where(choose, grad_gates[:, :, None], 0.0), axis=1)
    weight_grads = (
        owned_weight_grad(rows, grad_gate_act),
        owned_weight_grad(rows, grad_up_act),
        owned_weight_grad(grad_rows, kept[2]),
    )
    return (mixture, grad, by_expert, weight_grads)


def local(
    hidden_in,
    cotangent,
    w_query,
    w_key,
    w_value,
    w_out,
    w_router,
    norm_first,
    norm_second,
    query_gain,
    key_gain,
    w_gate,
    w_up,
    w_down,
    expert_ids,
):
    group_index = lax.axis_index(("context", "tensor"))
    row_count, model_width = hidden_in.shape
    column_span = w_query.shape[1]
    heads = column_span // HDIM
    expert_count = w_router.shape[1]
    top_count = expert_ids.shape[1]
    capacity = max(2, row_count * top_count * 5 // (4 * expert_count))
    by_blocks = 2 * capacity >= row_count
    block_rows = min(512, SEQ_LEN)
    device_count = model_width // norm_first.shape[0]

    router_rows = w_router.shape[0]
    small = gather_small(
        jnp.concatenate(
            [w_router.reshape(-1), norm_first, norm_second, query_gain, key_gain], axis=0
        )[None]
    )
    hidden_blocks = gather_group(hidden_in)
    packed = lax.all_gather(
        jnp.concatenate([w_query, w_key, w_value, w_out], axis=1), "shard", axis=0, tiled=True
    )
    router_size = router_rows * expert_count
    router_full = small[:, :router_size].reshape(model_width, expert_count)
    gains = [
        small[:, router_size + i * router_rows : router_size + (i + 1) * router_rows]
        .reshape(model_width)
        .astype(WIDE)
        for i in range(4)
    ]
    gain_first, gain_second, gain_query, gain_key = gains
    weights = tuple(
        jnp.concatenate([held[0], swap(held[0], "tensor")], axis=1)
        for held in (w_gate, w_up, w_down)
    )
    if by_blocks:
        all_ids = lax.all_gather(expert_ids, ("shard", "context"), axis=0, tiled=False)
        all_ids = all_ids.reshape(-1, row_count, top_count)
        cot_chunks = [gather_shard(cotangent), gather_shard(swap(cotangent, "context"))]

    qkv_cols = packed[:, : 3 * column_span]
    out_cols = packed[:, 3 * column_span :]
    inputs = hidden_in.astype(WIDE)
    factor_first = rms_scale(inputs, gain_first)[1]
    low_blocks, pre_blocks = [], []
    for block in hidden_blocks:
        low_block = rms_scale(block.astype(WIDE), gain_first)[0].astype(LOW)
        low_blocks.append(low_block)
        pre_blocks.append(plain(low_block, qkv_cols))
    low_group = jnp.concatenate(low_blocks, axis=0)
    pre = jnp.concatenate(pre_blocks, axis=0)
    group_rows = low_group.shape[0]
    query_pre = pre[:, :column_span]
    key_pre = pre[:, column_span : 2 * column_span]
    value_heads = pre[:, 2 * column_span :].astype(LOW)

    def over_group(sums):
        stacked = jnp.stack(sums).reshape(2, 4, -1)
        stacked = stacked + swap(stacked, "tensor")[:, jnp.array([1, 0, 3, 2])]
        stacked = stacked + swap(stacked, "context")[:, jnp.array([2, 3, 0, 1])]
        return stacked.reshape(2, -1)

    query_square, key_square = over_group(
        [jnp.sum(query_pre * query_pre, axis=1), jnp.sum(key_pre * key_pre, axis=1)]
    )
    query_factor = lax.rsqrt(query_square / model_width + EPSILON)[:, None]
    key_factor = lax.rsqrt(key_square / model_width + EPSILON)[:, None]
    gain_query_cols = lax.dynamic_slice_in_dim(
        gain_query, group_index * column_span, column_span, 0
    )
    gain_key_cols = lax.dynamic_slice_in_dim(gain_key, group_index * column_span, column_span, 0)
    line = jnp.arange(group_rows, dtype=jnp.int32)
    place = ((line // row_count) ^ group_index) * row_count + line % row_count
    cosine_table, sine_table = rope_tables(place, HDIM)
    head_shape = (group_rows, heads, HDIM)
    query_heads = rotate(
        (query_pre * query_factor * gain_query_cols).reshape(head_shape),
        cosine_table,
        sine_table,
        1.0,
    ).astype(LOW)
    key_heads = rotate(
        (key_pre * key_factor * gain_key_cols).reshape(head_shape), cosine_table, sine_table, 1.0
    ).astype(LOW)
    value_heads = value_heads.reshape(head_shape)
    attended_heads, log_sums = attend_forward(
        query_heads, key_heads, value_heads, place, block_rows
    )
    attended = attended_heads.reshape(group_rows, column_span)

    def block_of(values, k):
        return values[k * row_count : (k + 1) * row_count]

    middle = inputs + scatter_group(
        [contract_last(block_of(attended, k), out_cols) for k in range(4)]
    )
    normed_second, factor_second = rms_scale(middle, gain_second)
    low_second = normed_second.astype(LOW)
    router_probs = softmax_rows(plain(low_second, router_full))
    if by_blocks:
        mixture, grad_from_experts, grad_router_probs, expert_grads = experts_by_blocks(
            low_second, cot_chunks, all_ids, router_full, weights, capacity
        )
    else:
        mixture, grad_from_experts, grad_router_probs, expert_grads = experts_by_slots(
            low_second, cotangent, expert_ids, router_probs, weights, capacity
        )
    block_output = (middle + mixture).astype(LOW)
    grad_logits = (
        router_probs
        * (grad_router_probs - jnp.sum(router_probs * grad_router_probs, axis=1, keepdims=True))
    ).astype(LOW)
    grad_router_weight = contract_first(low_second, grad_logits)
    grad_second = grad_from_experts + contract_last(grad_logits, router_full)
    grad_normed_second, grad_gain_second = rms_back(middle, factor_second, gain_second, grad_second)
    grad_middle = cotangent.astype(WIDE) + grad_normed_second
    pieces = gather_group(grad_middle.astype(LOW))
    piece = jnp.concatenate(pieces, axis=0)
    out_total = contract_first(piece, attended)
    grad_rows = jnp.concatenate([plain(one, out_cols).astype(LOW) for one in pieces], axis=0)
    grad_query_heads, grad_key_heads, grad_value_heads = attend_backward(
        query_heads,
        key_heads,
        value_heads,
        grad_rows.reshape(head_shape),
        log_sums,
        place,
        block_rows,
    )
    grad_query_normed = rotate(
        grad_query_heads.astype(WIDE), cosine_table, sine_table, -1.0
    ).reshape(group_rows, column_span)
    grad_key_normed = rotate(grad_key_heads.astype(WIDE), cosine_table, sine_table, -1.0).reshape(
        group_rows, column_span
    )
    query_scaled = grad_query_normed * gain_query_cols
    key_scaled = grad_key_normed * gain_key_cols
    query_total, key_total = over_group(
        [jnp.sum(query_scaled * query_pre, axis=1), jnp.sum(key_scaled * key_pre, axis=1)]
    )
    grad_query_low = (
        query_factor * query_scaled
        - query_pre
        * (query_factor * query_factor * query_factor)
        * (query_total / model_width)[:, None]
    ).astype(LOW)
    grad_key_low = (
        key_factor * key_scaled
        - key_pre * (key_factor * key_factor * key_factor) * (key_total / model_width)[:, None]
    ).astype(LOW)
    grad_pre = jnp.concatenate(
        [grad_query_low, grad_key_low, grad_value_heads.reshape(group_rows, column_span)], axis=1
    )
    grad_first = scatter_group([contract_last(block_of(grad_pre, k), qkv_cols) for k in range(4)])
    grad_normed_first, grad_gain_first = rms_back(inputs, factor_first, gain_first, grad_first)
    grad_input = grad_middle + grad_normed_first
    packed_grads = jnp.concatenate(
        [contract_first(low_group, grad_pre).astype(LOW), out_total.astype(LOW)], axis=1
    )
    head_grads = lax.psum_scatter(packed_grads, "shard", scatter_dimension=0, tiled=True).astype(
        WIDE
    )
    zero_gain = jnp.zeros((model_width,), WIDE)
    grad_gain_query = lax.dynamic_update_slice_in_dim(
        zero_gain,
        jnp.sum(grad_query_normed * query_pre * query_factor, axis=0),
        group_index * column_span,
        0,
    )
    grad_gain_key = lax.dynamic_update_slice_in_dim(
        zero_gain,
        jnp.sum(grad_key_normed * key_pre * key_factor, axis=0),
        group_index * column_span,
        0,
    )
    by_device = [
        one.reshape(device_count, -1)
        for one in (grad_router_weight, grad_gain_second, grad_gain_query, grad_gain_key)
    ]
    early = scatter_small(jnp.concatenate(by_device, axis=1))[0]
    late = scatter_small(grad_gain_first.reshape(device_count, -1))[0]
    router_grad = early[:router_size].reshape(router_rows, expert_count)
    rest = early[router_size:].reshape(3, router_rows)
    return (
        block_output,
        grad_input,
        head_grads[:, :column_span],
        head_grads[:, column_span : 2 * column_span],
        head_grads[:, 2 * column_span : 3 * column_span],
        head_grads[:, 3 * column_span :],
        router_grad,
        late,
        rest[0],
        rest[1],
        rest[2],
        expert_grads[0],
        expert_grads[1],
        expert_grads[2],
    )


def solution(mesh):
    rows = P(("shard", "context", "tensor"), None)
    columns = P("shard", ("context", "tensor"))
    vector = P(("shard", "context", "tensor"))
    expert = P(("shard", "context"), None, "tensor")
    return jax.shard_map(
        local,
        mesh=mesh,
        in_specs=(
            (rows, rows)
            + (columns,) * 4
            + (rows,)
            + (vector,) * 4
            + (expert,) * 3
            + (rows,)
        ),
        out_specs=((rows, rows) + (columns,) * 4 + (rows,) + (vector,) * 4 + (expert,) * 3),
        check_vma=False,
    )
```

time: 2190 us -> 1480 us (0.68)
  waiting for transfers between devices: 1430 us -> 731 us
  matrix products: 275 us -> 346 us
  blocking collectives: 178 us -> 111 us
  starting transfers between devices: 23.3 us -> 83.5 us
  local copies, waits for them, and re-layouts: 135 us -> 95.6 us
  other arithmetic: 122 us -> 87 us
    ppermute x0 -> x85, waiting for transfers between devices: none -> 731 us  [the longest x26 438 us: swap(): return lax.ppermute(values, axis, SWAP)]
    all_to_all x4 -> x1, waiting for transfers between devices: 592 us -> 0.01 us  [experts_by_blocks(): lax.all_to_all(lines, ('shard', 'context'), split_axis=0, concat_axis=0,...]
    all_gather x9 -> x1, waiting for transfers between devices: 416 us -> 0.01 us  [local(): lax.all_gather(jnp.concatenate([w_query, w_key, w_value, w_out], axis=1),...]
    reduce_scatter x9 -> x1, waiting for transfers between devices: 304 us -> 0.01 us  [local(): lax.psum_scatter(packed_grads, 'shard', scatter_dimension=0, tiled=True)]
    unnamed x20 -> x2, waiting for transfers between devices: 115 us -> 0.03 us
    unnamed x2 -> x0, blocking collectives: 83.4 us -> none
    ppermute x0 -> x85, starting transfers between devices: none -> 79.9 us  [the longest x44 36.8 us: hop(): lax.ppermute(values, 'shard', tuple(((i, i ^ distance) for i in range(cou...]
    gather x5 -> x9, local copies, waits for them, and re-layouts: 80.4 us -> 5.01 us  [the longest x3 1.37 us: experts_by_blocks(): lines = jnp.take(lines, jnp.take(slots, shard ^ places), axis=0)]
  transfers between devices with their start and end apart: 23 -> 88, of which waited for: 16 -> 39; matrix products, arithmetic and copies ran while one was open for 18% -> 31% of each run, Pallas kernels for 0% -> 0%
where the time goes in v1:
time: 1480 us; the launch traced here: 1470 us
  waiting for transfers between devices  731 us (49%)
  matrix products  346 us (23%)
  blocking collectives  111 us (8%)
  local copies, waits for them, and re-layouts  95.6 us (6%)
  other arithmetic  87 us (6%)
  starting transfers between devices  83.5 us (6%)
  between operations  17.1 us (1%)
    ppermute x26, waiting for transfers between devices, swap(): return lax.ppermute(values, axis, SWAP)  438 us
    ppermute x44, waiting for transfers between devices, hop(): lax.ppermute(values, 'shard', tuple(((i, i ^ distance) for i in range(cou...  272 us
    all_gather x1, blocking collectives, local(): lax.all_gather(expert_ids, ('shard', 'context'), axis=0, tiled=False)  111 us
    dot_general x21, matrix products, plain(): return jnp.dot(left, right, preferred_element_type=jnp.float32)  92.2 us
    dot_general x15, matrix products, contract_last(): lax.dot_general(left, right, (((1,), (1,)), ((), ())), preferred_element_...  85.5 us
    dot_general x9, matrix products, contract_first(): lax.dot_general(left, right, (((0,), (0,)), ((), ())), preferred_element_...  77.7 us
    unnamed x314, local copies, waits for them, and re-layouts  44.8 us
    ppermute x44, starting transfers between devices, hop(): lax.ppermute(values, 'shard', tuple(((i, i ^ distance) for i in range(cou...  36.8 us
  transfers between devices with their start and end apart: 88, of which 39 were waited for; matrix products, arithmetic and copies ran while one was open for 31% of the time, Pallas kernels for 0%

profile of v1, /device:TPU:0, one launch (start us, length us, event | category | flops | bytes accessed | tf_op | source)
XLA Modules:
  0.0 1473.9 jit_solution(3240892313034633072)
XLA Ops:
  18.0 110.8 %all-gather = s32[4096,8]{0,1:T(8,128)S(1)} all-gather(s32[256,8]{0,1:T(8,128)S(1)} %copy-done.108), channel_id=2, replica_groups=mesh['shard'=8,'context'=2,'tensor'=2] {'shard','context'}, dimensions={0}, use_global_device_ids=true | all-gather | bytes 139264 | tf_op jit(solution)/shard_map/all_gather | solution.py:451
  162.5 37.9 %collective-permute-done.41 = bf16[256,2048]{1,0:T(8,128)(2,1)} collective-permute-done((bf16[256,2048]{1,0:T(8,128)(2,1)}, bf16[256,2048]{1,0:T(8,128)(2,1)}, u32[]{:S(2)}, u32[]{:S(2)}) %collective-permute-start.41) | collective-permute-done | bytes 1048608 | tf_op jit(solution)/shard_map/ppermute | solution.py:71
  216.4 98.8 %collective-permute-done.7 = bf16[256,2048]{1,0:T(8,128)(2,1)S(1)} collective-permute-done((bf16[256,2048]{1,0:T(8,128)(2,1)S(1)}, bf16[256,2048]{1,0:T(8,128)(2,1)S(1)}, u32[]{:S(2)}, u32[]{:S(2)}) %collective-permute-start.7) | collective-permute-done | bytes 1048608 | tf_op jit(solution)/shard_map/ppermute | solution.py:66
  321.1 38.3 %collective-permute-done.53 = bf16[256,2048]{1,0:T(8,128)(2,1)} collective-permute-done((bf16[256,2048]{1,0:T(8,128)(2,1)}, bf16[256,2048]{1,0:T(8,128)(2,1)}, u32[]{:S(2)}, u32[]{:S(2)}) %collective-permute-start.53) | collective-permute-done | bytes 1048608 | tf_op jit(solution)/shard_map/ppermute | solution.py:71
  361.8 7.2 convolution_convert_fusion.4
  412.1 20.6 %while.27 = (s32[]{:T(128)}, bf16[2,512,4,128]{3,2,1,0:T(4,128)(2,1)}, f32[2,4,512]{2,1,0:T(4,128)S(1)}, s32[2]{0:T(128)S(1)}, s32[1024]{0:T(1024)S(1)}, /*index...) while((s32[]{:T(128)}, ...), condition=%wide.region_9.10_spmd, body=%wide.region_6.9_spmd.sunk | while | flops 1099692032 | bytes 31533756 | solution.py:158
  445.9 17.1 %collective-permute-done.11 = bf16[256,2048]{1,0:T(8,128)(2,1)S(1)} collective-permute-done((bf16[256,2048]{1,0:T(8,128)(2,1)S(1)}, bf16[256,2048]{1,0:T(8,128)(2,1)S(1)}, u32[]{:S(2)}, u32[]{:S(2)}) %collective-permute-start.11) | collective-permute-done | bytes 1048608 | tf_op jit(solution)/shard_map/ppermute | solution.py:66
  472.6 32.9 %collective-permute-done.10 = bf16[256,2048]{1,0:T(8,128)(2,1)S(1)} collective-permute-done((bf16[256,2048]{1,0:T(8,128)(2,1)S(1)}, bf16[256,2048]{1,0:T(8,128)(2,1)S(1)}, u32[]{:S(2)}, u32[]{:S(2)}) %collective-permute-start.10) | collective-permute-done | bytes 1048608 | tf_op jit(solution)/shard_map/ppermute | solution.py:66
  505.5 9.1 collective-permute-done.12
  517.0 7.7 convolution_convert_fusion.3
  528.5 33.5 %collective-permute-done.27 = bf16[256,2048]{1,0:T(8,128)(2,1)S(1)} collective-permute-done((bf16[256,2048]{1,0:T(8,128)(2,1)S(1)}, bf16[256,2048]{1,0:T(8,128)(2,1)S(1)}, u32[]{:S(2)}, u32[]{:S(2)}) %collective-permute-start.27) | collective-permute-done | bytes 1048608 | tf_op jit(solution)/shard_map/ppermute | solution.py:66
  564.6 23.4 %collective-permute-done.15 = bf16[256,2048]{1,0:T(8,128)(2,1)S(1)} collective-permute-done((bf16[256,2048]{1,0:T(8,128)(2,1)S(1)}, bf16[256,2048]{1,0:T(8,128)(2,1)S(1)}, u32[]{:S(2)}, u32[]{:S(2)}) %collective-permute-start.15) | collective-permute-done | bytes 1048608 | tf_op jit(solution)/shard_map/ppermute | solution.py:71
  596.2 10.8 fusion.285
  606.9 9.8 collective-permute-done.28
  616.8 23.1 %collective-permute-done.29 = bf16[256,2048]{1,0:T(8,128)(2,1)S(1)} collective-permute-done((bf16[256,2048]{1,0:T(8,128)(2,1)S(1)}, bf16[256,2048]{1,0:T(8,128)(2,1)S(1)}, u32[]{:S(2)}, u32[]{:S(2)}) %collective-permute-start.29) | collective-permute-done | bytes 1048608 | tf_op jit(solution)/shard_map/ppermute | solution.py:71
  654.8 9.6 fusion.284
  664.5 9.6 fusion.281
  679.8 10.4 fusion.280
  690.2 13.2 multiply_convert_fusion.4
  703.5 14.3 multiply_convert_fusion.2
  717.7 12.0 fusion.57
  729.7 8.0 fusion.35
  740.1 9.7 fusion.37
  758.9 8.5 fusion.282
  767.3 8.2 add_convert_fusion
  778.7 10.7 fusion.283
  789.3 11.4 add_convert_fusion.1
  806.8 8.7 convolution_convert_fusion.7
  850.4 15.8 %collective-permute-done.60 = bf16[256,2048]{1,0:T(8,128)(2,1)S(1)} collective-permute-done((bf16[256,2048]{1,0:T(8,128)(2,1)S(1)}, bf16[256,2048]{1,0:T(8,128)(2,1)S(1)}, u32[]{:S(2)}, u32[]{:S(2)}) %collective-permute-start.60) | collective-permute-done | bytes 1048608 | tf_op jit(solution)/shard_map/ppermute | solution.py:71
  869.6 20.5 %collective-permute-done.62 = bf16[256,2048]{1,0:T(8,128)(2,1)S(1)} collective-permute-done((bf16[256,2048]{1,0:T(8,128)(2,1)S(1)}, bf16[256,2048]{1,0:T(8,128)(2,1)S(1)}, u32[]{:S(2)}, u32[]{:S(2)}) %collective-permute-start.62) | collective-permute-done | bytes 1048608 | tf_op jit(solution)/shard_map/ppermute | solution.py:71
  892.2 30.5 %collective-permute-done.37 = bf16[256,2048]{1,0:T(8,128)(2,1)S(1)} collective-permute-done((bf16[256,2048]{1,0:T(8,128)(2,1)S(1)}, bf16[256,2048]{1,0:T(8,128)(2,1)S(1)}, u32[]{:S(2)}, u32[]{:S(2)}) %collective-permute-start.37) | collective-permute-done | bytes 1048608 | tf_op jit(solution)/shard_map/ppermute | solution.py:71
  935.6 32.1 %collective-permute-done.49 = bf16[256,2048]{1,0:T(8,128)(2,1)S(1)} collective-permute-done((bf16[256,2048]{1,0:T(8,128)(2,1)S(1)}, bf16[256,2048]{1,0:T(8,128)(2,1)S(1)}, u32[]{:S(2)}, u32[]{:S(2)}) %collective-permute-start.49) | collective-permute-done | bytes 1048608 | tf_op jit(solution)/shard_map/ppermute | solution.py:71
  980.5 30.9 %collective-permute-done.25 = bf16[256,2048]{1,0:T(8,128)(2,1)S(1)} collective-permute-done((bf16[256,2048]{1,0:T(8,128)(2,1)S(1)}, bf16[256,2048]{1,0:T(8,128)(2,1)S(1)}, u32[]{:S(2)}, u32[]{:S(2)}) %collective-permute-start.25) | collective-permute-done | bytes 1048608 | tf_op jit(solution)/shard_map/ppermute | solution.py:71
  1016.7 6.0 fusion.288
  1026.6 9.5 convolution_convert_fusion.8
  1038.2 31.9 %collective-permute-done.65 = bf16[256,2048]{1,0:T(8,128)(2,1)S(1)} collective-permute-done((bf16[256,2048]{1,0:T(8,128)(2,1)S(1)}, bf16[256,2048]{1,0:T(8,128)(2,1)S(1)}, u32[]{:S(2)}, u32[]{:S(2)}) %collective-permute-start.65) | collective-permute-done | bytes 1048608 | tf_op jit(solution)/shard_map/ppermute | solution.py:66
  1079.1 148.4 %collective-permute-done.66 = bf16[256,2048]{1,0:T(8,128)(2,1)} collective-permute-done((bf16[256,2048]{1,0:T(8,128)(2,1)S(1)}, bf16[256,2048]{1,0:T(8,128)(2,1)}, u32[]{:S(2)}, u32[]{:S(2)}) %collective-permute-start.66) | collective-permute-done | bytes 1048608 | tf_op jit(solution)/shard_map/ppermute | solution.py:66
  1233.6 45.6 %while.28 = (s32[]{:T(128)}, f32[1024,4,128]{0,2,1:T(8,128)S(1)}, f32[1024,4,128]{0,2,1:T(8,128)}, bf16[2,512,4,128]{3,1,0,2:T(8,128)(2,1)}, s32[2]{0:T(128)S(1)...) while((s32[]{:T(128)}, f32[1024,4,128]{0,2,1:T(8,128)S(1)}, ...), condition=%wide.region_31.33_spmd.clone, body=%wide.region_29.32_spmd.clone.sunk | while | flops 2719479808 | bytes 180947984 | solution.py:197
  1289.4 10.1 add_bitcast_fusion
  1304.2 5.9 fusion.58
  1320.5 8.8 convolution_convert_fusion
  1329.2 7.8 pad_maximum_fusion.2
  1337.1 11.8 add_bitcast_fusion.1
  1364.1 33.3 %collective-permute-done.70 = bf16[256,2048]{1,0:T(8,128)(2,1)S(1)} collective-permute-done((bf16[256,2048]{1,0:T(8,128)(2,1)S(1)}, bf16[256,2048]{1,0:T(8,128)(2,1)S(1)}, u32[]{:S(2)}, u32[]{:S(2)}) %collective-permute-start.70) | collective-permute-done | bytes 1048608 | tf_op jit(solution)/shard_map/ppermute | solution.py:66
  1399.5 10.5 add_bitcast_fusion.2
  1410.5 6.6 collective-permute-done.69
  1417.1 19.1 %collective-permute-done.71 = bf16[256,2048]{1,0:T(8,128)(2,1)S(1)} collective-permute-done((bf16[256,2048]{1,0:T(8,128)(2,1)S(1)}, bf16[256,2048]{1,0:T(8,128)(2,1)S(1)}, u32[]{:S(2)}, u32[]{:S(2)}) %collective-permute-start.71) | collective-permute-done | bytes 1048608 | tf_op jit(solution)/shard_map/ppermute | solution.py:66
  1436.3 7.1 fusion.95
  (766 shorter events, 412.5 us)
Async XLA Ops:
  7.3 365.9 %all-gather.3.cloned.1.call-start = ((), (), s32[]{:S(2)}) async-start(), calls=%async_computation.2 | async-start | bytes 9437184 | tf_op jit(solution)/shard_map/all_gather | solution.py:434
  9.7 197.5 %collective-permute-start.6 = (bf16[256,2048]{1,0:T(8,128)(2,1)S(1)}, bf16[256,2048]{1,0:T(8,128)(2,1)S(1)}, u32[]{:S(2)}, u32[]{:S(2)}) collective-permute-start(bf16[256,2048]{1,0:T(8,128)(2,1)S(1)} %copy-done.31), channel_id=1, source_target_pairs={{0,2},{2,0},{1,3},{3,1},{4,6},{6,4},{5,7},{7,5},{8,10},{10,8},{9,1... | collective-permute-start | bytes 3145736 | tf_op jit(solution)/shard_map/ppermute | solution.py:66
  13.8 198.0 %collective-permute-start.5 = (bf16[256,2048]{1,0:T(8,128)(2,1)S(1)}, bf16[256,2048]{1,0:T(8,128)(2,1)}, u32[]{:S(2)}, u32[]{:S(2)}) collective-permute-start(bf16[256,2048]{1,0:T(8,128)(2,1)S(1)} %copy-done.31), channel_id=1, source_target_pairs={{0,1},{1,0},{2,3},{3,2},{4,5},{5,4},{6,7},{7,6},{8,9},{9,8},{10,11... | collective-permute-start | bytes 3145736 | tf_op jit(solution)/shard_map/ppermute | solution.py:66
  15.4 144.8 %collective-permute-start.40 = (bf16[256,2048]{1,0:T(8,128)(2,1)}, bf16[256,2048]{1,0:T(8,128)(2,1)}, u32[]{:S(2)}, u32[]{:S(2)}) collective-permute-start(bf16[256,2048]{1,0:T(8,128)(2,1)} %param.27), channel_id=1, source_target_pairs={{0,8},{4,12},{8,0},{12,4},{16,24},{20,28},{24,16},{28,20},{1,9},{5... | collective-permute-start | bytes 3145736 | tf_op jit(solution)/shard_map/ppermute | solution.py:71
  16.9 140.7 %collective-permute-start.51 = (bf16[256,2048]{1,0:T(8,128)(2,1)}, bf16[256,2048]{1,0:T(8,128)(2,1)}, u32[]{:S(2)}, u32[]{:S(2)}) collective-permute-start(bf16[256,2048]{1,0:T(8,128)(2,1)} %param.27), channel_id=1, source_target_pairs={{0,2},{2,0},{1,3},{3,1},{4,6},{6,4},{5,7},{7,5},{8,10},{10,8},{9,1... | collective-permute-start | bytes 3145736 | tf_op jit(solution)/shard_map/ppermute | solution.py:66
  17.5 123.1 %collective-permute-start = (bf16[1,1280]{1,0:T(2,128)(2,1)S(1)}, bf16[1,1280]{1,0:T(2,128)(2,1)S(1)}, u32[]{:S(2)}, u32[]{:S(2)}) collective-permute-start(bf16[1,1280]{1,0:T(2,128)(2,1)S(1)} %broadcast_in_dim.108), channel_id=1, source_target_pairs={{0,1},{1,0},{2,3},{3,2},{4,5},{5,4},{6,7},{7,6},{8,9},{9,8},{10,11... | collective-permute-start | bytes 7688 | tf_op jit(solution)/shard_map/ppermute | solution.py:111
  154.7 45.7 %collective-permute-start.41 = (bf16[256,2048]{1,0:T(8,128)(2,1)}, bf16[256,2048]{1,0:T(8,128)(2,1)}, u32[]{:S(2)}, u32[]{:S(2)}) collective-permute-start(bf16[256,2048]{1,0:T(8,128)(2,1)} %param.27), channel_id=1, source_target_pairs={{0,16},{4,20},{8,24},{12,28},{16,0},{20,4},{24,8},{28,12},{1,17},{... | collective-permute-start | bytes 3145736 | tf_op jit(solution)/shard_map/ppermute | solution.py:71
  157.5 50.0 %collective-permute-start.42 = (bf16[256,2048]{1,0:T(8,128)(2,1)}, bf16[256,2048]{1,0:T(8,128)(2,1)S(1)}, u32[]{:S(2)}, u32[]{:S(2)}) collective-permute-start(bf16[256,2048]{1,0:T(8,128)(2,1)} %param.27), channel_id=1, source_target_pairs={{0,24},{4,28},{8,16},{12,20},{16,8},{20,12},{24,0},{28,4},{1,25},{... | collective-permute-start | bytes 3145736 | tf_op jit(solution)/shard_map/ppermute | solution.py:71
  160.2 50.5 %collective-permute-start.43 = (bf16[256,2048]{1,0:T(8,128)(2,1)}, bf16[256,2048]{1,0:T(8,128)(2,1)S(1)}, u32[]{:S(2)}, u32[]{:S(2)}) collective-permute-start(bf16[256,2048]{1,0:T(8,128)(2,1)} %param.27), channel_id=1, source_target_pairs={{0,4},{4,0},{8,12},{12,8},{16,20},{20,16},{24,28},{28,24},{1,5},{5... | collective-permute-start | bytes 3145736 | tf_op jit(solution)/shard_map/ppermute | solution.py:71
  200.4 464.1 %collective-permute-start.22 = (bf16[2048,512]{1,0:T(8,128)(2,1)}, bf16[2048,512]{1,0:T(8,128)(2,1)}, u32[]{:S(2)}, u32[]{:S(2)}) collective-permute-start(bf16[2048,512]{1,0:T(8,128)(2,1)} %bitcast.23), channel_id=1, source_target_pairs={{0,1},{1,0},{2,3},{3,2},{4,5},{5,4},{6,7},{7,6},{8,9},{9,8},{10,11... | collective-permute-start | bytes 6291464 | tf_op jit(solution)/shard_map/ppermute | solution.py:66
  207.2 388.0 %collective-permute-start.21 = (bf16[2048,512]{1,0:T(8,128)(2,1)}, bf16[2048,512]{1,0:T(8,128)(2,1)}, u32[]{:S(2)}, u32[]{:S(2)}) collective-permute-start(bf16[2048,512]{1,0:T(8,128)(2,1)} %bitcast.22), channel_id=1, source_target_pairs={{0,1},{1,0},{2,3},{3,2},{4,5},{5,4},{6,7},{7,6},{8,9},{9,8},{10,11... | collective-permute-start | bytes 6291464 | tf_op jit(solution)/shard_map/ppermute | solution.py:66
  207.5 107.7 %collective-permute-start.7 = (bf16[256,2048]{1,0:T(8,128)(2,1)S(1)}, bf16[256,2048]{1,0:T(8,128)(2,1)S(1)}, u32[]{:S(2)}, u32[]{:S(2)}) collective-permute-start(bf16[256,2048]{1,0:T(8,128)(2,1)S(1)} %collective-permute-done.6), channel_id=1, source_target_pairs={{0,1},{1,0},{2,3},{3,2},{4,5},{5,4},{6,7},{7,6},{8,9},{9,8},{10,11... | collective-permute-start | bytes 3145736 | tf_op jit(solution)/shard_map/ppermute | solution.py:66
  213.8 103.1 %collective-permute-start.46 = (bf16[256,2048]{1,0:T(8,128)(2,1)S(1)}, bf16[256,2048]{1,0:T(8,128)(2,1)S(1)}, u32[]{:S(2)}, u32[]{:S(2)}) collective-permute-start(bf16[256,2048]{1,0:T(8,128)(2,1)S(1)} %collective-permute-done.42), channel_id=1, source_target_pairs={{0,4},{4,0},{8,12},{12,8},{16,20},{20,16},{24,28},{28,24},{1,5},{5... | collective-permute-start | bytes 3145736 | tf_op jit(solution)/shard_map/ppermute | solution.py:71
  215.1 103.7 %collective-permute-start.52 = (bf16[256,2048]{1,0:T(8,128)(2,1)}, bf16[256,2048]{1,0:T(8,128)(2,1)}, u32[]{:S(2)}, u32[]{:S(2)}) collective-permute-start(bf16[256,2048]{1,0:T(8,128)(2,1)} %collective-permute-done.51), channel_id=1, source_target_pairs={{0,8},{4,12},{8,0},{12,4},{16,24},{20,28},{24,16},{28,20},{1,9},{5... | collective-permute-start | bytes 3145736 | tf_op jit(solution)/shard_map/ppermute | solution.py:71
  315.3 44.2 %collective-permute-start.53 = (bf16[256,2048]{1,0:T(8,128)(2,1)}, bf16[256,2048]{1,0:T(8,128)(2,1)}, u32[]{:S(2)}, u32[]{:S(2)}) collective-permute-start(bf16[256,2048]{1,0:T(8,128)(2,1)} %collective-permute-done.51), channel_id=1, source_target_pairs={{0,16},{4,20},{8,24},{12,28},{16,0},{20,4},{24,8},{28,12},{1,17},{... | collective-permute-start | bytes 3145736 | tf_op jit(solution)/shard_map/ppermute | solution.py:71
  317.0 68.7 %collective-permute-start.54 = (bf16[256,2048]{1,0:T(8,128)(2,1)}, bf16[256,2048]{1,0:T(8,128)(2,1)}, u32[]{:S(2)}, u32[]{:S(2)}) collective-permute-start(bf16[256,2048]{1,0:T(8,128)(2,1)} %collective-permute-done.51), channel_id=1, source_target_pairs={{0,24},{4,28},{8,16},{12,20},{16,8},{20,12},{24,0},{28,4},{1,25},{... | collective-permute-start | bytes 3145736 | tf_op jit(solution)/shard_map/ppermute | solution.py:71
  318.8 118.6 %collective-permute-start.55 = (bf16[256,2048]{1,0:T(8,128)(2,1)}, bf16[256,2048]{1,0:T(8,128)(2,1)}, u32[]{:S(2)}, u32[]{:S(2)}) collective-permute-start(bf16[256,2048]{1,0:T(8,128)(2,1)} %collective-permute-done.51), channel_id=1, source_target_pairs={{0,4},{4,0},{8,12},{12,8},{16,20},{20,16},{24,28},{28,24},{1,5},{5... | collective-permute-start | bytes 3145736 | tf_op jit(solution)/shard_map/ppermute | solution.py:71
  359.4 81.5 %collective-permute-start.56 = (bf16[256,2048]{1,0:T(8,128)(2,1)}, bf16[256,2048]{1,0:T(8,128)(2,1)}, u32[]{:S(2)}, u32[]{:S(2)}) collective-permute-start(bf16[256,2048]{1,0:T(8,128)(2,1)} %collective-permute-done.52), channel_id=1, source_target_pairs={{0,4},{4,0},{8,12},{12,8},{16,20},{20,16},{24,28},{28,24},{1,5},{5... | collective-permute-start | bytes 3145736 | tf_op jit(solution)/shard_map/ppermute | solution.py:71
  394.9 71.6 %collective-permute-start.57 = (bf16[256,2048]{1,0:T(8,128)(2,1)}, bf16[256,2048]{1,0:T(8,128)(2,1)}, u32[]{:S(2)}, u32[]{:S(2)}) collective-permute-start(bf16[256,2048]{1,0:T(8,128)(2,1)} %collective-permute-done.53), channel_id=1, source_target_pairs={{0,4},{4,0},{8,12},{12,8},{16,20},{20,16},{24,28},{28,24},{1,5},{5... | collective-permute-start | bytes 3145736 | tf_op jit(solution)/shard_map/ppermute | solution.py:71
  466.6 48.0 %collective-permute-start.12 = (bf16[256,2048]{1,0:T(8,128)(2,1)S(1)}, bf16[256,2048]{1,0:T(8,128)(2,1)S(1)}, u32[]{:S(2)}, u32[]{:S(2)}) collective-permute-start(bf16[256,2048]{1,0:T(8,128)(2,1)S(1)} %add_convert_fusion.6), channel_id=1, source_target_pairs={{0,2},{2,0},{1,3},{3,1},{4,6},{6,4},{5,7},{7,5},{8,10},{10,8},{9,1... | collective-permute-start | bytes 3145736 | tf_op jit(solution)/shard_map/ppermute | solution.py:66
  516.9 45.1 %collective-permute-start.27 = (bf16[256,2048]{1,0:T(8,128)(2,1)S(1)}, bf16[256,2048]{1,0:T(8,128)(2,1)S(1)}, u32[]{:S(2)}, u32[]{:S(2)}) collective-permute-start(bf16[256,2048]{1,0:T(8,128)(2,1)S(1)} %get-tuple-element.317), channel_id=1, source_target_pairs={{0,2},{2,0},{1,3},{3,1},{4,6},{6,4},{5,7},{7,5},{8,10},{10,8},{9,1... | collective-permute-start | bytes 3145736 | tf_op jit(solution)/shard_map/ppermute | solution.py:66
  588.8 101.5 %collective-permute-start.20 = (bf16[2048,512]{1,0:T(8,128)(2,1)}, bf16[2048,512]{1,0:T(8,128)(2,1)}, u32[]{:S(2)}, u32[]{:S(2)}) collective-permute-start(bf16[2048,512]{1,0:T(8,128)(2,1)} %bitcast.21), channel_id=1, source_target_pairs={{0,1},{1,0},{2,3},{3,2},{4,5},{5,4},{6,7},{7,6},{8,9},{9,8},{10,11... | collective-permute-start | bytes 6291464 | tf_op jit(solution)/shard_map/ppermute | solution.py:66
  592.2 47.7 %collective-permute-start.29 = (bf16[256,2048]{1,0:T(8,128)(2,1)S(1)}, bf16[256,2048]{1,0:T(8,128)(2,1)S(1)}, u32[]{:S(2)}, u32[]{:S(2)}) collective-permute-start(bf16[256,2048]{1,0:T(8,128)(2,1)S(1)} %collective-permute-done.27), channel_id=1, source_target_pairs={{0,16},{4,20},{8,24},{12,28},{16,0},{20,4},{24,8},{28,12},{1,17},{... | collective-permute-start | bytes 3145736 | tf_op jit(solution)/shard_map/ppermute | solution.py:71
  595.2 44.7 %collective-permute-start.30 = (bf16[256,2048]{1,0:T(8,128)(2,1)S(1)}, bf16[256,2048]{1,0:T(8,128)(2,1)S(1)}, u32[]{:S(2)}, u32[]{:S(2)}) collective-permute-start(bf16[256,2048]{1,0:T(8,128)(2,1)S(1)} %collective-permute-done.27), channel_id=1, source_target_pairs={{0,24},{4,28},{8,16},{12,20},{16,8},{20,12},{24,0},{28,4},{1,25},{... | collective-permute-start | bytes 3145736 | tf_op jit(solution)/shard_map/ppermute | solution.py:71
  740.0 93.0 %collective-permute-start.23 = (bf16[640,2048]{1,0:T(8,128)(2,1)}, bf16[640,2048]{1,0:T(8,128)(2,1)}, u32[]{:S(2)}, u32[]{:S(2)}) collective-permute-start(bf16[640,2048]{1,0:T(8,128)(2,1)} %get-tuple-element.347), channel_id=1, source_target_pairs={{0,4},{4,0},{8,12},{12,8},{16,20},{20,16},{24,28},{28,24},{1,5},{5... | collective-permute-start | bytes 7864328 | tf_op jit(solution)/shard_map/ppermute | solution.py:71
  752.6 62.9 %collective-permute-start.35 = (bf16[640,2048]{1,0:T(8,128)(2,1)}, bf16[640,2048]{1,0:T(8,128)(2,1)}, u32[]{:S(2)}, u32[]{:S(2)}) collective-permute-start(bf16[640,2048]{1,0:T(8,128)(2,1)} %get-tuple-element.349), channel_id=1, source_target_pairs={{0,4},{4,0},{8,12},{12,8},{16,20},{20,16},{24,28},{28,24},{1,5},{5... | collective-permute-start | bytes 7864328 | tf_op jit(solution)/shard_map/ppermute | solution.py:71
  755.3 60.2 %all-to-all-start = ((f32[16,1,256]{2,1,0:T(1,128)}), f32[16,1,256]{2,1,0:T(1,128)S(1)}, u32[]{:S(2)}, u32[]{:S(2)}) async-start(f32[16,1,256]{2,1,0:T(1,128)} %broadcast_select_fusion.2), calls=%async_computation | async-start | bytes 32768 | tf_op jit(solution)/shard_map/all_to_all | solution.py:335
  758.8 702.6 %reduce-scatter.2.cloned.1.call-start = ((), (), s32[]{:S(2)}) async-start(), calls=%async_computation.3 | async-start | bytes 9437184 | tf_op jit(solution)/shard_map/reduce_scatter | solution.py:574
  778.4 43.1 %collective-permute-start.59 = (bf16[640,2048]{1,0:T(8,128)(2,1)}, bf16[640,2048]{1,0:T(8,128)(2,1)}, u32[]{:S(2)}, u32[]{:S(2)}) collective-permute-start(bf16[640,2048]{1,0:T(8,128)(2,1)} %get-tuple-element.341), channel_id=1, source_target_pairs={{0,4},{4,0},{8,12},{12,8},{16,20},{20,16},{24,28},{28,24},{1,5},{5... | collective-permute-start | bytes 7864328 | tf_op jit(solution)/shard_map/ppermute | solution.py:71
  833.0 57.2 %collective-permute-start.62 = (bf16[256,2048]{1,0:T(8,128)(2,1)S(1)}, bf16[256,2048]{1,0:T(8,128)(2,1)S(1)}, u32[]{:S(2)}, u32[]{:S(2)}) collective-permute-start(bf16[256,2048]{1,0:T(8,128)(2,1)S(1)} %convolution_convert_fusion.13), channel_id=1, source_target_pairs={{0,24},{4,28},{8,16},{12,20},{16,8},{20,12},{24,0},{28,4},{1,25},{... | collective-permute-start | bytes 3145736 | tf_op jit(solution)/shard_map/ppermute | solution.py:71
  840.0 82.7 %collective-permute-start.37 = (bf16[256,2048]{1,0:T(8,128)(2,1)S(1)}, bf16[256,2048]{1,0:T(8,128)(2,1)S(1)}, u32[]{:S(2)}, u32[]{:S(2)}) collective-permute-start(bf16[256,2048]{1,0:T(8,128)(2,1)S(1)} %convolution_convert_fusion.20), channel_id=1, source_target_pairs={{0,16},{4,20},{8,24},{12,28},{16,0},{20,4},{24,8},{28,12},{1,17},{... | collective-permute-start | bytes 3145736 | tf_op jit(solution)/shard_map/ppermute | solution.py:71
  843.8 83.5 %collective-permute-start.38 = (bf16[256,2048]{1,0:T(8,128)(2,1)S(1)}, bf16[256,2048]{1,0:T(8,128)(2,1)S(1)}, u32[]{:S(2)}, u32[]{:S(2)}) collective-permute-start(bf16[256,2048]{1,0:T(8,128)(2,1)S(1)} %convolution_convert_fusion.19), channel_id=1, source_target_pairs={{0,24},{4,28},{8,16},{12,20},{16,8},{20,12},{24,0},{28,4},{1,25},{... | collective-permute-start | bytes 3145736 | tf_op jit(solution)/shard_map/ppermute | solution.py:71
  866.2 67.5 %collective-permute-start.48 = (bf16[256,2048]{1,0:T(8,128)(2,1)S(1)}, bf16[256,2048]{1,0:T(8,128)(2,1)S(1)}, u32[]{:S(2)}, u32[]{:S(2)}) collective-permute-start(bf16[256,2048]{1,0:T(8,128)(2,1)S(1)} %convolution_convert_fusion.18), channel_id=1, source_target_pairs={{0,8},{4,12},{8,0},{12,4},{16,24},{20,28},{24,16},{28,20},{1,9},{5... | collective-permute-start | bytes 3145736 | tf_op jit(solution)/shard_map/ppermute | solution.py:71
  868.1 99.6 %collective-permute-start.49 = (bf16[256,2048]{1,0:T(8,128)(2,1)S(1)}, bf16[256,2048]{1,0:T(8,128)(2,1)S(1)}, u32[]{:S(2)}, u32[]{:S(2)}) collective-permute-start(bf16[256,2048]{1,0:T(8,128)(2,1)S(1)} %convolution_convert_fusion.17), channel_id=1, source_target_pairs={{0,16},{4,20},{8,24},{12,28},{16,0},{20,4},{24,8},{28,12},{1,17},{... | collective-permute-start | bytes 3145736 | tf_op jit(solution)/shard_map/ppermute | solution.py:71
  890.1 80.2 %collective-permute-start.50 = (bf16[256,2048]{1,0:T(8,128)(2,1)S(1)}, bf16[256,2048]{1,0:T(8,128)(2,1)S(1)}, u32[]{:S(2)}, u32[]{:S(2)}) collective-permute-start(bf16[256,2048]{1,0:T(8,128)(2,1)S(1)} %convolution_convert_fusion.16), channel_id=1, source_target_pairs={{0,24},{4,28},{8,16},{12,20},{16,8},{20,12},{24,0},{28,4},{1,25},{... | collective-permute-start | bytes 3145736 | tf_op jit(solution)/shard_map/ppermute | solution.py:71
  922.7 53.9 %collective-permute-start.63 = (bf16[256,2048]{1,0:T(8,128)(2,1)S(1)}, bf16[256,2048]{1,0:T(8,128)(2,1)S(1)}, u32[]{:S(2)}, u32[]{:S(2)}) collective-permute-start(bf16[256,2048]{1,0:T(8,128)(2,1)S(1)} %add_convert_fusion.3), channel_id=1, source_target_pairs={{0,2},{2,0},{1,3},{3,1},{4,6},{6,4},{5,7},{7,5},{8,10},{10,8},{9,1... | collective-permute-start | bytes 3145736 | tf_op jit(solution)/shard_map/ppermute | solution.py:66
  927.3 53.2 %collective-permute-start.24 = (bf16[256,2048]{1,0:T(8,128)(2,1)S(1)}, bf16[256,2048]{1,0:T(8,128)(2,1)S(1)}, u32[]{:S(2)}, u32[]{:S(2)}) collective-permute-start(bf16[256,2048]{1,0:T(8,128)(2,1)S(1)} %convolution_convert_fusion.24), channel_id=1, source_target_pairs={{0,8},{4,12},{8,0},{12,4},{16,24},{20,28},{24,16},{28,20},{1,9},{5... | collective-permute-start | bytes 3145736 | tf_op jit(solution)/shard_map/ppermute | solution.py:71
  933.7 77.7 %collective-permute-start.25 = (bf16[256,2048]{1,0:T(8,128)(2,1)S(1)}, bf16[256,2048]{1,0:T(8,128)(2,1)S(1)}, u32[]{:S(2)}, u32[]{:S(2)}) collective-permute-start(bf16[256,2048]{1,0:T(8,128)(2,1)S(1)} %convolution_convert_fusion.23), channel_id=1, source_target_pairs={{0,16},{4,20},{8,24},{12,28},{16,0},{20,4},{24,8},{28,12},{1,17},{... | collective-permute-start | bytes 3145736 | tf_op jit(solution)/shard_map/ppermute | solution.py:71
  967.7 43.7 %collective-permute-start.26 = (bf16[256,2048]{1,0:T(8,128)(2,1)S(1)}, bf16[256,2048]{1,0:T(8,128)(2,1)S(1)}, u32[]{:S(2)}, u32[]{:S(2)}) collective-permute-start(bf16[256,2048]{1,0:T(8,128)(2,1)S(1)} %convolution_convert_fusion.22), channel_id=1, source_target_pairs={{0,24},{4,28},{8,16},{12,20},{16,8},{20,12},{24,0},{28,4},{1,25},{... | collective-permute-start | bytes 3145736 | tf_op jit(solution)/shard_map/ppermute | solution.py:71
  970.3 45.4 %collective-permute-start.39 = (bf16[256,2048]{1,0:T(8,128)(2,1)S(1)}, bf16[256,2048]{1,0:T(8,128)(2,1)S(1)}, u32[]{:S(2)}, u32[]{:S(2)}) collective-permute-start(bf16[256,2048]{1,0:T(8,128)(2,1)S(1)} %add_convert_fusion.5), channel_id=1, source_target_pairs={{0,2},{2,0},{1,3},{3,1},{4,6},{6,4},{5,7},{7,5},{8,10},{10,8},{9,1... | collective-permute-start | bytes 3145736 | tf_op jit(solution)/shard_map/ppermute | solution.py:66
  1022.7 47.4 %collective-permute-start.65 = (bf16[256,2048]{1,0:T(8,128)(2,1)S(1)}, bf16[256,2048]{1,0:T(8,128)(2,1)S(1)}, u32[]{:S(2)}, u32[]{:S(2)}) collective-permute-start(bf16[256,2048]{1,0:T(8,128)(2,1)S(1)} %get-tuple-element.309), channel_id=1, source_target_pairs={{0,2},{2,0},{1,3},{3,1},{4,6},{6,4},{5,7},{7,5},{8,10},{10,8},{9,1... | collective-permute-start | bytes 3145736 | tf_op jit(solution)/shard_map/ppermute | solution.py:66
  1022.7 53.7 %collective-permute-start.64 = (bf16[256,2048]{1,0:T(8,128)(2,1)S(1)}, bf16[256,2048]{1,0:T(8,128)(2,1)}, u32[]{:S(2)}, u32[]{:S(2)}) collective-permute-start(bf16[256,2048]{1,0:T(8,128)(2,1)S(1)} %get-tuple-element.309), channel_id=1, source_target_pairs={{0,1},{1,0},{2,3},{3,2},{4,5},{5,4},{6,7},{7,6},{8,9},{9,8},{10,11... | collective-permute-start | bytes 3145736 | tf_op jit(solution)/shard_map/ppermute | solution.py:66
  1036.1 253.2 %collective-permute-start.84 = (bf16[2048,512]{1,0:T(8,128)(2,1)}, bf16[2048,512]{1,0:T(8,128)(2,1)}, u32[]{:S(2)}, u32[]{:S(2)}) collective-permute-start(bf16[2048,512]{1,0:T(8,128)(2,1)} %fusion.57), channel_id=1, source_target_pairs={{0,1},{1,0},{2,3},{3,2},{4,5},{5,4},{6,7},{7,6},{8,9},{9,8},{10,11... | collective-permute-start | bytes 6291464 | tf_op jit(solution)/shard_map/ppermute | solution.py:66
  1036.1 301.0 %collective-permute-start.83 = (bf16[2048,512]{1,0:T(8,128)(2,1)}, bf16[2048,512]{1,0:T(8,128)(2,1)}, u32[]{:S(2)}, u32[]{:S(2)}) collective-permute-start(bf16[2048,512]{1,0:T(8,128)(2,1)} %convolution_convert_fusion.7), channel_id=1, source_target_pairs={{0,1},{1,0},{2,3},{3,2},{4,5},{5,4},{6,7},{7,6},{8,9},{9,8},{10,11... | collective-permute-start | bytes 6291464 | tf_op jit(solution)/shard_map/ppermute | solution.py:66
  1038.1 361.3 %collective-permute-start.82 = (bf16[2048,512]{1,0:T(8,128)(2,1)}, bf16[2048,512]{1,0:T(8,128)(2,1)}, u32[]{:S(2)}, u32[]{:S(2)}) collective-permute-start(bf16[2048,512]{1,0:T(8,128)(2,1)} %convolution_convert_fusion.8), channel_id=1, source_target_pairs={{0,1},{1,0},{2,3},{3,2},{4,5},{5,4},{6,7},{7,6},{8,9},{9,8},{10,11... | collective-permute-start | bytes 6291464 | tf_op jit(solution)/shard_map/ppermute | solution.py:66
  1070.0 157.5 %collective-permute-start.66 = (bf16[256,2048]{1,0:T(8,128)(2,1)S(1)}, bf16[256,2048]{1,0:T(8,128)(2,1)}, u32[]{:S(2)}, u32[]{:S(2)}) collective-permute-start(bf16[256,2048]{1,0:T(8,128)(2,1)S(1)} %collective-permute-done.65), channel_id=1, source_target_pairs={{0,1},{1,0},{2,3},{3,2},{4,5},{5,4},{6,7},{7,6},{8,9},{9,8},{10,11... | collective-permute-start | bytes 3145736 | tf_op jit(solution)/shard_map/ppermute | solution.py:66
  1361.9 55.2 %collective-permute-start.69 = (bf16[256,2048]{1,0:T(8,128)(2,1)S(1)}, bf16[256,2048]{1,0:T(8,128)(2,1)S(1)}, u32[]{:S(2)}, u32[]{:S(2)}) collective-permute-start(bf16[256,2048]{1,0:T(8,128)(2,1)S(1)} %convolution_convert_fusion.12), channel_id=1, source_target_pairs={{0,1},{1,0},{2,3},{3,2},{4,5},{5,4},{6,7},{7,6},{8,9},{9,8},{10,11... | collective-permute-start | bytes 3145736 | tf_op jit(solution)/shard_map/ppermute | solution.py:66
  1364.1 45.9 %collective-permute-start.75 = (f32[2,1216]{1,0:T(2,128)S(1)}, f32[2,1216]{1,0:T(2,128)S(1)}, u32[]{:S(2)}, u32[]{:S(2)}) collective-permute-start(f32[2,1216]{1,0:T(2,128)S(1)} %broadcast_select_fusion.4), channel_id=1, source_target_pairs={{0,2},{2,0},{1,3},{3,1},{4,6},{6,4},{5,7},{7,5},{8,10},{10,8},{9,1... | collective-permute-start | bytes 29192 | tf_op jit(solution)/shard_map/ppermute | solution.py:111
  (198 other events, 5080.0 us)
Sparse Core Ops, SparseCore 0:
  10.6 67.9 all-gather.2
  1337.2 67.7 reduce-scatter.1

commit v2 on v1

v2 whole, which is shorter than its diff:
```python
import jax
import jax.numpy as jnp
from jax import lax
from jax.experimental import pallas as pl
from jax.experimental.pallas import tpu as pltpu
from jax.sharding import PartitionSpec as P

HDIM = 128


EPSILON = 1e-05
MASKED = -1e30
LOW = jnp.bfloat16
WIDE = jnp.float32
SWAP = ((0, 1), (1, 0))


def sync(*values):
    return lax.optimization_barrier(values)


def rms_scale(values, gain):
    factor = lax.rsqrt(jnp.mean(values * values, axis=-1, keepdims=True) + EPSILON)
    return (values * factor * gain, factor)


def rms_back(values, factor, gain, grad_out):
    scaled = grad_out * gain
    mean_term = jnp.mean(scaled * values, axis=-1, keepdims=True)
    grad_values = factor * scaled - values * (factor * factor * factor) * mean_term
    return (grad_values, jnp.sum(grad_out * values * factor, axis=0))


def rope_tables(positions):
    half_size = HDIM // 2
    frequency = 10000.0 ** (-2.0 * jnp.arange(half_size, dtype=WIDE) / HDIM)
    angles = positions.astype(WIDE)[:, None] * frequency[None, :]
    cosine, sine = jnp.cos(angles), jnp.sin(angles)
    return (
        jnp.concatenate([cosine, cosine], axis=1),
        jnp.concatenate([-sine, sine], axis=1),
    )


def contract_last(left, right):
    return lax.dot_general(
        left, right, (((1,), (1,)), ((), ())), preferred_element_type=jnp.float32
    )


def contract_first(left, right):
    return lax.dot_general(
        left, right, (((0,), (0,)), ((), ())), preferred_element_type=jnp.float32
    )


def plain(left, right):
    return jnp.dot(left, right, preferred_element_type=jnp.float32)


def swap(values, axis):
    return lax.ppermute(values, axis, SWAP)


def hop(values, distance):
    count = lax.axis_size("shard")
    return lax.ppermute(values, "shard", tuple((i, i ^ distance) for i in range(count)))


def gather_group(block):
    near = swap(block, "tensor")
    across = swap(block, "context")
    return [block, near, across, swap(across, "tensor")]


def scatter_group(parts):
    far, near = sync(swap(parts[3].astype(LOW), "tensor"), parts[1].astype(LOW))
    across = swap((parts[2] + far.astype(WIDE)).astype(LOW), "context")
    return parts[0] + swap(near, "tensor").astype(WIDE) + across.astype(WIDE)


def over_chips(blocks):
    count = lax.axis_size("shard")
    groups = [list(range(core, count, 2)) for core in range(2)]
    return lax.all_to_all(
        blocks, "shard", split_axis=0, concat_axis=0, axis_index_groups=groups, tiled=True
    )


def gather_chips(block):
    chips = lax.axis_size("shard") // 2
    return over_chips(jnp.broadcast_to(block[None], (chips,) + block.shape))


DEVICES = ("shard", "context", "tensor")


def deal(rows):
    return lax.all_to_all(rows, DEVICES, split_axis=0, concat_axis=0, tiled=True)


def device_total():
    return lax.axis_size("shard") * lax.axis_size("context") * lax.axis_size("tensor")


def gather_small(row):
    return deal(jnp.broadcast_to(row[None], (device_total(), row.shape[0])))


def scatter_small(rows):
    return jnp.sum(deal(rows), axis=0)


def params():
    return pltpu.CompilerParams(vmem_limit_bytes=48 * 1024 * 1024)


def as_column(row, width):
    return jnp.broadcast_to(row, (width, row.shape[1])).T


def turn(values, cosine, sine):
    return values * cosine + pltpu.roll(values, HDIM // 2, 1) * sine


def norm_factors(squares_ref, width):
    factors = lax.rsqrt(squares_ref[...] / width + EPSILON)
    return as_column(factors[0:1], HDIM), as_column(factors[1:2], HDIM)


def prepare_kernel(width, pre_ref, squares_ref, gain_ref, cos_ref, sin_ref, q_ref, k_ref, v_ref):
    span = q_ref.shape[1]
    cosine, sine = cos_ref[...], sin_ref[...]
    factors = norm_factors(squares_ref, width)
    for which, out_ref in ((0, q_ref), (1, k_ref)):
        for first in range(0, span, HDIM):
            cols = slice(which * span + first, which * span + first + HDIM)
            gain = gain_ref[which : which + 1, first : first + HDIM]
            normed = pre_ref[:, cols] * factors[which] * gain
            out_ref[:, first : first + HDIM] = turn(normed, cosine, sine).astype(LOW)
    v_ref[...] = pre_ref[:, 2 * span :].astype(LOW)


def prepare(pre, squares, gain_cols, cosine, sine, width, block):
    rows, total = pre.shape
    span = total // 3
    row_block = lambda cols: pl.BlockSpec((block, cols), lambda i: (i, 0))
    return pl.pallas_call(
        lambda *refs: prepare_kernel(width, *refs),
        grid=(rows // block,),
        in_specs=[
            row_block(total),
            pl.BlockSpec((2, block), lambda i: (0, i)),
            pl.BlockSpec((2, span), lambda i: (0, 0)),
            row_block(HDIM),
            row_block(HDIM),
        ],
        out_specs=[row_block(span)] * 3,
        out_shape=[jax.ShapeDtypeStruct((rows, span), LOW)] * 3,
        compiler_params=params(),
        cost_estimate=pl.CostEstimate(
            flops=10 * rows * total, bytes_accessed=6 * rows * total, transcendentals=0
        ),
    )(pre, squares, gain_cols, cosine, sine)


def visible(group, which, keys, queries):
    line = lax.broadcasted_iota(jnp.int32, (keys, queries), 0)
    key_place = ((line // queries) ^ group) * queries + line % queries
    query_place = (which ^ group) * queries + lax.broadcasted_iota(
        jnp.int32, (keys, queries), 1
    )
    return query_place >= key_place


def dot_last(left, right):
    return lax.dot_general(left, right, (((1,), (1,)), ((), ())), preferred_element_type=WIDE)


def dot_first(left, right):
    return lax.dot_general(left, right, (((0,), (0,)), ((), ())), preferred_element_type=WIDE)


def attend_kernel(which, group_ref, q_ref, k_ref, v_ref, out_ref, log_ref):
    keys, queries = k_ref.shape[0], q_ref.shape[0]
    scores = dot_last(k_ref[...], q_ref[...]) * HDIM ** (-0.5)
    scores = jnp.where(visible(group_ref[0], which, keys, queries), scores, MASKED)
    maximum = jnp.max(scores, axis=0, keepdims=True)
    weights = jnp.exp(scores - maximum)
    total = jnp.sum(weights, axis=0, keepdims=True)
    attn_low = (weights * (1.0 / total)).astype(LOW)
    out_ref[...] = dot_first(v_ref[...], attn_low).T.astype(LOW)
    log_ref[...] = (maximum + jnp.log(total))[None]


def attend_block(which, group, queries, keys, values, block):
    rows, span = queries.shape
    heads = span // HDIM
    whole = pl.BlockSpec((rows, HDIM), lambda h, g: (0, h))
    return pl.pallas_call(
        lambda *refs: attend_kernel(which, *refs),
        grid_spec=pltpu.PrefetchScalarGridSpec(
            num_scalar_prefetch=1,
            grid=(heads,),
            in_specs=[pl.BlockSpec((block, HDIM), lambda h, g: (which, h)), whole, whole],
            out_specs=[
                pl.BlockSpec((block, HDIM), lambda h, g: (0, h)),
                pl.BlockSpec((1, 1, block), lambda h, g: (h, 0, 0)),
            ],
        ),
        out_shape=[
            jax.ShapeDtypeStruct((block, span), LOW),
            jax.ShapeDtypeStruct((heads, 1, block), WIDE),
        ],
        compiler_params=params(),
        cost_estimate=pl.CostEstimate(
            flops=4 * block * rows * span,
            bytes_accessed=4 * rows * span,
            transcendentals=block * rows * heads,
        ),
    )(group, queries, keys, values)


def attend_back_kernel(which, first, group_ref, q_ref, k_ref, v_ref, grad_ref, log_ref, *refs):
    keys, queries = k_ref.shape[0], q_ref.shape[0]
    grad_q_ref, grad_k_ref, grad_v_ref = refs[-3:]
    scores = dot_last(k_ref[...], q_ref[...]) * HDIM ** (-0.5)
    probs = jnp.exp(scores - log_ref[0])
    probs = jnp.where(visible(group_ref[0], which, keys, queries), probs, 0.0)
    grad_probs = dot_last(v_ref[...], grad_ref[...])
    delta = jnp.sum(probs * grad_probs, axis=0, keepdims=True)
    grad_scores = (probs * (grad_probs - delta)).astype(LOW)
    grad_q_ref[...] = (dot_first(k_ref[...], grad_scores).T * HDIM ** (-0.5)).astype(LOW)
    key_part = plain(grad_scores, q_ref[...]) * HDIM ** (-0.5)
    value_part = plain(probs.astype(LOW), grad_ref[...])
    grad_k_ref[...] = key_part if first else refs[0][...] + key_part
    grad_v_ref[...] = value_part if first else refs[1][...] + value_part


def attend_block_back(which, group, queries, keys, values, grad, logs, sums, block):
    rows, span = queries.shape
    heads = span // HDIM
    whole = pl.BlockSpec((rows, HDIM), lambda h, g: (0, h))
    own = pl.BlockSpec((block, HDIM), lambda h, g: (0, h))
    carried = [] if sums is None else list(sums)
    return pl.pallas_call(
        lambda *refs: attend_back_kernel(which, sums is None, *refs),
        grid_spec=pltpu.PrefetchScalarGridSpec(
            num_scalar_prefetch=1,
            grid=(heads,),
            in_specs=[
                pl.BlockSpec((block, HDIM), lambda h, g: (which, h)),
                whole,
                whole,
                own,
                pl.BlockSpec((1, 1, block), lambda h, g: (h, 0, 0)),
            ]
            + [whole] * len(carried),
            out_specs=[own, whole, whole],
        ),
        out_shape=[
            jax.ShapeDtypeStruct((block, span), LOW),
            jax.ShapeDtypeStruct((rows, span), WIDE),
            jax.ShapeDtypeStruct((rows, span), WIDE),
        ],
        compiler_params=params(),
        cost_estimate=pl.CostEstimate(
            flops=10 * block * rows * span,
            bytes_accessed=20 * rows * span,
            transcendentals=block * rows * heads,
        ),
    )(group, queries, keys, values, grad, logs, *carried)


def turned_back(which, first, grads, cosine, sine):
    values = grads[which][:, first : first + HDIM].astype(WIDE)
    return turn(values, cosine, -sine)


def norm_sums_kernel(
    width, gq_ref, gk_ref, pre_ref, squares_ref, gain_ref, cos_ref, sin_ref, total_ref, col_ref
):
    span = gq_ref.shape[1]
    cosine, sine = cos_ref[...], sin_ref[...]
    factors = norm_factors(squares_ref, width)

    @pl.when(pl.program_id(0) == 0)
    def _():
        col_ref[...] = jnp.zeros_like(col_ref)

    for which in range(2):
        total = jnp.zeros(cosine.shape, WIDE)
        for first in range(0, span, HDIM):
            grad = turned_back(which, first, (gq_ref, gk_ref), cosine, sine)
            cols = slice(which * span + first, which * span + first + HDIM)
            product = grad * pre_ref[:, cols]
            total = total + product * gain_ref[which : which + 1, first : first + HDIM]
            col_ref[which : which + 1, first : first + HDIM] += jnp.sum(
                product * factors[which], axis=0, keepdims=True
            )
        total_ref[which : which + 1, :] = jnp.sum(total.T, axis=0, keepdims=True)


def norm_grads_kernel(
    width,
    gq_ref,
    gk_ref,
    gv_ref,
    pre_ref,
    squares_ref,
    total_ref,
    gain_ref,
    cos_ref,
    sin_ref,
    out_ref,
):
    span = gq_ref.shape[1]
    cosine, sine = cos_ref[...], sin_ref[...]
    factors = norm_factors(squares_ref, width)
    for which in range(2):
        factor = factors[which]
        mean = as_column(total_ref[which : which + 1] / width, HDIM)
        pull = factor * factor * factor * mean
        for first in range(0, span, HDIM):
            grad = turned_back(which, first, (gq_ref, gk_ref), cosine, sine)
            cols = slice(which * span + first, which * span + first + HDIM)
            scaled = grad * gain_ref[which : which + 1, first : first + HDIM]
            out_ref[:, cols] = (factor * scaled - pre_ref[:, cols] * pull).astype(LOW)
    out_ref[:, 2 * span :] = gv_ref[...].astype(LOW)


def norm_call(body, operands, kinds, outs, width, block):
    def spec(shape, kind):
        if kind == "rows":
            return pl.BlockSpec((block, shape[1]), lambda i: (i, 0))
        if kind == "line":
            return pl.BlockSpec((shape[0], block), lambda i: (0, i))
        return pl.BlockSpec(shape, lambda i: (0, 0))

    size = sum(o.size * o.dtype.itemsize for o in operands)
    return pl.pallas_call(
        lambda *refs: body(width, *refs),
        grid=(operands[0].shape[0] // block,),
        in_specs=[spec(o.shape, kind) for o, kind in zip(operands, kinds)],
        out_specs=[spec(shape, kind) for shape, _, kind in outs],
        out_shape=[jax.ShapeDtypeStruct(shape, dtype) for shape, dtype, _ in outs],
        compiler_params=params(),
        cost_estimate=pl.CostEstimate(flops=4 * size, bytes_accessed=size, transcendentals=0),
    )(*operands)


def silu_parts(gate_act):
    sigmoid_value = jax.nn.sigmoid(gate_act)
    return (gate_act * sigmoid_value, sigmoid_value)


def expert_hidden(rows, weights):
    gate_act = plain(rows, weights[0])
    up_act = plain(rows, weights[1])
    return (gate_act, up_act, (silu_parts(gate_act)[0] * up_act).astype(LOW))


def expert_produce(hidden_act, weights):
    return contract_last(hidden_act, weights[2]).astype(LOW)


def expert_forward(rows, weights):
    kept = expert_hidden(rows, weights)
    return (expert_produce(kept[2], weights), kept)


def expert_backward(grad_rows, kept, weights):
    gate_weight, up_weight, down_weight = weights
    gate_act, up_act, hidden_act = kept
    grad_hidden = plain(grad_rows, down_weight)
    activated, sigmoid_value = silu_parts(gate_act)
    grad_gate_act = (
        grad_hidden * up_act * sigmoid_value * (1.0 + gate_act * (1.0 - sigmoid_value))
    ).astype(LOW)
    grad_up_act = (grad_hidden * activated).astype(LOW)
    grad_route = contract_last(grad_gate_act, gate_weight) + contract_last(grad_up_act, up_weight)
    return (grad_route, grad_gate_act, grad_up_act)


def their_grad(left, right):
    return contract_first(left, right[:, right.shape[1] // 2 :]).astype(LOW)


def own_grad(left, right, arrived):
    mine = contract_first(left, right[:, : right.shape[1] // 2])
    return (mine + arrived.astype(WIDE))[None]


def halves(values):
    half = values.shape[0] // 2
    return (values[:half], values[half:])


def with_partner(held):
    return jnp.concatenate([held, swap(held, "tensor")], axis=1)


def softmax_rows(logits):
    weights = jnp.exp(logits - jnp.max(logits, axis=-1, keepdims=True))
    return weights / jnp.sum(weights, axis=-1, keepdims=True)


def pick_rows(picks, other_picks, blocks):
    pick = jnp.concatenate([picks, other_picks], axis=1)
    chosen = jnp.einsum("bst,btd->bsd", pick, blocks, preferred_element_type=jnp.float32)
    chosen = chosen.astype(LOW)
    capacity, width = picks.shape[1], blocks.shape[2]
    kept = chosen[:, :capacity].reshape(-1, width)
    arrived = hop(chosen[:, capacity:].reshape(-1, width), 1)
    return jnp.concatenate([kept, arrived], axis=0)


def slot_picks(ids, expert, capacity):
    routed = jnp.any(ids == expert, axis=1)
    tokens = ids.shape[2]
    line = jnp.arange(tokens, dtype=jnp.int32)
    earlier = (line[:, None] < line[None, :]).astype(LOW)
    position = plain(routed.astype(LOW), earlier).astype(jnp.int32)
    position = jnp.where(routed, position, -1)
    slots = jnp.arange(capacity, dtype=jnp.int32)
    return (position[:, None, :] == slots[None, :, None]).astype(LOW)


def chip_parts(rows, picks, other_picks):
    half = rows.shape[0] // 2
    return combine(rows[:half], hop(rows[half:], 1), picks, other_picks)


def combine(kept, arrived, picks, other_picks):
    shape = picks.shape[:2] + kept.shape[1:]
    both = jnp.concatenate([kept.reshape(shape), arrived.reshape(shape)], axis=1)
    pick = jnp.concatenate([picks, other_picks], axis=1)
    parts = jnp.einsum("bst,bsd->btd", pick, both, preferred_element_type=jnp.float32)
    return parts.astype(LOW)


def sum_chips(parts):
    return jnp.sum(over_chips(parts).astype(WIDE), axis=0)


def experts_by_blocks(
    low_second, cot_near, cot_far, all_ids, router, gate_weight, w_up, w_down, capacity
):
    shard, context = lax.axis_index("shard"), lax.axis_index("context")
    contexts = lax.axis_size("context")
    expert = shard * contexts + context
    other_expert = (shard ^ 1) * contexts + context
    token_count = low_second.shape[0]
    chips = lax.axis_size("shard") // 2
    same_core = 2 * jnp.arange(chips, dtype=jnp.int32) + (shard & 1)
    picks = []
    for turn in range(2):
        ids = jnp.take(all_ids, same_core * contexts + (context ^ turn), axis=0)
        far_ids = jnp.take(all_ids, (same_core ^ 1) * contexts + (context ^ turn), axis=0)
        picks.append(
            (
                slot_picks(ids, expert, capacity),
                slot_picks(ids, other_expert, capacity),
                slot_picks(far_ids, expert, capacity),
            )
        )

    def arrive(turn, rows):
        probs = softmax_rows(plain(rows, router))
        mine = jnp.arange(probs.shape[1], dtype=jnp.int32)[None, :] == expert
        return jnp.sum(jnp.where(mine, probs, 0.0), axis=1, keepdims=True)

    def leave(turn, produced, cot_rows, gate):
        cot_wide = cot_rows.astype(WIDE)
        produced_wide = produced.astype(WIDE)
        slot_grad = jnp.sum(produced_wide * cot_wide, axis=1)
        all_picks = jnp.concatenate([picks[turn][0], picks[turn][2]], axis=0).astype(WIDE)
        gate_grad = jnp.sum(all_picks * slot_grad.reshape(2 * chips, capacity)[:, :, None], axis=1)
        return (gate_grad, (gate * cot_wide).astype(LOW), (gate * produced_wide).astype(LOW))

    up_halves = halves(w_up)
    near_chunk, across, up_first, up_late = sync(
        gather_chips(low_second),
        swap(low_second, "context"),
        swap(up_halves[0], "tensor"),
        up_halves[1],
    )
    near_rows = pick_rows(*picks[0][:2], near_chunk)
    near_rows, up_second, w_down, cot_near = sync(
        near_rows, swap(up_late, "tensor"), w_down, cot_near
    )
    up_arrived = jnp.concatenate([up_first, up_second], axis=0)
    weights = (
        gate_weight,
        jnp.concatenate([w_up, up_arrived], axis=1),
        with_partner(w_down),
    )
    near_kept = expert_hidden(near_rows, weights)
    near_hidden, far_chunk = sync(near_kept[2], gather_chips(across))
    near_kept = near_kept[:2] + (near_hidden,)
    far_rows = pick_rows(*picks[1][:2], far_chunk)
    far_kept = expert_hidden(far_rows, weights)
    near_cot, far_cot = pick_rows(*picks[0][:2], cot_near), pick_rows(*picks[1][:2], cot_far)
    gate = arrive(0, near_rows)
    produced = expert_produce(near_hidden, weights)
    near_gate_grad, near_grad_rows, weighted = leave(0, produced, near_cot, gate)
    mixture_parts = chip_parts(weighted, *picks[0][:2])
    gate = arrive(1, far_rows)
    produced = expert_produce(far_kept[2], weights)
    far_gate_grad, far_grad_rows, far_weighted = leave(1, produced, far_cot, gate)
    gate_grads = [near_gate_grad, far_gate_grad]
    rest_parts = chip_parts(far_weighted, *picks[1][:2])
    far_grad_rows, mixture_parts = sync(far_grad_rows, mixture_parts)
    mixture = sum_chips(mixture_parts)

    def both(near, far):
        return jnp.concatenate([near, far], axis=0)

    far_route, far_gate_act, far_up_act = expert_backward(far_grad_rows, far_kept, weights)
    down_pair = (both(near_grad_rows, far_grad_rows), both(near_kept[2], far_kept[2]))
    down_theirs = their_grad(*down_pair)
    far_parts = chip_parts(far_route.astype(LOW), *picks[1][:2])
    near_grad_rows, far_parts, down_theirs, mixture, rest_parts = sync(
        near_grad_rows, far_parts, down_theirs, mixture, rest_parts
    )
    near_route, near_gate_act, near_up_act = expert_backward(near_grad_rows, near_kept, weights)
    near_route = near_route.astype(LOW)
    near_half = near_route.shape[0] // 2
    near_swapped, far_grad = sync(
        hop(near_route[near_half:], 1), sum_chips(far_parts).astype(LOW)
    )
    near_parts = combine(near_route[:near_half], near_swapped, *picks[0][:2])
    all_rows = both(near_rows, far_rows)
    gate_pair = (all_rows, both(near_gate_act, far_gate_act))
    up_pair = (all_rows, both(near_up_act, far_up_act))
    gate_theirs = their_grad(*gate_pair)
    far_arrived = swap(far_grad, "context")
    grad, rest_parts, gate_theirs, down_arrived = sync(
        sum_chips(near_parts) + far_arrived.astype(WIDE),
        rest_parts,
        gate_theirs,
        swap(down_theirs, "tensor"),
    )
    up_theirs = their_grad(*up_pair)
    lines = jnp.stack(gate_grads, axis=1)
    lines = jnp.where(context == 0, lines, lines[:, ::-1])
    mine, far = lines[:chips], lines[chips:]
    low_core = (shard & 1) == 0
    lines = jnp.stack([jnp.where(low_core, mine, far), jnp.where(low_core, far, mine)], axis=1)
    lines = lines.reshape(-1, token_count)
    by_expert = lax.all_to_all(lines, ("shard", "context"), split_axis=0, concat_axis=0, tiled=True)
    later = (mixture, rest_parts, gate_theirs, up_theirs, gate_pair, up_pair, down_pair, down_arrived)
    return (grad, by_expert.T, later)


def move_slots(buffer):
    return lax.all_to_all(buffer, ("shard", "context"), split_axis=0, concat_axis=0, tiled=True)


def experts_by_slots(low_second, cotangent, expert_ids, router_probs, weights, capacity):
    row_count, model_width = low_second.shape
    expert_count = router_probs.shape[1]
    top_count = expert_ids.shape[1]
    choose = expert_ids[:, :, None] == jnp.arange(expert_count, dtype=jnp.int32)[None, None, :]
    gate_probs = jnp.sum(jnp.where(choose, router_probs[:, None, :], 0.0), axis=2)
    route_total = row_count * top_count
    flat_ids = expert_ids.reshape(-1)
    onehot = (flat_ids[:, None] == jnp.arange(expert_count, dtype=jnp.int32)[None, :]).astype(
        jnp.int32
    )
    before = jnp.cumsum(onehot, axis=0) - onehot
    route_slot = flat_ids * capacity + jnp.sum(before * onehot, axis=1)
    route_of_slot = (
        jnp.full((expert_count * capacity,), route_total, jnp.int32)
        .at[route_slot]
        .set(jnp.arange(route_total, dtype=jnp.int32))
    )
    filled = route_of_slot < route_total
    route_clipped = jnp.minimum(route_of_slot, route_total - 1)
    token_of_slot = route_clipped // top_count
    slot_shape = (expert_count, capacity, model_width)
    flat_shape = (expert_count * capacity, model_width)
    sending = jnp.where(filled[:, None], low_second[token_of_slot], jnp.zeros((), LOW))
    rows = move_slots(sending.reshape(slot_shape)).reshape(flat_shape)
    produced, kept = expert_forward(rows, weights)
    returned = move_slots(produced.reshape(slot_shape)).reshape(flat_shape)
    chosen = returned[route_slot].reshape(row_count, top_count, model_width).astype(WIDE)
    mixture = jnp.sum(gate_probs[:, :, None] * chosen, axis=1)
    grad_top = cotangent.astype(WIDE)
    grad_gates = jnp.sum(chosen * grad_top[:, None, :], axis=2)
    slot_gate = jnp.where(filled, gate_probs.reshape(-1)[route_clipped], 0.0)
    sending_grad = (slot_gate[:, None] * grad_top[token_of_slot]).astype(LOW)
    grad_rows = move_slots(sending_grad.reshape(slot_shape)).reshape(flat_shape)
    grad_route, grad_gate_act, grad_up_act = expert_backward(grad_rows, kept, weights)
    returned_grad = move_slots(grad_route.astype(LOW).reshape(slot_shape)).reshape(flat_shape)
    grad = jnp.sum(
        returned_grad[route_slot].reshape(row_count, top_count, model_width).astype(WIDE), axis=1
    )
    by_expert = jnp.sum(jnp.where(choose, grad_gates[:, :, None], 0.0), axis=1)
    pairs = [(rows, grad_gate_act), (rows, grad_up_act), (grad_rows, kept[2])]
    grads = tuple(own_grad(*pair, swap(their_grad(*pair), "tensor")) for pair in pairs)
    return (grad, by_expert, mixture, grads)


def local(
    hidden_in,
    cotangent,
    w_query,
    w_key,
    w_value,
    w_out,
    w_router,
    norm_first,
    norm_second,
    query_gain,
    key_gain,
    w_gate,
    w_up,
    w_down,
    expert_ids,
):
    group_index = lax.axis_index(("context", "tensor"))
    row_count, model_width = hidden_in.shape
    column_span = w_query.shape[1]
    expert_count = w_router.shape[1]
    top_count = expert_ids.shape[1]
    capacity = max(2, row_count * top_count * 5 // (4 * expert_count))
    by_blocks = 2 * capacity >= row_count
    device_count = model_width // norm_first.shape[0]

    router_rows = w_router.shape[0]
    small = gather_small(
        jnp.concatenate(
            [
                w_router.reshape(-1),
                norm_first,
                norm_second,
                query_gain,
                key_gain,
                expert_ids.T.reshape(-1).astype(LOW),
            ],
            axis=0,
        )
    )
    hidden_blocks = gather_group(hidden_in)
    hidden_blocks[3], gate_early = sync(hidden_blocks[3], w_gate[0, : model_width // 2])
    packed = lax.all_gather(
        jnp.concatenate([w_query, w_key, w_value, w_out], axis=1), "shard", axis=0, tiled=True
    )
    router_size = router_rows * expert_count
    router_full = small[:, :router_size].reshape(model_width, expert_count)
    gains = [
        small[:, router_size + i * router_rows : router_size + (i + 1) * router_rows]
        .reshape(model_width)
        .astype(WIDE)
        for i in range(4)
    ]
    gain_first, gain_second, gain_query, gain_key = gains
    if by_blocks:
        tensors = lax.axis_size("tensor")
        all_ids = small[:, router_size + 4 * router_rows :].astype(jnp.int32)
        all_ids = all_ids.reshape(-1, tensors, top_count, row_count)
        all_ids = lax.dynamic_index_in_dim(all_ids, lax.axis_index("tensor"), 1, False)

    qkv_cols = packed[:, : 3 * column_span]
    out_cols = packed[:, 3 * column_span :]
    inputs = hidden_in.astype(WIDE)
    factor_first = rms_scale(inputs, gain_first)[1]
    low_blocks, pre_blocks = [], []
    for block in hidden_blocks:
        low_block = rms_scale(block.astype(WIDE), gain_first)[0].astype(LOW)
        low_blocks.append(low_block)
        pre_blocks.append(plain(low_block, qkv_cols))
    low_group = jnp.concatenate(low_blocks, axis=0)
    pre = jnp.concatenate(pre_blocks, axis=0)
    group_rows = low_group.shape[0]
    line = jnp.arange(group_rows, dtype=jnp.int32)
    place = ((line // row_count) ^ group_index) * row_count + line % row_count
    cosine, sine = rope_tables(place)
    gain_cols = jnp.stack(
        [
            lax.dynamic_slice_in_dim(gain, group_index * column_span, column_span, 0)
            for gain in (gain_query, gain_key)
        ]
    )

    def over_group(stacked):
        stacked = stacked.reshape(2, 4, -1)
        stacked = stacked + swap(stacked, "tensor")[:, jnp.array([1, 0, 3, 2])]
        stacked = stacked + swap(stacked, "context")[:, jnp.array([2, 3, 0, 1])]
        return stacked.reshape(2, -1)

    half_rows = model_width // 2
    gate_first = swap(gate_early, "tensor")
    own_squares, gate_first, early_cot = sync(
        jnp.stack(
            [
                jnp.sum(jnp.square(pre[:, i * column_span : (i + 1) * column_span]), axis=1)
                for i in range(2)
            ]
        ),
        gate_first,
        cotangent,
    )
    if by_blocks:
        cot_near = gather_chips(early_cot)
        cot_across = swap(early_cot, "context")
    squares, gate_late = sync(over_group(own_squares), w_gate[0, half_rows:])
    gate_second = swap(gate_late, "tensor")
    query_heads, key_heads, value_heads = prepare(
        pre, squares, gain_cols, cosine, sine, model_width, row_count
    )
    group = group_index[None].astype(jnp.int32)
    blocks, logs = [None] * 4, [None] * 4
    for k in (3, 2, 1, 0):
        blocks[k], logs[k] = attend_block(
            k, group, query_heads, key_heads, value_heads, row_count
        )
    parts = [contract_last(block, out_cols) for block in blocks]
    far_part, gate_second = sync(parts[3].astype(LOW), gate_second)
    gate_weight = jnp.concatenate(
        [w_gate[0], jnp.concatenate([gate_first, gate_second], axis=0)], axis=1
    )
    far = swap(far_part, "tensor")
    far, near_part, part = sync(far, parts[1].astype(LOW), parts[2])
    if by_blocks:
        far, cot_near, cot_across = sync(far, cot_near, cot_across)
    across = swap((part + far.astype(WIDE)).astype(LOW), "context")
    near = swap(near_part, "tensor")
    if by_blocks:
        across, cot_far, gate_weight = sync(across, gather_chips(cot_across), gate_weight)
    middle = inputs + parts[0] + near.astype(WIDE) + across.astype(WIDE)
    normed_second, factor_second = rms_scale(middle, gain_second)
    low_second = normed_second.astype(LOW)
    router_probs = softmax_rows(plain(low_second, router_full))
    low_second, late_up, late_down = sync(low_second, w_up[0], w_down[0])
    if by_blocks:
        grad_from_experts, grad_router_probs, later = experts_by_blocks(
            low_second,
            cot_near,
            cot_far,
            all_ids,
            router_full,
            gate_weight,
            late_up,
            late_down,
            capacity,
        )
        mixture, rest_parts, gate_theirs, up_theirs, gate_pair, up_pair, down_pair, arrived = later
    else:
        weights = (gate_weight, with_partner(late_up), with_partner(late_down))
        grad_from_experts, grad_router_probs, mixture, expert_grads = experts_by_slots(
            low_second, cotangent, expert_ids, router_probs, weights, capacity
        )
    grad_logits = (
        router_probs
        * (grad_router_probs - jnp.sum(router_probs * grad_router_probs, axis=1, keepdims=True))
    ).astype(LOW)
    grad_router_weight = contract_first(low_second, grad_logits)
    grad_second = grad_from_experts + contract_last(grad_logits, router_full)
    grad_normed_second, grad_gain_second = rms_back(middle, factor_second, gain_second, grad_second)
    grad_middle = cotangent.astype(WIDE) + grad_normed_second
    grad_branch = grad_middle.astype(LOW)
    near_piece, across = swap(grad_branch, "tensor"), swap(grad_branch, "context")

    def piece_back(k, piece, sums):
        grad_queries, *sums = attend_block_back(
            k,
            group,
            query_heads,
            key_heads,
            value_heads,
            plain(piece, out_cols).astype(LOW),
            logs[k],
            sums,
            row_count,
        )
        return (grad_queries, tuple(sums))

    own_query, own_sums = piece_back(0, grad_branch, None)
    if by_blocks:
        down_grad = own_grad(*down_pair, arrived)
        rest = sum_chips(rest_parts).astype(LOW)
    near_query, near_sums = piece_back(1, near_piece, own_sums)
    if by_blocks:
        across, near_sums, down_grad, rest, up_theirs = sync(
            across, near_sums, down_grad, rest, up_theirs
        )
        rest_arrived = swap(rest, "context")
    last = swap(across, "tensor")
    across_query, across_sums = piece_back(2, across, near_sums)
    if by_blocks:
        gate_halves = halves(gate_theirs)
        last, across_sums, gate_early = sync(last, across_sums, gate_halves[0])
    pieces = [grad_branch, near_piece, across, last]
    last_query, sums = piece_back(3, last, across_sums)
    grad_queries = [own_query, near_query, across_query, last_query]
    grad_query_heads = jnp.concatenate(grad_queries, axis=0)
    out_total = contract_first(pieces[0], blocks[0])
    for k in range(1, 4):
        out_total = out_total + contract_first(pieces[k], blocks[k])
    out_grad = lax.psum_scatter(out_total.astype(LOW), "shard", scatter_dimension=0, tiled=True)
    totals, gain_grads = norm_call(
        norm_sums_kernel,
        (grad_query_heads, sums[0], pre, squares, gain_cols, cosine, sine),
        ("rows", "rows", "rows", "line", "whole", "rows", "rows"),
        (((2, group_rows), WIDE, "line"), ((2, column_span), WIDE, "whole")),
        model_width,
        row_count,
    )
    if by_blocks:
        totals, rest_arrived, gate_first, gate_late = sync(
            totals, rest_arrived, swap(gate_early, "tensor"), gate_halves[1]
        )
        mixture = mixture + rest_arrived.astype(WIDE)
    block_output = (middle + mixture).astype(LOW)
    totals = over_group(totals)
    if by_blocks:
        totals, gate_late = sync(totals, gate_late)
    (grad_pre,) = norm_call(
        norm_grads_kernel,
        (grad_query_heads, *sums, pre, squares, totals, gain_cols, cosine, sine),
        ("rows", "rows", "rows", "rows", "line", "line", "whole", "rows", "rows"),
        (((group_rows, 3 * column_span), LOW, "rows"),),
        model_width,
        row_count,
    )

    def block_of(values, k):
        return values[k * row_count : (k + 1) * row_count]

    far_part = contract_last(block_of(grad_pre, 3), qkv_cols).astype(LOW)
    if by_blocks:
        far_part, grad_pre, gate_second = sync(far_part, grad_pre, swap(gate_late, "tensor"))
    far = swap(far_part, "tensor")
    head_total = contract_first(low_group, grad_pre).astype(LOW)
    parts = [contract_last(block_of(grad_pre, k), qkv_cols) for k in range(3)]
    far, head_total, parts[1], parts[2] = sync(far, head_total, parts[1].astype(LOW), parts[2])
    across = swap((parts[2] + far.astype(WIDE)).astype(LOW), "context")
    near = swap(parts[1], "tensor")
    head_grads = lax.psum_scatter(head_total, "shard", scatter_dimension=0, tiled=True).astype(WIDE)
    if by_blocks:
        near, across, gain_grads, up_theirs = sync(near, across, gain_grads, up_theirs)
        up_arrived = swap(up_theirs, "tensor")
        gate_arrived = jnp.concatenate([gate_first, gate_second], axis=0)
        expert_grads = (
            own_grad(*gate_pair, gate_arrived),
            own_grad(*up_pair, up_arrived),
            down_grad,
        )
    grad_first = parts[0] + near.astype(WIDE) + across.astype(WIDE)
    grad_normed_first, grad_gain_first = rms_back(inputs, factor_first, gain_first, grad_first)
    grad_input = grad_middle + grad_normed_first
    zero_gain = jnp.zeros((2, model_width), WIDE)
    grad_gains = lax.dynamic_update_slice(zero_gain, gain_grads, (0, group_index * column_span))
    by_device = [
        one.reshape(device_count, -1)
        for one in (grad_router_weight, grad_gain_second, grad_gains[0], grad_gains[1])
    ]
    early = scatter_small(jnp.concatenate(by_device, axis=1))
    late = scatter_small(grad_gain_first.reshape(device_count, -1))
    router_grad = early[:router_size].reshape(router_rows, expert_count)
    rest = early[router_size:].reshape(3, router_rows)
    return (
        block_output,
        grad_input,
        head_grads[:, :column_span],
        head_grads[:, column_span : 2 * column_span],
        head_grads[:, 2 * column_span : 3 * column_span],
        out_grad.astype(WIDE),
        router_grad,
        late,
        rest[0],
        rest[1],
        rest[2],
        expert_grads[0],
        expert_grads[1],
        expert_grads[2],
    )


def solution(mesh):
    rows = P(("shard", "context", "tensor"), None)
    columns = P("shard", ("context", "tensor"))
    vector = P(("shard", "context", "tensor"))
    expert = P(("shard", "context"), None, "tensor")
    return jax.shard_map(
        local,
        mesh=mesh,
        in_specs=(
            (rows, rows)
            + (columns,) * 4
            + (rows,)
            + (vector,) * 4
            + (expert,) * 3
            + (rows,)
        ),
        out_specs=((rows, rows) + (columns,) * 4 + (rows,) + (vector,) * 4 + (expert,) * 3),
        check_vma=False,
    )
```

time: 1480 us -> 1040 us (0.70)
  waiting for transfers between devices: 731 us -> 347 us
  blocking collectives: 111 us -> 0 us
  Pallas kernels: 0 us -> 64.4 us
  starting transfers between devices: 83.5 us -> 116 us
  matrix products: 346 us -> 321 us
    ppermute x44 -> x8, waiting for transfers between devices: 272 us -> 0.02 us  [hop(): lax.ppermute(values, 'shard', tuple(((i, i ^ distance) for i in range(cou...]
    ppermute x26 -> x29, waiting for transfers between devices: 438 us -> 266 us  [swap(): return lax.ppermute(values, axis, SWAP)]
    all_gather x1 -> x0, blocking collectives: 111 us -> none  [local(): lax.all_gather(expert_ids, ('shard', 'context'), axis=0, tiled=False)]
    all_to_all x0 -> x11, waiting for transfers between devices: none -> 80.7 us  [the longest x3 43.1 us: deal(): lax.all_to_all(rows, DEVICES, split_axis=0, concat_axis=0, tiled=True)]
    pallas_call x0 -> x11, Pallas kernels: none -> 64.4 us  [the longest x4 29 us: attend_block_back(): pl.pallas_call(lambda *refs: attend_back_kernel(which, sums is None, *ref...]
    all_to_all x0 -> x11, starting transfers between devices: none -> 50 us  [the longest x8 40.4 us: over_chips(): lax.all_to_all(blocks, 'shard', split_axis=0, concat_axis=0, axis_index_g...]
    dot_general x34 -> x8, matrix products: 90.2 us -> 43.6 us  [the longest x4 25.5 us: combine(): jnp.einsum('bst,bsd->btd', pick, both, preferred_element_type=jnp.float32)]
    ppermute x44 -> x8, starting transfers between devices: 36.8 us -> 1.37 us  [hop(): lax.ppermute(values, 'shard', tuple(((i, i ^ distance) for i in range(cou...]
  transfers between devices with their start and end apart: 88 -> 52, of which waited for: 39 -> 25; matrix products, arithmetic and copies ran while one was open for 31% -> 42% of each run, Pallas kernels for 0% -> 6%
where the time goes in v2:
time: 1040 us; the launch traced here: 1030 us
  waiting for transfers between devices  347 us (33%)
  matrix products  321 us (31%)
  starting transfers between devices  116 us (11%)
  other arithmetic  84.8 us (8%)
  local copies, waits for them, and re-layouts  83.4 us (8%)
  Pallas kernels  64.4 us (6%)
  between operations  15.9 us (2%)
    ppermute x29, waiting for transfers between devices, swap(): return lax.ppermute(values, axis, SWAP)  266 us
    dot_general x15, matrix products, contract_last(): lax.dot_general(left, right, (((1,), (1,)), ((), ())), preferred_element_...  102 us
    dot_general x12, matrix products, contract_first(): lax.dot_general(left, right, (((0,), (0,)), ((), ())), preferred_element_...  89.5 us
    dot_general x23, matrix products, plain(): return jnp.dot(left, right, preferred_element_type=jnp.float32)  86.2 us
    ppermute x29, starting transfers between devices, swap(): return lax.ppermute(values, axis, SWAP)  60.6 us
    all_to_all x3, waiting for transfers between devices, deal(): lax.all_to_all(rows, DEVICES, split_axis=0, concat_axis=0, tiled=True)  43.1 us
    all_to_all x8, starting transfers between devices, over_chips(): lax.all_to_all(blocks, 'shard', split_axis=0, concat_axis=0, axis_index_g...  40.4 us
    all_to_all x8, waiting for transfers between devices, over_chips(): lax.all_to_all(blocks, 'shard', split_axis=0, concat_axis=0, axis_index_g...  37.6 us
  transfers between devices with their start and end apart: 52, of which 25 were waited for; matrix products, arithmetic and copies ran while one was open for 42% of the time, Pallas kernels for 6%

profile of v2, /device:TPU:0, one launch (start us, length us, event | category | flops | bytes accessed | tf_op | source)
XLA Modules:
  0.0 1031.8 jit_solution(11302055440080893128)
XLA Ops:
  29.4 31.7 %collective-permute-done.1 = bf16[256,2048]{1,0:T(8,128)(2,1)} collective-permute-done((bf16[256,2048]{1,0:T(8,128)(2,1)}, bf16[256,2048]{1,0:T(8,128)(2,1)}, u32[]{:S(2)}, u32[]{:S(2)}) %collective-permute-start.1) | collective-permute-done | bytes 1048608 | tf_op jit(solution)/shard_map/ppermute | solution.py:62
  69.0 16.8 %collective-permute-done.2 = bf16[256,2048]{1,0:T(8,128)(2,1)S(1)} collective-permute-done((bf16[256,2048]{1,0:T(8,128)(2,1)}, bf16[256,2048]{1,0:T(8,128)(2,1)S(1)}, u32[]{:S(2)}, u32[]{:S(2)}) %collective-permute-start.2) | collective-permute-done | bytes 1048608 | tf_op jit(solution)/shard_map/ppermute | solution.py:62
  153.4 14.1 %collective-permute-start.9 = (bf16[256,2048]{1,0:T(8,128)(2,1)S(1)}, bf16[256,2048]{1,0:T(8,128)(2,1)}, u32[]{:S(2)}, u32[]{:S(2)}) collective-permute-start(bf16[256,2048]{1,0:T(8,128)(2,1)S(1)} %copy-done.50), channel_id=1, source_target_pairs={{0,2},{2,0},{1,3},{3,1},{4,6},{6,4},{5,7},{7,5},{8,10},{10,8},{9,1... | collective-permute-start | bytes 3145736 | tf_op jit(solution)/shard_map/ppermute | solution.py:62
  180.5 15.1 %collective-permute-done.7 = bf16[256,2048]{1,0:T(8,128)(2,1)S(1)} collective-permute-done((bf16[256,2048]{1,0:T(8,128)(2,1)S(1)}, bf16[256,2048]{1,0:T(8,128)(2,1)S(1)}, u32[]{:S(2)}, u32[]{:S(2)}) %collective-permute-start.7) | collective-permute-done | bytes 1048608 | tf_op jit(solution)/shard_map/ppermute | solution.py:62
  210.2 7.7 collective-permute-start.8
  230.5 24.8 %collective-permute-done.10 = bf16[256,2048]{1,0:T(8,128)(2,1)} collective-permute-done((bf16[256,2048]{1,0:T(8,128)(2,1)}, bf16[256,2048]{1,0:T(8,128)(2,1)}, u32[]{:S(2)}, u32[]{:S(2)}) %collective-permute-start.10) | collective-permute-done | bytes 1048608 | tf_op jit(solution)/shard_map/ppermute | solution.py:62
  277.4 39.1 %collective-permute-done.11 = bf16[256,2048]{1,0:T(8,128)(2,1)} collective-permute-done((bf16[256,2048]{1,0:T(8,128)(2,1)}, bf16[256,2048]{1,0:T(8,128)(2,1)}, u32[]{:S(2)}, u32[]{:S(2)}) %collective-permute-start.11) | collective-permute-done | bytes 1048608 | tf_op jit(solution)/shard_map/ppermute | solution.py:62
  346.9 12.9 %collective-permute-done.14 = bf16[1024,512]{1,0:T(8,128)(2,1)} collective-permute-done((bf16[1024,512]{1,0:T(8,128)(2,1)}, bf16[1024,512]{1,0:T(8,128)(2,1)}, u32[]{:S(2)}, u32[]{:S(2)}) %collective-permute-start.14) | collective-permute-done | bytes 1048608 | tf_op jit(solution)/shard_map/ppermute | solution.py:62
  359.9 6.1 convolution_convert_fusion.5
  374.1 9.5 multiply_convert_fusion.5
  383.7 8.5 all-to-all-done.4
  420.9 12.7 %fusion.3 = (f32[1280]{0:T(1024)}, bf16[1280,2048]{1,0:T(8,128)(2,1)}, bf16[1280,2048]{1,0:T(8,128)(2,1)S(1)}) fusion(bf16[640,2048]{1,0:T(8,128)(2,1)} %collective-permute-done.15, bf16[640,2048]{1,0:T(8,128)(2,1)S(1)} %bitcast.164, f32[1280]{0:T(1024)S(1)} %get-tuple-element.276, bf16[1280,1024]{1,0:T(8,128)(2,1)} %get-tuple-element.147, ...), kind=kOutput, calls=%fused_computation.17 | convolution fusion | flops 5400165376 | bytes 22554624 | tf_op jit(solution)/shard_map/dot_general | solution.py:46
  440.8 7.9 fusion.76
  448.7 6.2 fusion.42
  459.7 10.4 %fusion.176 = f32[1280,1024]{1,0:T(8,128)} fusion(bf16[1280,2048]{1,0:T(8,128)(2,1)} %fusion.1, bf16[2048,1024]{1,0:T(8,128)(2,1)} %copy-done.75), kind=kOutput, calls=%fused_computation.349 | convolution fusion | flops 5368709120 | bytes 14680064 | tf_op jit(solution)/shard_map/dot_general | solution.py:58
  470.1 14.8 %multiply_convert_fusion.2 = (bf16[1280,1024]{1,0:T(8,128)(2,1)}, bf16[1280,1024]{1,0:T(8,128)(2,1)}, bf16[1280,1024]{1,0:T(8,128)(2,1)}) fusion(f32[1280,1024]{1,0:T(8,128)} %fusion.76, f32[1280,1024]{1,0:T(8,128)} %fusion.176, bf16[1024,512]{1,0:T(8,128)(2,1)} %collective-permute-done.14, bf16[1024,512]{1,0:T(8,128)(2,1)} %collective-permute-done.12, ...), kind=kOutput, calls=%fused_computation.60 | convolution fusion | flops 5411438592 | bytes 27787264 | tf_op jit(solution)/shard_map/dot_general | solution.py:58
  484.9 10.2 fusion.5
  498.4 10.3 fusion.154
  508.6 9.3 add_convert_fusion.1
  520.6 10.4 %fusion.45 = bf16[2048,512]{1,0:T(8,128)(2,1)} fusion(bf16[1280,2048]{1,0:T(8,128)(2,1)S(1)} %bitcast.152, bf16[1280,2048]{1,0:T(8,128)(2,1)} %get-tuple-element.152, bf16[1280,1024]{1,0:T(8,128)(2,1)} %get-tuple-element.147, bf16[1280,1024]{1,0:T(8,128)(2,1)} %get-tuple-element.291), kind=kOutput, calls=%fused_computation.95 | convolution fusion | flops 5395972096 | bytes 17825792 | tf_op jit(solution)/shard_map/dot_general | solution.py:52
  531.1 6.1 fusion.36
  537.2 6.1 fusion.39
  552.9 12.6 %multiply_convert_fusion.1 = (bf16[1280,1024]{1,0:T(8,128)(2,1)S(1)}, bf16[1280,1024]{1,0:T(8,128)(2,1)S(1)}) fusion(f32[1280,1024]{1,0:T(8,128)} %copy-done.103, f32[1280,1024]{1,0:T(8,128)} %get-tuple-element.345, bf16[1280,2048]{1,0:T(8,128)(2,1)} %get-tuple-element.152, bf16[2048,1024]{1,0:T(8,128)(2,1)} %copy-done.75), kind=kOutput, calls=%fused_computation.59 | convolution fusion | flops 5385748480 | bytes 25165824 | tf_op jit(solution)/shard_map/dot_general | solution.py:58
  565.5 11.5 %fusion.153 = f32[1280,2048]{1,0:T(8,128)} fusion(bf16[1280,1024]{1,0:T(8,128)(2,1)S(1)} %get-tuple-element.290, bf16[1024,512]{1,0:T(8,128)(2,1)} %collective-permute-done.14, bf16[1024,512]{1,0:T(8,128)(2,1)} %collective-permute-done.12, bf16[2048,512]{1,0:T(8,128)(2,1)S(1)} %bitcast.178), kind=kOutput, calls=%fused_computation.328 | convolution fusion | flops 5381292032 | bytes 17301504 | tf_op jit(solution)/shard_map/dot_general | solution.py:46
  577.0 8.4 add_convert_fusion
  608.6 7.1 fusion.33
  621.5 10.4 %convolution_convert_fusion.8 = bf16[2048,512]{1,0:T(8,128)(2,1)} fusion(bf16[1280,1024]{1,0:T(8,128)(2,1)} %copy-done.109, bf16[1280,1024]{1,0:T(8,128)(2,1)} %get-tuple-element.292, bf16[640,2048]{1,0:T(8,128)(2,1)} %collective-permute-done.16, bf16[640,2048]{1,0:T(8,128)(2,1)} %bitcast.157, bf16[1280,2048]{1,0:T(8,128)(2,1)} %copy-done.27), kind=kOutput, calls=%fused_computation.97 | convolution fusion | flops 5406457856 | bytes 17825792 | tf_op jit(solution)/shard_map/dot_general | solution.py:52
  634.7 9.0 convolution_convert_fusion.7
  643.7 25.3 %all-to-all-done.7 = bf16[4,256,2048]{2,1,0:T(8,128)(2,1)} async-done(((bf16[4,256,2048]{2,1,0:T(8,128)(2,1)}), bf16[4,256,2048]{2,1,0:T(8,128)(2,1)}, u32[]{:S(2)}, u32[]{:S(2)}) %all-to-all-start.7) | async-done | bytes 4194336 | tf_op jit(solution)/shard_map/all_to_all | solution.py:85
  672.2 17.4 %collective-permute-done.23 = bf16[256,2048]{1,0:T(8,128)(2,1)} collective-permute-done((bf16[256,2048]{1,0:T(8,128)(2,1)}, bf16[256,2048]{1,0:T(8,128)(2,1)}, u32[]{:S(2)}, u32[]{:S(2)}) %collective-permute-start.23) | collective-permute-done | bytes 1048608 | tf_op jit(solution)/shard_map/ppermute | solution.py:62
  710.2 10.1 add_bitcast_fusion.2
  722.2 6.3 shard_map.295
  728.6 25.3 %collective-permute-done.25 = bf16[256,2048]{1,0:T(8,128)(2,1)S(1)} collective-permute-done((bf16[256,2048]{1,0:T(8,128)(2,1)}, bf16[256,2048]{1,0:T(8,128)(2,1)S(1)}, u32[]{:S(2)}, u32[]{:S(2)}) %collective-permute-start.25) | collective-permute-done | bytes 1048608 | tf_op jit(solution)/shard_map/ppermute | solution.py:62
  754.9 7.5 shard_map.296
  779.9 7.5 shard_map.297
  787.4 24.8 %collective-permute-done.27 = bf16[256,2048]{1,0:T(8,128)(2,1)S(1)} collective-permute-done((bf16[256,2048]{1,0:T(8,128)(2,1)}, bf16[256,2048]{1,0:T(8,128)(2,1)S(1)}, u32[]{:S(2)}, u32[]{:S(2)}) %collective-permute-start.27) | collective-permute-done | bytes 1048608 | tf_op jit(solution)/shard_map/ppermute | solution.py:62
  818.9 7.6 shard_map.298
  826.6 6.3 shard_map.299
  851.3 7.1 add_convert_fusion.2
  859.8 6.7 shard_map.300
  866.4 6.3 convolution_convert_fusion.12
  874.7 8.7 convolution_convert_fusion
  883.3 6.0 fusion.85
  906.6 10.5 %add_bitcast_fusion.1 = f32[1,2048,512]{2,1,0:T(8,128)} fusion(bf16[1280,1024]{1,0:T(8,128)(2,1)S(1)} %copy-done.108, bf16[1280,1024]{1,0:T(8,128)(2,1)} %copy-done.109, bf16[1024,512]{1,0:T(8,128)(2,1)} %collective-permute-done.32, bf16[1024,512]{1,0:T(8,128)(2,1)S(1)} %copy-done.101, bf16[640,2048]{1,0:T(8,128)(2,1)} %collective-permute-done.16, ...), kind=kOutput, calls=%fused_computation.84 | convolution fusion | flops 5410652160 | bytes 22020096 | tf_op jit(solution)/shard_map/dot_general | solution.py:52
  919.0 30.0 %collective-permute-done.35 = bf16[256,2048]{1,0:T(8,128)(2,1)S(1)} collective-permute-done((bf16[256,2048]{1,0:T(8,128)(2,1)S(1)}, bf16[256,2048]{1,0:T(8,128)(2,1)S(1)}, u32[]{:S(2)}, u32[]{:S(2)}) %collective-permute-start.35) | collective-permute-done | bytes 1048608 | tf_op jit(solution)/shard_map/ppermute | solution.py:62
  950.0 7.8 fusion.73
  964.8 34.3 %all-to-all-done.11 = f32[32,1,64]{2,1,0:T(1,128)S(1)} async-done(((f32[32,1,64]{2,1,0:T(1,128)}), f32[32,1,64]{2,1,0:T(1,128)S(1)}, u32[]{:S(2)}, u32[]{:S(2)}) %all-to-all-start.11) | async-done | bytes 8224 | tf_op jit(solution)/shard_map/all_to_all | solution.py:99
  1012.0 10.7 %add_bitcast_fusion = f32[1,2048,512]{2,1,0:T(8,128)} fusion(bf16[2048,512]{1,0:T(8,128)(2,1)} %collective-permute-done.36, bf16[1280,1024]{1,0:T(8,128)(2,1)} %get-tuple-element.293, bf16[1280,1024]{1,0:T(8,128)(2,1)} %copy-done.106, bf16[640,2048]{1,0:T(8,128)(2,1)} %collective-permute-done.16, bf16[640,2048]{1,0:T(8,128)(2,1)} %bitcast.158, ...), kind=kOutput, calls=%fused_computation.83 | convolution fusion | flops 5407506432 | bytes 22020096 | tf_op jit(solution)/shard_map/dot_general | solution.py:52
  (526 shorter events, 400.1 us)
Async XLA Ops:
  7.2 84.5 %all-gather.2.cloned.1.call-start = ((), (), s32[]{:S(2)}) async-start(), calls=%async_computation.14 | async-start | bytes 9437184 | tf_op jit(solution)/shard_map/all_gather | solution.py:647
  9.7 51.4 %collective-permute-start.1 = (bf16[256,2048]{1,0:T(8,128)(2,1)}, bf16[256,2048]{1,0:T(8,128)(2,1)}, u32[]{:S(2)}, u32[]{:S(2)}) collective-permute-start(bf16[256,2048]{1,0:T(8,128)(2,1)} %param.21), channel_id=1, source_target_pairs={{0,2},{2,0},{1,3},{3,1},{4,6},{6,4},{5,7},{7,5},{8,10},{10,8},{9,1... | collective-permute-start | bytes 3145736 | tf_op jit(solution)/shard_map/ppermute | solution.py:62
  13.8 53.7 %collective-permute-start = (bf16[256,2048]{1,0:T(8,128)(2,1)}, bf16[256,2048]{1,0:T(8,128)(2,1)}, u32[]{:S(2)}, u32[]{:S(2)}) collective-permute-start(bf16[256,2048]{1,0:T(8,128)(2,1)} %param.21), channel_id=1, source_target_pairs={{0,1},{1,0},{2,3},{3,2},{4,5},{5,4},{6,7},{7,6},{8,9},{9,8},{10,11... | collective-permute-start | bytes 3145736 | tf_op jit(solution)/shard_map/ppermute | solution.py:62
  24.9 40.8 %all-to-all-start = ((bf16[32,2,1664]{2,1,0:T(2,128)(2,1)}), bf16[32,2,1664]{2,1,0:T(2,128)(2,1)S(1)}, u32[]{:S(2)}, u32[]{:S(2)}) async-start(bf16[32,2,1664]{2,1,0:T(2,128)(2,1)} %reshape.404), calls=%async_computation | async-start | bytes 425984 | tf_op jit(solution)/shard_map/all_to_all | solution.py:99
  61.1 24.8 %collective-permute-start.2 = (bf16[256,2048]{1,0:T(8,128)(2,1)}, bf16[256,2048]{1,0:T(8,128)(2,1)S(1)}, u32[]{:S(2)}, u32[]{:S(2)}) collective-permute-start(bf16[256,2048]{1,0:T(8,128)(2,1)} %collective-permute-done.1), channel_id=1, source_target_pairs={{0,1},{1,0},{2,3},{3,2},{4,5},{5,4},{6,7},{7,6},{8,9},{9,8},{10,11... | collective-permute-start | bytes 3145736 | tf_op jit(solution)/shard_map/ppermute | solution.py:62
  85.8 24.1 %collective-permute-start.3 = (bf16[1024,512]{1,0:T(8,128)(2,1)}, bf16[1024,512]{1,0:T(8,128)(2,1)}, u32[]{:S(2)}, u32[]{:S(2)}) collective-permute-start(bf16[1024,512]{1,0:T(8,128)(2,1)} %get-tuple-element.112), channel_id=1, source_target_pairs={{0,1},{1,0},{2,3},{3,2},{4,5},{5,4},{6,7},{7,6},{8,9},{9,8},{10,11... | collective-permute-start | bytes 3145736 | tf_op jit(solution)/shard_map/ppermute | solution.py:62
  112.5 85.7 %all-to-all-start.1 = ((bf16[4,256,2048]{2,1,0:T(8,128)(2,1)}), bf16[4,256,2048]{2,1,0:T(8,128)(2,1)}, u32[]{:S(2)}, u32[]{:S(2)}) async-start(bf16[4,256,2048]{2,1,0:T(8,128)(2,1)} %broadcast_in_dim.62), calls=%async_computation.1 | async-start | bytes 8388608 | tf_op jit(solution)/shard_map/all_to_all | solution.py:85
  128.1 23.6 %collective-permute-start.6 = (bf16[1024,512]{1,0:T(8,128)(2,1)}, bf16[1024,512]{1,0:T(8,128)(2,1)}, u32[]{:S(2)}, u32[]{:S(2)}) collective-permute-start(bf16[1024,512]{1,0:T(8,128)(2,1)} %get-tuple-element.120), channel_id=1, source_target_pairs={{0,1},{1,0},{2,3},{3,2},{4,5},{5,4},{6,7},{7,6},{8,9},{9,8},{10,11... | collective-permute-start | bytes 3145736 | tf_op jit(solution)/shard_map/ppermute | solution.py:62
  151.7 43.8 %collective-permute-start.7 = (bf16[256,2048]{1,0:T(8,128)(2,1)S(1)}, bf16[256,2048]{1,0:T(8,128)(2,1)S(1)}, u32[]{:S(2)}, u32[]{:S(2)}) collective-permute-start(bf16[256,2048]{1,0:T(8,128)(2,1)S(1)} %convolution_convert_fusion.10), channel_id=1, source_target_pairs={{0,1},{1,0},{2,3},{3,2},{4,5},{5,4},{6,7},{7,6},{8,9},{9,8},{10,11... | collective-permute-start | bytes 3145736 | tf_op jit(solution)/shard_map/ppermute | solution.py:62
  153.4 44.8 %collective-permute-start.9 = (bf16[256,2048]{1,0:T(8,128)(2,1)S(1)}, bf16[256,2048]{1,0:T(8,128)(2,1)}, u32[]{:S(2)}, u32[]{:S(2)}) collective-permute-start(bf16[256,2048]{1,0:T(8,128)(2,1)S(1)} %copy-done.50), channel_id=1, source_target_pairs={{0,2},{2,0},{1,3},{3,1},{4,6},{6,4},{5,7},{7,5},{8,10},{10,8},{9,1... | collective-permute-start | bytes 3145736 | tf_op jit(solution)/shard_map/ppermute | solution.py:62
  202.0 53.4 %all-to-all-start.2 = ((bf16[4,256,2048]{2,1,0:T(8,128)(2,1)}), bf16[4,256,2048]{2,1,0:T(8,128)(2,1)}, u32[]{:S(2)}, u32[]{:S(2)}) async-start(bf16[4,256,2048]{2,1,0:T(8,128)(2,1)} %broadcast_in_dim.63), calls=%async_computation.2 | async-start | bytes 8388608 | tf_op jit(solution)/shard_map/all_to_all | solution.py:85
  210.1 45.2 %collective-permute-start.10 = (bf16[256,2048]{1,0:T(8,128)(2,1)}, bf16[256,2048]{1,0:T(8,128)(2,1)}, u32[]{:S(2)}, u32[]{:S(2)}) collective-permute-start(bf16[256,2048]{1,0:T(8,128)(2,1)} %add_convert_fusion.5), channel_id=1, source_target_pairs={{0,2},{2,0},{1,3},{3,1},{4,6},{6,4},{5,7},{7,5},{8,10},{10,8},{9,1... | collective-permute-start | bytes 3145736 | tf_op jit(solution)/shard_map/ppermute | solution.py:62
  210.2 45.3 %collective-permute-start.8 = (bf16[256,2048]{1,0:T(8,128)(2,1)}, bf16[256,2048]{1,0:T(8,128)(2,1)}, u32[]{:S(2)}, u32[]{:S(2)}) collective-permute-start(bf16[256,2048]{1,0:T(8,128)(2,1)} %convolution_convert_fusion.9), channel_id=1, source_target_pairs={{0,1},{1,0},{2,3},{3,2},{4,5},{5,4},{6,7},{7,6},{8,9},{9,8},{10,11... | collective-permute-start | bytes 3145736 | tf_op jit(solution)/shard_map/ppermute | solution.py:62
  265.4 56.2 %all-to-all-start.3 = ((bf16[4,256,2048]{2,1,0:T(8,128)(2,1)}), bf16[4,256,2048]{2,1,0:T(8,128)(2,1)}, u32[]{:S(2)}, u32[]{:S(2)}) async-start(bf16[4,256,2048]{2,1,0:T(8,128)(2,1)} %broadcast_in_dim.66), calls=%async_computation.3 | async-start | bytes 8388608 | tf_op jit(solution)/shard_map/all_to_all | solution.py:85
  270.9 45.5 %collective-permute-start.11 = (bf16[256,2048]{1,0:T(8,128)(2,1)}, bf16[256,2048]{1,0:T(8,128)(2,1)}, u32[]{:S(2)}, u32[]{:S(2)}) collective-permute-start(bf16[256,2048]{1,0:T(8,128)(2,1)} %copy-done.32), channel_id=1, source_target_pairs={{0,2},{2,0},{1,3},{3,1},{4,6},{6,4},{5,7},{7,5},{8,10},{10,8},{9,1... | collective-permute-start | bytes 3145736 | tf_op jit(solution)/shard_map/ppermute | solution.py:62
  274.3 47.2 %collective-permute-start.12 = (bf16[1024,512]{1,0:T(8,128)(2,1)}, bf16[1024,512]{1,0:T(8,128)(2,1)}, u32[]{:S(2)}, u32[]{:S(2)}) collective-permute-start(bf16[1024,512]{1,0:T(8,128)(2,1)} %get-tuple-element.318), channel_id=1, source_target_pairs={{0,1},{1,0},{2,3},{3,2},{4,5},{5,4},{6,7},{7,6},{8,9},{9,8},{10,11... | collective-permute-start | bytes 3145736 | tf_op jit(solution)/shard_map/ppermute | solution.py:62
  328.5 15.3 %collective-permute-start.13 = (bf16[640,2048]{1,0:T(8,128)(2,1)}, bf16[640,2048]{1,0:T(8,128)(2,1)}, u32[]{:S(2)}, u32[]{:S(2)}) collective-permute-start(bf16[640,2048]{1,0:T(8,128)(2,1)} %bitcast.19), channel_id=1, source_target_pairs={{0,4},{4,0},{8,12},{12,8},{16,20},{20,16},{24,28},{28,24},{1,5},{5... | collective-permute-start | bytes 7864328 | tf_op jit(solution)/shard_map/ppermute | solution.py:67
  334.0 25.9 %collective-permute-start.14 = (bf16[1024,512]{1,0:T(8,128)(2,1)}, bf16[1024,512]{1,0:T(8,128)(2,1)}, u32[]{:S(2)}, u32[]{:S(2)}) collective-permute-start(bf16[1024,512]{1,0:T(8,128)(2,1)} %get-tuple-element.136), channel_id=1, source_target_pairs={{0,1},{1,0},{2,3},{3,2},{4,5},{5,4},{6,7},{7,6},{8,9},{9,8},{10,11... | collective-permute-start | bytes 3145736 | tf_op jit(solution)/shard_map/ppermute | solution.py:62
  338.7 53.4 %all-to-all-start.4 = ((bf16[4,256,2048]{2,1,0:T(8,128)(2,1)}), bf16[4,256,2048]{2,1,0:T(8,128)(2,1)}, u32[]{:S(2)}, u32[]{:S(2)}) async-start(bf16[4,256,2048]{2,1,0:T(8,128)(2,1)} %broadcast_in_dim.68), calls=%async_computation.4 | async-start | bytes 8388608 | tf_op jit(solution)/shard_map/all_to_all | solution.py:85
  365.9 47.6 %collective-permute-start.18 = (bf16[2048,512]{1,0:T(8,128)(2,1)}, bf16[2048,512]{1,0:T(8,128)(2,1)}, u32[]{:S(2)}, u32[]{:S(2)}) collective-permute-start(bf16[2048,512]{1,0:T(8,128)(2,1)} %bitcast.17), channel_id=1, source_target_pairs={{0,1},{1,0},{2,3},{3,2},{4,5},{5,4},{6,7},{7,6},{8,9},{9,8},{10,11... | collective-permute-start | bytes 6291464 | tf_op jit(solution)/shard_map/ppermute | solution.py:62
  396.8 18.6 %collective-permute-start.16 = (bf16[640,2048]{1,0:T(8,128)(2,1)S(1)}, bf16[640,2048]{1,0:T(8,128)(2,1)}, u32[]{:S(2)}, u32[]{:S(2)}) collective-permute-start(bf16[640,2048]{1,0:T(8,128)(2,1)S(1)} %bitcast.166), channel_id=1, source_target_pairs={{0,4},{4,0},{8,12},{12,8},{16,20},{20,16},{24,28},{28,24},{1,5},{5... | collective-permute-start | bytes 7864328 | tf_op jit(solution)/shard_map/ppermute | solution.py:67
  400.3 20.6 %collective-permute-start.15 = (bf16[640,2048]{1,0:T(8,128)(2,1)S(1)}, bf16[640,2048]{1,0:T(8,128)(2,1)}, u32[]{:S(2)}, u32[]{:S(2)}) collective-permute-start(bf16[640,2048]{1,0:T(8,128)(2,1)S(1)} %bitcast.165), channel_id=1, source_target_pairs={{0,4},{4,0},{8,12},{12,8},{16,20},{20,16},{24,28},{28,24},{1,5},{5... | collective-permute-start | bytes 7864328 | tf_op jit(solution)/shard_map/ppermute | solution.py:67
  405.2 30.5 %collective-permute-start.17 = (bf16[640,2048]{1,0:T(8,128)(2,1)S(1)}, bf16[640,2048]{1,0:T(8,128)(2,1)}, u32[]{:S(2)}, u32[]{:S(2)}) collective-permute-start(bf16[640,2048]{1,0:T(8,128)(2,1)S(1)} %bitcast.163), channel_id=1, source_target_pairs={{0,4},{4,0},{8,12},{12,8},{16,20},{20,16},{24,28},{28,24},{1,5},{5... | collective-permute-start | bytes 7864328 | tf_op jit(solution)/shard_map/ppermute | solution.py:67
  435.7 13.0 %collective-permute-start.19 = (bf16[640,2048]{1,0:T(8,128)(2,1)}, bf16[640,2048]{1,0:T(8,128)(2,1)}, u32[]{:S(2)}, u32[]{:S(2)}) collective-permute-start(bf16[640,2048]{1,0:T(8,128)(2,1)} %get-tuple-element.306), channel_id=1, source_target_pairs={{0,4},{4,0},{8,12},{12,8},{16,20},{20,16},{24,28},{28,24},{1,5},{5... | collective-permute-start | bytes 7864328 | tf_op jit(solution)/shard_map/ppermute | solution.py:67
  454.9 88.5 %all-to-all-start.5 = ((bf16[4,256,2048]{2,1,0:T(8,128)(2,1)}), bf16[4,256,2048]{2,1,0:T(8,128)(2,1)}, u32[]{:S(2)}, u32[]{:S(2)}) async-start(bf16[4,256,2048]{2,1,0:T(8,128)(2,1)} %fusion.42), calls=%async_computation.5 | async-start | bytes 8388608 | tf_op jit(solution)/shard_map/all_to_all | solution.py:85
  497.0 34.1 %collective-permute-start.21 = (bf16[640,2048]{1,0:T(8,128)(2,1)}, bf16[640,2048]{1,0:T(8,128)(2,1)}, u32[]{:S(2)}, u32[]{:S(2)}) collective-permute-start(bf16[640,2048]{1,0:T(8,128)(2,1)} %get-tuple-element.302), channel_id=1, source_target_pairs={{0,4},{4,0},{8,12},{12,8},{16,20},{20,16},{24,28},{28,24},{1,5},{5... | collective-permute-start | bytes 7864328 | tf_op jit(solution)/shard_map/ppermute | solution.py:67
  520.1 17.1 %collective-permute-start.20 = (bf16[640,2048]{1,0:T(8,128)(2,1)}, bf16[640,2048]{1,0:T(8,128)(2,1)}, u32[]{:S(2)}, u32[]{:S(2)}) collective-permute-start(bf16[640,2048]{1,0:T(8,128)(2,1)} %get-tuple-element.304), channel_id=1, source_target_pairs={{0,4},{4,0},{8,12},{12,8},{16,20},{20,16},{24,28},{28,24},{1,5},{5... | collective-permute-start | bytes 7864328 | tf_op jit(solution)/shard_map/ppermute | solution.py:67
  547.8 53.1 %all-to-all-start.6 = ((bf16[4,256,2048]{2,1,0:T(8,128)(2,1)}), bf16[4,256,2048]{2,1,0:T(8,128)(2,1)}, u32[]{:S(2)}, u32[]{:S(2)}) async-start(bf16[4,256,2048]{2,1,0:T(8,128)(2,1)} %fusion.39), calls=%async_computation.6 | async-start | bytes 8388608 | tf_op jit(solution)/shard_map/all_to_all | solution.py:85
  588.3 20.3 %collective-permute-start.22 = (bf16[640,2048]{1,0:T(8,128)(2,1)}, bf16[640,2048]{1,0:T(8,128)(2,1)}, u32[]{:S(2)}, u32[]{:S(2)}) collective-permute-start(bf16[640,2048]{1,0:T(8,128)(2,1)} %get-tuple-element.300), channel_id=1, source_target_pairs={{0,4},{4,0},{8,12},{12,8},{16,20},{20,16},{24,28},{28,24},{1,5},{5... | collective-permute-start | bytes 7864328 | tf_op jit(solution)/shard_map/ppermute | solution.py:67
  600.9 14.9 %all-to-all-start.8 = ((f32[16,1,256]{2,1,0:T(1,128)}), f32[16,1,256]{2,1,0:T(1,128)S(1)}, u32[]{:S(2)}, u32[]{:S(2)}) async-start(f32[16,1,256]{2,1,0:T(1,128)} %all_to_all.59), calls=%async_computation.8 | async-start | bytes 32768 | tf_op jit(solution)/shard_map/all_to_all | solution.py:551
  615.8 53.2 %all-to-all-start.7 = ((bf16[4,256,2048]{2,1,0:T(8,128)(2,1)}), bf16[4,256,2048]{2,1,0:T(8,128)(2,1)}, u32[]{:S(2)}, u32[]{:S(2)}) async-start(bf16[4,256,2048]{2,1,0:T(8,128)(2,1)} %fusion.33), calls=%async_computation.7 | async-start | bytes 8388608 | tf_op jit(solution)/shard_map/all_to_all | solution.py:85
  620.9 71.6 %collective-permute-start.24 = (bf16[2048,512]{1,0:T(8,128)(2,1)}, bf16[2048,512]{1,0:T(8,128)(2,1)}, u32[]{:S(2)}, u32[]{:S(2)}) collective-permute-start(bf16[2048,512]{1,0:T(8,128)(2,1)} %fusion.45), channel_id=1, source_target_pairs={{0,1},{1,0},{2,3},{3,2},{4,5},{5,4},{6,7},{7,6},{8,9},{9,8},{10,11... | collective-permute-start | bytes 6291464 | tf_op jit(solution)/shard_map/ppermute | solution.py:62
  632.0 57.7 %collective-permute-start.23 = (bf16[256,2048]{1,0:T(8,128)(2,1)}, bf16[256,2048]{1,0:T(8,128)(2,1)}, u32[]{:S(2)}, u32[]{:S(2)}) collective-permute-start(bf16[256,2048]{1,0:T(8,128)(2,1)} %reduce_sum.265), channel_id=1, source_target_pairs={{0,2},{2,0},{1,3},{3,1},{4,6},{6,4},{5,7},{7,5},{8,10},{10,8},{9,1... | collective-permute-start | bytes 3145736 | tf_op jit(solution)/shard_map/ppermute | solution.py:62
  692.6 71.2 %all-to-all-start.9 = ((bf16[4,256,2048]{2,1,0:T(8,128)(2,1)}), bf16[4,256,2048]{2,1,0:T(8,128)(2,1)}, u32[]{:S(2)}, u32[]{:S(2)}) async-start(bf16[4,256,2048]{2,1,0:T(8,128)(2,1)} %fusion.36), calls=%async_computation.9 | async-start | bytes 8388608 | tf_op jit(solution)/shard_map/all_to_all | solution.py:85
  697.6 219.6 %reduce-scatter.5.cloned.1.call-start = ((), (), s32[]{:S(2)}) async-start(), calls=%async_computation.16 | async-start | bytes 2359296 | tf_op jit(solution)/shard_map/reduce_scatter | solution.py:802
  705.6 62.4 %collective-permute-start.26 = (bf16[256,2048]{1,0:T(8,128)(2,1)}, bf16[256,2048]{1,0:T(8,128)(2,1)}, u32[]{:S(2)}, u32[]{:S(2)}) collective-permute-start(bf16[256,2048]{1,0:T(8,128)(2,1)} %get-tuple-element.277), channel_id=1, source_target_pairs={{0,2},{2,0},{1,3},{3,1},{4,6},{6,4},{5,7},{7,5},{8,10},{10,8},{9,1... | collective-permute-start | bytes 3145736 | tf_op jit(solution)/shard_map/ppermute | solution.py:62
  709.0 44.9 %collective-permute-start.25 = (bf16[256,2048]{1,0:T(8,128)(2,1)}, bf16[256,2048]{1,0:T(8,128)(2,1)S(1)}, u32[]{:S(2)}, u32[]{:S(2)}) collective-permute-start(bf16[256,2048]{1,0:T(8,128)(2,1)} %get-tuple-element.277), channel_id=1, source_target_pairs={{0,1},{1,0},{2,3},{3,2},{4,5},{5,4},{6,7},{7,6},{8,9},{9,8},{10,11... | collective-permute-start | bytes 3145736 | tf_op jit(solution)/shard_map/ppermute | solution.py:62
  768.0 44.2 %collective-permute-start.27 = (bf16[256,2048]{1,0:T(8,128)(2,1)}, bf16[256,2048]{1,0:T(8,128)(2,1)S(1)}, u32[]{:S(2)}, u32[]{:S(2)}) collective-permute-start(bf16[256,2048]{1,0:T(8,128)(2,1)} %collective-permute-done.26), channel_id=1, source_target_pairs={{0,1},{1,0},{2,3},{3,2},{4,5},{5,4},{6,7},{7,6},{8,9},{9,8},{10,11... | collective-permute-start | bytes 3145736 | tf_op jit(solution)/shard_map/ppermute | solution.py:62
  773.9 59.0 %collective-permute-start.28 = (bf16[256,2048]{1,0:T(8,128)(2,1)S(1)}, bf16[256,2048]{1,0:T(8,128)(2,1)S(1)}, u32[]{:S(2)}, u32[]{:S(2)}) collective-permute-start(bf16[256,2048]{1,0:T(8,128)(2,1)S(1)} %copy-done.77), channel_id=1, source_target_pairs={{0,2},{2,0},{1,3},{3,1},{4,6},{6,4},{5,7},{7,5},{8,10},{10,8},{9,1... | collective-permute-start | bytes 3145736 | tf_op jit(solution)/shard_map/ppermute | solution.py:62
  812.1 26.0 %collective-permute-start.29 = (bf16[1024,512]{1,0:T(8,128)(2,1)S(1)}, bf16[1024,512]{1,0:T(8,128)(2,1)S(1)}, u32[]{:S(2)}, u32[]{:S(2)}) collective-permute-start(bf16[1024,512]{1,0:T(8,128)(2,1)S(1)} %get-tuple-element.185), channel_id=1, source_target_pairs={{0,1},{1,0},{2,3},{3,2},{4,5},{5,4},{6,7},{7,6},{8,9},{9,8},{10,11... | collective-permute-start | bytes 3145736 | tf_op jit(solution)/shard_map/ppermute | solution.py:62
  850.1 22.6 %collective-permute-start.32 = (bf16[1024,512]{1,0:T(8,128)(2,1)}, bf16[1024,512]{1,0:T(8,128)(2,1)}, u32[]{:S(2)}, u32[]{:S(2)}) collective-permute-start(bf16[1024,512]{1,0:T(8,128)(2,1)} %get-tuple-element.191), channel_id=1, source_target_pairs={{0,1},{1,0},{2,3},{3,2},{4,5},{5,4},{6,7},{7,6},{8,9},{9,8},{10,11... | collective-permute-start | bytes 3145736 | tf_op jit(solution)/shard_map/ppermute | solution.py:62
  858.5 164.3 %reduce-scatter.3.cloned.1.call-start = ((), (), s32[]{:S(2)}) async-start(), calls=%async_computation.15 | async-start | bytes 7077888 | tf_op jit(solution)/shard_map/reduce_scatter | solution.py:841
  872.7 22.2 %collective-permute-start.33 = (bf16[256,2048]{1,0:T(8,128)(2,1)}, bf16[256,2048]{1,0:T(8,128)(2,1)}, u32[]{:S(2)}, u32[]{:S(2)}) collective-permute-start(bf16[256,2048]{1,0:T(8,128)(2,1)} %convolution_convert_fusion.12), channel_id=1, source_target_pairs={{0,1},{1,0},{2,3},{3,2},{4,5},{5,4},{6,7},{7,6},{8,9},{9,8},{10,11... | collective-permute-start | bytes 3145736 | tf_op jit(solution)/shard_map/ppermute | solution.py:62
  905.5 43.4 %collective-permute-start.35 = (bf16[256,2048]{1,0:T(8,128)(2,1)S(1)}, bf16[256,2048]{1,0:T(8,128)(2,1)S(1)}, u32[]{:S(2)}, u32[]{:S(2)}) collective-permute-start(bf16[256,2048]{1,0:T(8,128)(2,1)S(1)} %add_convert_fusion.3), channel_id=1, source_target_pairs={{0,2},{2,0},{1,3},{3,1},{4,6},{6,4},{5,7},{7,5},{8,10},{10,8},{9,1... | collective-permute-start | bytes 3145736 | tf_op jit(solution)/shard_map/ppermute | solution.py:62
  905.6 43.4 %collective-permute-start.34 = (bf16[256,2048]{1,0:T(8,128)(2,1)}, bf16[256,2048]{1,0:T(8,128)(2,1)}, u32[]{:S(2)}, u32[]{:S(2)}) collective-permute-start(bf16[256,2048]{1,0:T(8,128)(2,1)} %convolution_convert_fusion.11), channel_id=1, source_target_pairs={{0,1},{1,0},{2,3},{3,2},{4,5},{5,4},{6,7},{7,6},{8,9},{9,8},{10,11... | collective-permute-start | bytes 3145736 | tf_op jit(solution)/shard_map/ppermute | solution.py:62
  950.0 62.0 %collective-permute-start.36 = (bf16[2048,512]{1,0:T(8,128)(2,1)}, bf16[2048,512]{1,0:T(8,128)(2,1)}, u32[]{:S(2)}, u32[]{:S(2)}) collective-permute-start(bf16[2048,512]{1,0:T(8,128)(2,1)} %convolution_convert_fusion.7), channel_id=1, source_target_pairs={{0,1},{1,0},{2,3},{3,2},{4,5},{5,4},{6,7},{7,6},{8,9},{9,8},{10,11... | collective-permute-start | bytes 6291464 | tf_op jit(solution)/shard_map/ppermute | solution.py:62
  958.5 40.5 %all-to-all-start.11 = ((f32[32,1,64]{2,1,0:T(1,128)}), f32[32,1,64]{2,1,0:T(1,128)S(1)}, u32[]{:S(2)}, u32[]{:S(2)}) async-start(f32[32,1,64]{2,1,0:T(1,128)} %all_to_all.65), calls=%async_computation.13 | async-start | bytes 32768 | tf_op jit(solution)/shard_map/all_to_all | solution.py:99
  999.0 11.5 %all-to-all-start.10 = ((f32[32,1,1216]{2,1,0:T(1,128)}), f32[32,1,1216]{2,1,0:T(1,128)S(1)}, u32[]{:S(2)}, u32[]{:S(2)}) async-start(f32[32,1,1216]{2,1,0:T(1,128)} %copy.67), calls=%async_computation.12 | async-start | bytes 327680 | tf_op jit(solution)/shard_map/all_to_all | solution.py:99
  (127 other events, 1525.1 us)
Sparse Core Ops, SparseCore 0:
  10.5 59.0 all-gather.1
  858.6 39.6 reduce-scatter.4
  902.0 61.7 reduce-scatter.2

commit v3 on v2

--- a/solution.py
+++ b/solution.py
@@ -382,13 +382,26 @@
     return (grad_route, grad_gate_act, grad_up_act)
 
 
+def weight_total(left, right):
+    return contract_first(left, right).astype(LOW)
+
+
+def columns_of(values, tensor):
+    half = values.shape[1] // 2
+    return lax.dynamic_slice_in_dim(values, tensor * half, half, 1)
+
+
 def their_grad(left, right):
-    return contract_first(left, right[:, right.shape[1] // 2 :]).astype(LOW)
+    return contract_first(left, columns_of(right, 1 - lax.axis_index("tensor"))).astype(LOW)
 
 
 def own_grad(left, right, arrived):
-    mine = contract_first(left, right[:, : right.shape[1] // 2])
-    return (mine + arrived.astype(WIDE))[None]
+    mine = contract_first(left, columns_of(right, lax.axis_index("tensor")))
+    return mine + arrived.astype(WIDE)
+
+
+def owned_grad(total):
+    return lax.psum_scatter(total, "tensor", scatter_dimension=1, tiled=True)
 
 
 def halves(values):
@@ -396,8 +409,8 @@
     return (values[:half], values[half:])
 
 
-def with_partner(held):
-    return jnp.concatenate([held, swap(held, "tensor")], axis=1)
+def whole_weight(held):
+    return lax.all_gather(held, "tensor", axis=1, tiled=True)
 
 
 def softmax_rows(logits):
@@ -444,7 +457,7 @@
 
 
 def experts_by_blocks(
-    low_second, cot_near, cot_far, all_ids, router, gate_weight, w_up, w_down, capacity
+    low_second, cot_near, cotangent, all_ids, router, gate_weight, w_up, w_down, capacity
 ):
     shard, context = lax.axis_index("shard"), lax.axis_index("context")
     contexts = lax.axis_size("context")
@@ -478,27 +491,21 @@
         gate_grad = jnp.sum(all_picks * slot_grad.reshape(2 * chips, capacity)[:, :, None], axis=1)
         return (gate_grad, (gate * cot_wide).astype(LOW), (gate * produced_wide).astype(LOW))
 
-    up_halves = halves(w_up)
-    near_chunk, across, up_first, up_late = sync(
-        gather_chips(low_second),
-        swap(low_second, "context"),
-        swap(up_halves[0], "tensor"),
-        up_halves[1],
-    )
+    up_weight = whole_weight(w_up)
+    near_chunk, across, w_down, cot_near, cotangent = sync(
+        gather_chips(low_second), swap(low_second, "context"), w_down, cot_near, cotangent
+    )
+    cot_across = swap(cotangent, "context")
     near_rows = pick_rows(*picks[0][:2], near_chunk)
-    near_rows, up_second, w_down, cot_near = sync(
-        near_rows, swap(up_late, "tensor"), w_down, cot_near
-    )
-    up_arrived = jnp.concatenate([up_first, up_second], axis=0)
-    weights = (
-        gate_weight,
-        jnp.concatenate([w_up, up_arrived], axis=1),
-        with_partner(w_down),
-    )
+    down_weight = whole_weight(w_down)
+    weights = (gate_weight, up_weight, down_weight)
     near_kept = expert_hidden(near_rows, weights)
-    near_hidden, far_chunk = sync(near_kept[2], gather_chips(across))
+    near_hidden, far_chunk, cot_across = sync(near_kept[2], gather_chips(across), cot_across)
     near_kept = near_kept[:2] + (near_hidden,)
+    cot_far = gather_chips(cot_across)
     far_rows = pick_rows(*picks[1][:2], far_chunk)
+    far_rows, down_weight = sync(far_rows, down_weight)
+    weights = (gate_weight, up_weight, down_weight)
     far_kept = expert_hidden(far_rows, weights)
     near_cot, far_cot = pick_rows(*picks[0][:2], cot_near), pick_rows(*picks[1][:2], cot_far)
     gate = arrive(0, near_rows)
@@ -508,48 +515,51 @@
     gate = arrive(1, far_rows)
     produced = expert_produce(far_kept[2], weights)
     far_gate_grad, far_grad_rows, far_weighted = leave(1, produced, far_cot, gate)
-    gate_grads = [near_gate_grad, far_gate_grad]
     rest_parts = chip_parts(far_weighted, *picks[1][:2])
-    far_grad_rows, mixture_parts = sync(far_grad_rows, mixture_parts)
-    mixture = sum_chips(mixture_parts)
-
-    def both(near, far):
-        return jnp.concatenate([near, far], axis=0)
-
-    far_route, far_gate_act, far_up_act = expert_backward(far_grad_rows, far_kept, weights)
-    down_pair = (both(near_grad_rows, far_grad_rows), both(near_kept[2], far_kept[2]))
-    down_theirs = their_grad(*down_pair)
-    far_parts = chip_parts(far_route.astype(LOW), *picks[1][:2])
-    near_grad_rows, far_parts, down_theirs, mixture, rest_parts = sync(
-        near_grad_rows, far_parts, down_theirs, mixture, rest_parts
-    )
-    near_route, near_gate_act, near_up_act = expert_backward(near_grad_rows, near_kept, weights)
-    near_route = near_route.astype(LOW)
-    near_half = near_route.shape[0] // 2
-    near_swapped, far_grad = sync(
-        hop(near_route[near_half:], 1), sum_chips(far_parts).astype(LOW)
-    )
-    near_parts = combine(near_route[:near_half], near_swapped, *picks[0][:2])
-    all_rows = both(near_rows, far_rows)
-    gate_pair = (all_rows, both(near_gate_act, far_gate_act))
-    up_pair = (all_rows, both(near_up_act, far_up_act))
-    gate_theirs = their_grad(*gate_pair)
-    far_arrived = swap(far_grad, "context")
-    grad, rest_parts, gate_theirs, down_arrived = sync(
-        sum_chips(near_parts) + far_arrived.astype(WIDE),
-        rest_parts,
-        gate_theirs,
-        swap(down_theirs, "tensor"),
-    )
-    up_theirs = their_grad(*up_pair)
-    lines = jnp.stack(gate_grads, axis=1)
+    lines = jnp.stack([near_gate_grad, far_gate_grad], axis=1)
     lines = jnp.where(context == 0, lines, lines[:, ::-1])
     mine, far = lines[:chips], lines[chips:]
     low_core = (shard & 1) == 0
     lines = jnp.stack([jnp.where(low_core, mine, far), jnp.where(low_core, far, mine)], axis=1)
     lines = lines.reshape(-1, token_count)
     by_expert = lax.all_to_all(lines, ("shard", "context"), split_axis=0, concat_axis=0, tiled=True)
-    later = (mixture, rest_parts, gate_theirs, up_theirs, gate_pair, up_pair, down_pair, down_arrived)
+
+    def both(near, far):
+        return jnp.concatenate([near, far], axis=0)
+
+    far_route, far_gate_act, far_up_act = expert_backward(far_grad_rows, far_kept, weights)
+    far_route, near_grad_rows, far_grad_rows = sync(far_route, near_grad_rows, far_grad_rows)
+    down_pair = (both(near_grad_rows, far_grad_rows), both(near_kept[2], far_kept[2]))
+    down_total = weight_total(*down_pair)
+    far_parts = chip_parts(far_route.astype(LOW), *picks[1][:2])
+    near_grad_rows, far_parts, by_expert, down_total = sync(
+        near_grad_rows, far_parts, by_expert, down_total
+    )
+    down_grad = owned_grad(down_total)
+    near_route, near_gate_act, near_up_act = expert_backward(near_grad_rows, near_kept, weights)
+    near_route = near_route.astype(LOW)
+    near_half = near_route.shape[0] // 2
+    near_swapped = hop(near_route[near_half:], 1)
+    near_route, near_gate_act = sync(near_route, near_gate_act)
+    all_rows = both(near_rows, far_rows)
+    near_swapped, far_grad, near_up_act, gate_total = sync(
+        near_swapped,
+        sum_chips(far_parts).astype(LOW),
+        near_up_act,
+        weight_total(all_rows, both(near_gate_act, far_gate_act)),
+    )
+    gate_grad = owned_grad(gate_total)
+    near_parts = combine(near_route[:near_half], near_swapped, *picks[0][:2])
+    up_pair = (all_rows, both(near_up_act, far_up_act))
+    far_arrived = swap(far_grad, "context")
+    grad, mixture_parts, rest_parts, up_theirs, down_grad = sync(
+        sum_chips(near_parts) + far_arrived.astype(WIDE),
+        mixture_parts,
+        rest_parts,
+        their_grad(*up_pair),
+        down_grad,
+    )
+    later = (mixture_parts, rest_parts, gate_grad, down_grad, up_theirs, up_pair)
     return (grad, by_expert.T, later)
 
 
@@ -598,7 +608,7 @@
     )
     by_expert = jnp.sum(jnp.where(choose, grad_gates[:, :, None], 0.0), axis=1)
     pairs = [(rows, grad_gate_act), (rows, grad_up_act), (grad_rows, kept[2])]
-    grads = tuple(own_grad(*pair, swap(their_grad(*pair), "tensor")) for pair in pairs)
+    grads = tuple(owned_grad(weight_total(*pair)) for pair in pairs)
     return (grad, by_expert, mixture, grads)
 
 
@@ -643,7 +653,8 @@
         )
     )
     hidden_blocks = gather_group(hidden_in)
-    hidden_blocks[3], gate_early = sync(hidden_blocks[3], w_gate[0, : model_width // 2])
+    hidden_blocks[3], gate_early = sync(hidden_blocks[3], w_gate[0])
+    gate_weight = whole_weight(gate_early)
     packed = lax.all_gather(
         jnp.concatenate([w_query, w_key, w_value, w_out], axis=1), "shard", axis=0, tiled=True
     )
@@ -690,23 +701,18 @@
         stacked = stacked + swap(stacked, "context")[:, jnp.array([2, 3, 0, 1])]
         return stacked.reshape(2, -1)
 
-    half_rows = model_width // 2
-    gate_first = swap(gate_early, "tensor")
-    own_squares, gate_first, early_cot = sync(
+    own_squares, early_cot = sync(
         jnp.stack(
             [
                 jnp.sum(jnp.square(pre[:, i * column_span : (i + 1) * column_span]), axis=1)
                 for i in range(2)
             ]
         ),
-        gate_first,
         cotangent,
     )
     if by_blocks:
         cot_near = gather_chips(early_cot)
-        cot_across = swap(early_cot, "context")
-    squares, gate_late = sync(over_group(own_squares), w_gate[0, half_rows:])
-    gate_second = swap(gate_late, "tensor")
+    squares = over_group(own_squares)
     query_heads, key_heads, value_heads = prepare(
         pre, squares, gain_cols, cosine, sine, model_width, row_count
     )
@@ -717,18 +723,13 @@
             k, group, query_heads, key_heads, value_heads, row_count
         )
     parts = [contract_last(block, out_cols) for block in blocks]
-    far_part, gate_second = sync(parts[3].astype(LOW), gate_second)
-    gate_weight = jnp.concatenate(
-        [w_gate[0], jnp.concatenate([gate_first, gate_second], axis=0)], axis=1
-    )
+    far_part, gate_weight = sync(parts[3].astype(LOW), gate_weight)
     far = swap(far_part, "tensor")
     far, near_part, part = sync(far, parts[1].astype(LOW), parts[2])
-    if by_blocks:
-        far, cot_near, cot_across = sync(far, cot_near, cot_across)
     across = swap((part + far.astype(WIDE)).astype(LOW), "context")
     near = swap(near_part, "tensor")
     if by_blocks:
-        across, cot_far, gate_weight = sync(across, gather_chips(cot_across), gate_weight)
+        across, cot_near = sync(across, cot_near)
     middle = inputs + parts[0] + near.astype(WIDE) + across.astype(WIDE)
     normed_second, factor_second = rms_scale(middle, gain_second)
     low_second = normed_second.astype(LOW)
@@ -738,7 +739,7 @@
         grad_from_experts, grad_router_probs, later = experts_by_blocks(
             low_second,
             cot_near,
-            cot_far,
+            cotangent,
             all_ids,
             router_full,
             gate_weight,
@@ -746,9 +747,10 @@
             late_down,
             capacity,
         )
-        mixture, rest_parts, gate_theirs, up_theirs, gate_pair, up_pair, down_pair, arrived = later
+        mixture_parts, rest_parts, gate_grad, down_grad, up_theirs, up_pair = later
+        up_halves = halves(up_theirs)
     else:
-        weights = (gate_weight, with_partner(late_up), with_partner(late_down))
+        weights = (gate_weight, whole_weight(late_up), whole_weight(late_down))
         grad_from_experts, grad_router_probs, mixture, expert_grads = experts_by_slots(
             low_second, cotangent, expert_ids, router_probs, weights, capacity
         )
@@ -779,19 +781,17 @@
 
     own_query, own_sums = piece_back(0, grad_branch, None)
     if by_blocks:
-        down_grad = own_grad(*down_pair, arrived)
         rest = sum_chips(rest_parts).astype(LOW)
+    if by_blocks:
+        across, own_sums, rest, gate_grad = sync(across, tuple(own_sums), rest, gate_grad)
+        others = lax.all_gather(rest, "context", axis=0, tiled=False)
+    last = swap(across, "tensor")
     near_query, near_sums = piece_back(1, near_piece, own_sums)
-    if by_blocks:
-        across, near_sums, down_grad, rest, up_theirs = sync(
-            across, near_sums, down_grad, rest, up_theirs
-        )
-        rest_arrived = swap(rest, "context")
-    last = swap(across, "tensor")
     across_query, across_sums = piece_back(2, across, near_sums)
-    if by_blocks:
-        gate_halves = halves(gate_theirs)
-        last, across_sums, gate_early = sync(last, across_sums, gate_halves[0])
+    last, across_sums = sync(last, across_sums)
+    if by_blocks:
+        last, up_early, mixture_parts = sync(last, up_halves[0], mixture_parts)
+        mixture = sum_chips(mixture_parts)
     pieces = [grad_branch, near_piece, across, last]
     last_query, sums = piece_back(3, last, across_sums)
     grad_queries = [own_query, near_query, across_query, last_query]
@@ -799,7 +799,7 @@
     out_total = contract_first(pieces[0], blocks[0])
     for k in range(1, 4):
         out_total = out_total + contract_first(pieces[k], blocks[k])
-    out_grad = lax.psum_scatter(out_total.astype(LOW), "shard", scatter_dimension=0, tiled=True)
+    out_total = out_total.astype(LOW)
     totals, gain_grads = norm_call(
         norm_sums_kernel,
         (grad_query_heads, sums[0], pre, squares, gain_cols, cosine, sine),
@@ -809,14 +809,10 @@
         row_count,
     )
     if by_blocks:
-        totals, rest_arrived, gate_first, gate_late = sync(
-            totals, rest_arrived, swap(gate_early, "tensor"), gate_halves[1]
-        )
-        mixture = mixture + rest_arrived.astype(WIDE)
-    block_output = (middle + mixture).astype(LOW)
+        totals, up_first = sync(totals, swap(up_early, "tensor"))
     totals = over_group(totals)
     if by_blocks:
-        totals, gate_late = sync(totals, gate_late)
+        totals, up_late = sync(totals, up_halves[1])
     (grad_pre,) = norm_call(
         norm_grads_kernel,
         (grad_query_heads, *sums, pre, squares, totals, gain_cols, cosine, sine),
@@ -831,26 +827,16 @@
 
     far_part = contract_last(block_of(grad_pre, 3), qkv_cols).astype(LOW)
     if by_blocks:
-        far_part, grad_pre, gate_second = sync(far_part, grad_pre, swap(gate_late, "tensor"))
+        far_part, grad_pre, up_second, others, mixture, out_total = sync(
+            far_part, grad_pre, swap(up_late, "tensor"), others, mixture, out_total
+        )
+        other = lax.dynamic_index_in_dim(others, lax.axis_index("context") ^ 1, 0, False)
+        mixture = mixture + other.astype(WIDE)
+    block_output = (middle + mixture).astype(LOW)
+    out_dealt = lax.all_to_all(out_total, "shard", split_axis=0, concat_axis=0, tiled=True)
     far = swap(far_part, "tensor")
     head_total = contract_first(low_group, grad_pre).astype(LOW)
     parts = [contract_last(block_of(grad_pre, k), qkv_cols) for k in range(3)]
-    far, head_total, parts[1], parts[2] = sync(far, head_total, parts[1].astype(LOW), parts[2])
-    across = swap((parts[2] + far.astype(WIDE)).astype(LOW), "context")
-    near = swap(parts[1], "tensor")
-    head_grads = lax.psum_scatter(head_total, "shard", scatter_dimension=0, tiled=True).astype(WIDE)
-    if by_blocks:
-        near, across, gain_grads, up_theirs = sync(near, across, gain_grads, up_theirs)
-        up_arrived = swap(up_theirs, "tensor")
-        gate_arrived = jnp.concatenate([gate_first, gate_second], axis=0)
-        expert_grads = (
-            own_grad(*gate_pair, gate_arrived),
-            own_grad(*up_pair, up_arrived),
-            down_grad,
-        )
-    grad_first = parts[0] + near.astype(WIDE) + across.astype(WIDE)
-    grad_normed_first, grad_gain_first = rms_back(inputs, factor_first, gain_first, grad_first)
-    grad_input = grad_middle + grad_normed_first
     zero_gain = jnp.zeros((2, model_width), WIDE)
     grad_gains = lax.dynamic_update_slice(zero_gain, gain_grads, (0, group_index * column_span))
     by_device = [
@@ -858,6 +844,22 @@
         for one in (grad_router_weight, grad_gain_second, grad_gains[0], grad_gains[1])
     ]
     early = scatter_small(jnp.concatenate(by_device, axis=1))
+    far, head_total, near_part, early, out_dealt, *parts = sync(
+        far, head_total, parts[1].astype(LOW), early, out_dealt, parts[0], parts[2]
+    )
+    across = swap((parts[1] + far.astype(WIDE)).astype(LOW), "context")
+    near = swap(near_part, "tensor")
+    head_grads = lax.psum_scatter(head_total, "shard", scatter_dimension=0, tiled=True).astype(WIDE)
+    if by_blocks:
+        up_arrived = jnp.concatenate([up_first, up_second], axis=0)
+        near, gate_grad, down_grad, up_arrived = sync(near, gate_grad, down_grad, up_arrived)
+        expert_grads = (gate_grad, own_grad(*up_pair, up_arrived), down_grad)
+    out_grad = jnp.sum(
+        out_dealt.reshape((lax.axis_size("shard"),) + w_out.shape).astype(WIDE), axis=0
+    )
+    grad_first = parts[0] + near.astype(WIDE) + across.astype(WIDE)
+    grad_normed_first, grad_gain_first = rms_back(inputs, factor_first, gain_first, grad_first)
+    grad_input = grad_middle + grad_normed_first
     late = scatter_small(grad_gain_first.reshape(device_count, -1))
     router_grad = early[:router_size].reshape(router_rows, expert_count)
     rest = early[router_size:].reshape(3, router_rows)
@@ -867,15 +869,13 @@
         head_grads[:, :column_span],
         head_grads[:, column_span : 2 * column_span],
         head_grads[:, 2 * column_span : 3 * column_span],
-        out_grad.astype(WIDE),
+        out_grad,
         router_grad,
         late,
         rest[0],
         rest[1],
         rest[2],
-        expert_grads[0],
-        expert_grads[1],
-        expert_grads[2],
+        *(grad.astype(WIDE)[None] for grad in expert_grads),
     )
 
 

time: 1040 us -> 1010 us (0.971)
  starting transfers between devices: 116 us -> 83.3 us
  waiting for transfers between devices: 347 us -> 321 us
  blocking collectives: 0 us -> 13 us
    ppermute x29 -> x21, waiting for transfers between devices: 266 us -> 221 us  [swap(): return lax.ppermute(values, axis, SWAP)]
    all_to_all x3 -> x2, waiting for transfers between devices: 43.1 us -> 2.21 us  [deal(): lax.all_to_all(rows, DEVICES, split_axis=0, concat_axis=0, tiled=True)]
    ppermute x29 -> x21, starting transfers between devices: 60.6 us -> 25.5 us  [swap(): return lax.ppermute(values, axis, SWAP)]
    all_gather x0 -> x4, waiting for transfers between devices: none -> 30.5 us  [the longest x3 16 us: whole_weight(): return lax.all_gather(held, 'tensor', axis=1, tiled=True)]
    all_to_all x8, waiting for transfers between devices: 37.6 us -> 67.3 us  [over_chips(): lax.all_to_all(blocks, 'shard', split_axis=0, concat_axis=0, axis_index_g...]
    dot_general x23, matrix products: 86.2 us -> 102 us  [plain(): return jnp.dot(left, right, preferred_element_type=jnp.float32)]
    all_to_all x0 -> x1, blocking collectives: none -> 13 us  [deal(): lax.all_to_all(rows, DEVICES, split_axis=0, concat_axis=0, tiled=True)]
    dot_general x12 -> x10, matrix products: 89.5 us -> 83.1 us  [contract_first(): lax.dot_general(left, right, (((0,), (0,)), ((), ())), preferred_element_...]
  transfers between devices with their start and end apart: 52 -> 49, of which waited for: 25 -> 23; matrix products, arithmetic and copies ran while one was open for 42% -> 42% of each run, Pallas kernels for 6% -> 6%
where the time goes in v3:
time: 1010 us; the launch traced here: 1000 us
  matrix products  325 us (32%)
  waiting for transfers between devices  321 us (32%)
  other arithmetic  91.7 us (9%)
  local copies, waits for them, and re-layouts  88.2 us (9%)
  starting transfers between devices  83.3 us (8%)
  Pallas kernels  64 us (6%)
  between operations  16.1 us (2%)
  blocking collectives  13 us (1%)
    ppermute x21, waiting for transfers between devices, swap(): return lax.ppermute(values, axis, SWAP)  221 us
    dot_general x23, matrix products, plain(): return jnp.dot(left, right, preferred_element_type=jnp.float32)  102 us
    dot_general x15, matrix products, contract_last(): lax.dot_general(left, right, (((1,), (1,)), ((), ())), preferred_element_...  97.4 us
    dot_general x10, matrix products, contract_first(): lax.dot_general(left, right, (((0,), (0,)), ((), ())), preferred_element_...  83.1 us
    all_to_all x8, waiting for transfers between devices, over_chips(): lax.all_to_all(blocks, 'shard', split_axis=0, concat_axis=0, axis_index_g...  67.3 us
    all_to_all x8, starting transfers between devices, over_chips(): lax.all_to_all(blocks, 'shard', split_axis=0, concat_axis=0, axis_index_g...  40.1 us
    pallas_call x4, Pallas kernels, attend_block_back(): pl.pallas_call(lambda *refs: attend_back_kernel(which, sums is None, *ref...  29.1 us
    dot_general x4, matrix products, combine(): jnp.einsum('bst,bsd->btd', pick, both, preferred_element_type=jnp.float32)  26.8 us
  transfers between devices with their start and end apart: 49, of which 23 were waited for; matrix products, arithmetic and copies ran while one was open for 42% of the time, Pallas kernels for 6%

profile of v3, /device:TPU:0, one launch (start us, length us, event | category | flops | bytes accessed | tf_op | source)
XLA Modules:
  0.0 1002.3 jit_solution(9679541090282186296)
XLA Ops:
  32.2 31.8 %collective-permute-done.1 = bf16[256,2048]{1,0:T(8,128)(2,1)S(1)} collective-permute-done((bf16[256,2048]{1,0:T(8,128)(2,1)}, bf16[256,2048]{1,0:T(8,128)(2,1)S(1)}, u32[]{:S(2)}, u32[]{:S(2)}) %collective-permute-start.1) | collective-permute-done | bytes 1048608 | tf_op jit(solution)/shard_map/ppermute | solution.py:62
  69.1 16.9 %collective-permute-done.2 = bf16[256,2048]{1,0:T(8,128)(2,1)} collective-permute-done((bf16[256,2048]{1,0:T(8,128)(2,1)S(1)}, bf16[256,2048]{1,0:T(8,128)(2,1)}, u32[]{:S(2)}, u32[]{:S(2)}) %collective-permute-start.2) | collective-permute-done | bytes 1048608 | tf_op jit(solution)/shard_map/ppermute | solution.py:62
  136.9 7.9 all-gather.9.cloned.1.call-done
  159.8 10.1 %collective-permute-done.5 = bf16[256,2048]{1,0:T(8,128)(2,1)S(1)} collective-permute-done((bf16[256,2048]{1,0:T(8,128)(2,1)}, bf16[256,2048]{1,0:T(8,128)(2,1)S(1)}, u32[]{:S(2)}, u32[]{:S(2)}) %collective-permute-start.5) | collective-permute-done | bytes 1048608 | tf_op jit(solution)/shard_map/ppermute | solution.py:62
  183.4 35.6 %collective-permute-done.7 = bf16[256,2048]{1,0:T(8,128)(2,1)} collective-permute-done((bf16[256,2048]{1,0:T(8,128)(2,1)}, bf16[256,2048]{1,0:T(8,128)(2,1)}, u32[]{:S(2)}, u32[]{:S(2)}) %collective-permute-start.7) | collective-permute-done | bytes 1048608 | tf_op jit(solution)/shard_map/ppermute | solution.py:62
  238.1 44.9 %collective-permute-done.8 = bf16[256,2048]{1,0:T(8,128)(2,1)} collective-permute-done((bf16[256,2048]{1,0:T(8,128)(2,1)}, bf16[256,2048]{1,0:T(8,128)(2,1)}, u32[]{:S(2)}, u32[]{:S(2)}) %collective-permute-start.8) | collective-permute-done | bytes 1048608 | tf_op jit(solution)/shard_map/ppermute | solution.py:62
  304.3 10.5 %fusion.90 = f32[1280,1024]{1,0:T(8,128)} fusion(bf16[2048,1024]{1,0:T(8,128)(2,1)} %all-gather.9.cloned.1.call-done, bf16[640,2048]{1,0:T(8,128)(2,1)} %collective-permute-done.9, bf16[640,2048]{1,0:T(8,128)(2,1)} %bitcast.169), kind=kOutput, calls=%fused_computation.153 | convolution fusion | flops 5379194880 | bytes 14680064 | tf_op jit(solution)/shard_map/dot_general | solution.py:58
  317.5 14.5 %multiply_convert_fusion.5 = (bf16[1280,1024]{1,0:T(8,128)(2,1)}, f32[1280,1024]{1,0:T(8,128)}) fusion(f32[1280,1024]{1,0:T(8,128)} %fusion.90, bf16[2048,1024]{1,0:T(8,128)(2,1)} %all-gather.11.cloned.1.call-done, bf16[640,2048]{1,0:T(8,128)(2,1)} %collective-permute-done.9, bf16[640,2048]{1,0:T(8,128)(2,1)} %bitcast.170), kind=kOutput, calls=%fused_computation.71 | convolution fusion | flops 5387059200 | bytes 22544384 | tf_op jit(solution)/shard_map/dot_general | solution.py:58
  332.0 21.1 %collective-permute-done.10 = bf16[256,2048]{1,0:T(8,128)(2,1)} collective-permute-done((bf16[256,2048]{1,0:T(8,128)(2,1)}, bf16[256,2048]{1,0:T(8,128)(2,1)}, u32[]{:S(2)}, u32[]{:S(2)}) %collective-permute-start.10) | collective-permute-done | bytes 1048608 | tf_op jit(solution)/shard_map/ppermute | solution.py:62
  402.4 17.7 %all-to-all-done.4 = bf16[4,256,2048]{2,1,0:T(8,128)(2,1)} async-done(((bf16[4,256,2048]{2,1,0:T(8,128)(2,1)}), bf16[4,256,2048]{2,1,0:T(8,128)(2,1)}, u32[]{:S(2)}, u32[]{:S(2)}) %all-to-all-start.4) | async-done | bytes 4194336 | tf_op jit(solution)/shard_map/all_to_all | solution.py:85
  429.6 10.2 %fusion.3 = (bf16[1280,2048]{1,0:T(8,128)(2,1)}, f32[1280]{0:T(1024)S(1)}, bf16[1280,2048]{1,0:T(8,128)(2,1)}) fusion(f32[1280]{0:T(1024)S(1)} %get-tuple-element.281, bf16[640,2048]{1,0:T(8,128)(2,1)} %collective-permute-done.13, bf16[640,2048]{1,0:T(8,128)(2,1)S(1)} %bitcast.178, bf16[1280,1024]{1,0:T(8,128)(2,1)S(1)} %copy-done.92, ...), kind=kOutput, calls=%fused_computation.17 | convolution fusion | flops 5400165376 | bytes 22554624 | tf_op jit(solution)/shard_map/dot_general | solution.py:46
  441.2 10.5 %fusion.181 = f32[1280,1024]{1,0:T(8,128)} fusion(bf16[1280,2048]{1,0:T(8,128)(2,1)} %pad_maximum_fusion.3, bf16[2048,1024]{1,0:T(8,128)(2,1)} %all-gather.9.cloned.1.call-done), kind=kOutput, calls=%fused_computation.341 | convolution fusion | flops 5368709120 | bytes 14680064 | tf_op jit(solution)/shard_map/dot_general | solution.py:58
  454.7 7.3 fusion.180
  462.0 13.1 %multiply_convert_fusion.2 = (bf16[1280,1024]{1,0:T(8,128)(2,1)}, bf16[1280,1024]{1,0:T(8,128)(2,1)}, bf16[1280,1024]{1,0:T(8,128)(2,1)S(1)}) fusion(f32[1280,1024]{1,0:T(8,128)} %fusion.181, f32[1280,1024]{1,0:T(8,128)} %fusion.180, bf16[1280,2048]{1,0:T(8,128)(2,1)S(1)} %bitcast.155, bf16[2048,1024]{1,0:T(8,128)(2,1)} %all-gather.11.cloned.1.call-done), kind=kOutput, calls=%fused_computation.66 | convolution fusion | flops 5388369920 | bytes 27787264 | tf_op jit(solution)/shard_map/dot_general | solution.py:58
  475.1 10.9 %fusion.182 = f32[1280,2048]{1,0:T(8,128)} fusion(bf16[1280,1024]{1,0:T(8,128)(2,1)} %get-tuple-element.298, bf16[2048,1024]{1,0:T(8,128)(2,1)S(1)} %copy-done.82), kind=kOutput, calls=%fused_computation.342 | convolution fusion | flops 5368709120 | bytes 17301504 | tf_op jit(solution)/shard_map/dot_general | solution.py:46
  486.0 9.8 convolution_add_fusion
  500.8 9.4 fusion.5
  515.9 17.2 %fusion.45 = bf16[2048,1024]{1,0:T(8,128)(2,1)} fusion(bf16[1280,1024]{1,0:T(8,128)(2,1)} %get-tuple-element.297, bf16[1280,1024]{1,0:T(8,128)(2,1)} %get-tuple-element.146, bf16[1280,2048]{1,0:T(8,128)(2,1)} %copy-done.36, bf16[1280,2048]{1,0:T(8,128)(2,1)} %get-tuple-element.148), kind=kOutput, calls=%fused_computation.95 | convolution fusion | flops 10770972672 | bytes 19922944 | tf_op jit(solution)/shard_map/dot_general | solution.py:52
  533.1 7.0 fusion.59
  540.2 5.8 fusion.168
  551.2 13.4 %multiply_convert_fusion = (bf16[1280,1024]{1,0:T(8,128)(2,1)S(1)}, bf16[1280,1024]{1,0:T(8,128)(2,1)S(1)}) fusion(f32[1280,1024]{1,0:T(8,128)} %fusion.90, f32[1280,1024]{1,0:T(8,128)} %get-tuple-element.345, bf16[1280,2048]{1,0:T(8,128)(2,1)} %get-tuple-element.148, bf16[2048,1024]{1,0:T(8,128)(2,1)} %all-gather.13.cloned.1.call-done), kind=kOutput, calls=%fused_computation.64 | convolution fusion | flops 5385748480 | bytes 25165824 | tf_op jit(solution)/shard_map/dot_general | solution.py:58
  564.7 8.3 fusion.183
  573.0 11.4 %add_convert_fusion = bf16[1280,2048]{1,0:T(8,128)(2,1)} fusion(f32[1280,2048]{1,0:T(8,128)} %fusion.183, bf16[1280,1024]{1,0:T(8,128)(2,1)S(1)} %get-tuple-element.154, bf16[2048,1024]{1,0:T(8,128)(2,1)} %all-gather.11.cloned.1.call-done), kind=kOutput, calls=%fused_computation.25 | convolution fusion | flops 5373952000 | bytes 22544384 | tf_op jit(solution)/shard_map/dot_general | solution.py:46
  591.3 16.1 %fusion.42 = bf16[2048,1024]{1,0:T(8,128)(2,1)} fusion(bf16[1280,1024]{1,0:T(8,128)(2,1)} %get-tuple-element.298, bf16[1280,1024]{1,0:T(8,128)(2,1)} %copy-done.91, bf16[1280,2048]{1,0:T(8,128)(2,1)S(1)} %bitcast.157, bf16[640,2048]{1,0:T(8,128)(2,1)} %collective-permute-done.9, bf16[640,2048]{1,0:T(8,128)(2,1)S(1)} %bitcast.172), kind=kOutput, calls=%fused_computation.94 | convolution fusion | flops 10781458432 | bytes 19922944 | tf_op jit(solution)/shard_map/dot_general | solution.py:52
  613.6 6.2 fusion.56
  624.9 7.2 fusion.53
  632.1 6.3 fusion.50
  641.1 8.2 convolution_convert_fusion.7
  649.3 23.6 %all-to-all-done.7 = bf16[4,256,2048]{2,1,0:T(8,128)(2,1)} async-done(((bf16[4,256,2048]{2,1,0:T(8,128)(2,1)}), bf16[4,256,2048]{2,1,0:T(8,128)(2,1)}, u32[]{:S(2)}, u32[]{:S(2)}) %all-to-all-start.7) | async-done | bytes 4194336 | tf_op jit(solution)/shard_map/all_to_all | solution.py:85
  676.2 10.7 %collective-permute-done.16 = bf16[256,2048]{1,0:T(8,128)(2,1)} collective-permute-done((bf16[256,2048]{1,0:T(8,128)(2,1)}, bf16[256,2048]{1,0:T(8,128)(2,1)}, u32[]{:S(2)}, u32[]{:S(2)}) %collective-permute-start.16) | collective-permute-done | bytes 1048608 | tf_op jit(solution)/shard_map/ppermute | solution.py:62
  715.3 6.3 shard_map.295
  725.1 17.1 %all-to-all-done.8 = bf16[4,256,2048]{2,1,0:T(8,128)(2,1)} async-done(((bf16[4,256,2048]{2,1,0:T(8,128)(2,1)}), bf16[4,256,2048]{2,1,0:T(8,128)(2,1)}, u32[]{:S(2)}, u32[]{:S(2)}) %all-to-all-start.8) | async-done | bytes 4194336 | tf_op jit(solution)/shard_map/all_to_all | solution.py:85
  746.6 8.2 collective-permute-done.20
  757.9 7.6 shard_map.296
  768.9 7.6 shard_map.297
  781.9 7.6 shard_map.298
  789.6 6.1 shard_map.299
  796.2 13.0 %all_to_all.91 = f32[32,1,1216]{2,1,0:T(1,128)} all-to-all(f32[32,1,1216]{2,1,0:T(1,128)S(1)} %copy.67), channel_id=1, replica_groups=mesh['shard'=8,'context'=2,'tensor'=2] {'shard','context','tensor'}, dimensions={0} | all-to-all | bytes 311296 | tf_op jit(solution)/shard_map/all_to_all | solution.py:99
  830.6 7.5 add_convert_fusion.1
  840.4 6.5 shard_map.300
  846.9 5.8 convolution_convert_fusion.11
  852.8 8.8 all-to-all-done.9
  864.7 14.5 %all-gather.15.cloned.1.call-done = bf16[512,2048]{1,0:T(8,128)(2,1)} async-done(((bf16[256,2048]{1,0:T(8,128)(2,1)}), bf16[512,2048]{1,0:T(8,128)(2,1)}) %all-gather.15.cloned.1.call-update) | async-done | bytes 2097168 | tf_op jit(solution)/shard_map/all_gather | solution.py:787
  883.7 11.2 %convolution_convert_fusion = bf16[2048,1536]{1,0:T(8,128)(2,1)} fusion(bf16[1024,1536]{1,0:T(8,128)(2,1)} %shard_map.300, bf16[256,2048]{1,0:T(8,128)(2,1)} %get-tuple-element.336, bf16[256,2048]{1,0:T(8,128)(2,1)} %get-tuple-element.335, bf16[256,2048]{1,0:T(8,128)(2,1)} %get-tuple-element.334, bf16[256,2048]{1,0:T(8,128)(2,1)S(1)} %copy-done.59), kind=kOutput, calls=%fused_computation.29 | convolution fusion | flops 6462373888 | bytes 13631488 | tf_op jit(solution)/shard_map/dot_general | solution.py:52
  894.9 6.3 fusion.99
  901.2 6.1 fusion.97
  926.6 34.4 %collective-permute-done.27 = bf16[256,2048]{1,0:T(8,128)(2,1)} collective-permute-done((bf16[256,2048]{1,0:T(8,128)(2,1)}, bf16[256,2048]{1,0:T(8,128)(2,1)}, u32[]{:S(2)}, u32[]{:S(2)}) %collective-permute-start.27) | collective-permute-done | bytes 1048608 | tf_op jit(solution)/shard_map/ppermute | solution.py:62
  979.2 10.6 %add_bitcast_fusion = f32[1,2048,512]{2,1,0:T(8,128)} fusion(bf16[2048,512]{1,0:T(8,128)(2,1)S(1)} %copy-done.57, s32[]{:T(128)S(6)} %select_n.127, bf16[1280,1024]{1,0:T(8,128)(2,1)} %copy-done.89, bf16[1280,1024]{1,0:T(8,128)(2,1)} %copy-done.87, bf16[1280,2048]{1,0:T(8,128)(2,1)S(1)} %bitcast.161, bf16[640,2048]{1,0:T(8,128)(2,1)} %collective-permute-done.9, ...), kind=kOutput, calls=%fused_computation.88 | convolution fusion | flops 5407506432 | bytes 22020100 | tf_op jit(solution)/shard_map/dot_general | solution.py:52
  (493 shorter events, 377.2 us)
Async XLA Ops:
  7.2 84.6 %all-gather.7.cloned.1.call-start = ((), (), s32[]{:S(2)}) async-start(), calls=%async_computation.16 | async-start | bytes 9437184 | tf_op jit(solution)/shard_map/all_gather | solution.py:658
  9.6 59.2 %collective-permute-start = (bf16[256,2048]{1,0:T(8,128)(2,1)}, bf16[256,2048]{1,0:T(8,128)(2,1)S(1)}, u32[]{:S(2)}, u32[]{:S(2)}) collective-permute-start(bf16[256,2048]{1,0:T(8,128)(2,1)} %param.21), channel_id=1, source_target_pairs={{0,1},{1,0},{2,3},{3,2},{4,5},{5,4},{6,7},{7,6},{8,9},{9,8},{10,11... | collective-permute-start | bytes 3145736 | tf_op jit(solution)/shard_map/ppermute | solution.py:62
  12.7 51.3 %collective-permute-start.1 = (bf16[256,2048]{1,0:T(8,128)(2,1)}, bf16[256,2048]{1,0:T(8,128)(2,1)S(1)}, u32[]{:S(2)}, u32[]{:S(2)}) collective-permute-start(bf16[256,2048]{1,0:T(8,128)(2,1)} %param.21), channel_id=1, source_target_pairs={{0,2},{2,0},{1,3},{3,1},{4,6},{6,4},{5,7},{7,5},{8,10},{10,8},{9,1... | collective-permute-start | bytes 3145736 | tf_op jit(solution)/shard_map/ppermute | solution.py:62
  24.8 41.6 %all-to-all-start = ((bf16[32,2,1664]{2,1,0:T(2,128)(2,1)}), bf16[32,2,1664]{2,1,0:T(2,128)(2,1)S(1)}, u32[]{:S(2)}, u32[]{:S(2)}) async-start(bf16[32,2,1664]{2,1,0:T(2,128)(2,1)} %reshape.416), calls=%async_computation | async-start | bytes 425984 | tf_op jit(solution)/shard_map/all_to_all | solution.py:99
  27.5 117.3 %all-gather.9.cloned.1.call-start = ((), (), s32[]{:S(2)}) async-start(), calls=%async_computation.17 | async-start | bytes 6291456 | tf_op jit(solution)/shard_map/all_gather | solution.py:413
  64.0 22.1 %collective-permute-start.2 = (bf16[256,2048]{1,0:T(8,128)(2,1)S(1)}, bf16[256,2048]{1,0:T(8,128)(2,1)}, u32[]{:S(2)}, u32[]{:S(2)}) collective-permute-start(bf16[256,2048]{1,0:T(8,128)(2,1)S(1)} %collective-permute-done.1), channel_id=1, source_target_pairs={{0,1},{1,0},{2,3},{3,2},{4,5},{5,4},{6,7},{7,6},{8,9},{9,8},{10,11... | collective-permute-start | bytes 3145736 | tf_op jit(solution)/shard_map/ppermute | solution.py:62
  112.6 8.5 collective-permute-start.4
  116.1 102.9 %all-to-all-start.1 = ((bf16[4,256,2048]{2,1,0:T(8,128)(2,1)}), bf16[4,256,2048]{2,1,0:T(8,128)(2,1)}, u32[]{:S(2)}, u32[]{:S(2)}) async-start(bf16[4,256,2048]{2,1,0:T(8,128)(2,1)} %broadcast_in_dim.68), calls=%async_computation.1 | async-start | bytes 8388608 | tf_op jit(solution)/shard_map/all_to_all | solution.py:85
  144.8 25.1 %collective-permute-start.5 = (bf16[256,2048]{1,0:T(8,128)(2,1)}, bf16[256,2048]{1,0:T(8,128)(2,1)S(1)}, u32[]{:S(2)}, u32[]{:S(2)}) collective-permute-start(bf16[256,2048]{1,0:T(8,128)(2,1)} %convolution_convert_fusion.9), channel_id=1, source_target_pairs={{0,1},{1,0},{2,3},{3,2},{4,5},{5,4},{6,7},{7,6},{8,9},{9,8},{10,11... | collective-permute-start | bytes 3145736 | tf_op jit(solution)/shard_map/ppermute | solution.py:62
  171.2 47.8 %collective-permute-start.7 = (bf16[256,2048]{1,0:T(8,128)(2,1)}, bf16[256,2048]{1,0:T(8,128)(2,1)}, u32[]{:S(2)}, u32[]{:S(2)}) collective-permute-start(bf16[256,2048]{1,0:T(8,128)(2,1)} %add_convert_fusion.3), channel_id=1, source_target_pairs={{0,2},{2,0},{1,3},{3,1},{4,6},{6,4},{5,7},{7,5},{8,10},{10,8},{9,1... | collective-permute-start | bytes 3145736 | tf_op jit(solution)/shard_map/ppermute | solution.py:62
  173.6 46.4 %collective-permute-start.6 = (bf16[256,2048]{1,0:T(8,128)(2,1)}, bf16[256,2048]{1,0:T(8,128)(2,1)}, u32[]{:S(2)}, u32[]{:S(2)}) collective-permute-start(bf16[256,2048]{1,0:T(8,128)(2,1)} %convolution_convert_fusion.8), channel_id=1, source_target_pairs={{0,1},{1,0},{2,3},{3,2},{4,5},{5,4},{6,7},{7,6},{8,9},{9,8},{10,11... | collective-permute-start | bytes 3145736 | tf_op jit(solution)/shard_map/ppermute | solution.py:62
  231.0 52.0 %all-to-all-start.2 = ((bf16[4,256,2048]{2,1,0:T(8,128)(2,1)}), bf16[4,256,2048]{2,1,0:T(8,128)(2,1)}, u32[]{:S(2)}, u32[]{:S(2)}) async-start(bf16[4,256,2048]{2,1,0:T(8,128)(2,1)} %broadcast_in_dim.71), calls=%async_computation.2 | async-start | bytes 8388608 | tf_op jit(solution)/shard_map/all_to_all | solution.py:85
  235.9 81.7 %all-gather.11.cloned.1.call-start = ((), (), s32[]{:S(2)}) async-start(), calls=%async_computation.18 | async-start | bytes 6291456 | tf_op jit(solution)/shard_map/all_gather | solution.py:413
  236.1 46.9 %collective-permute-start.8 = (bf16[256,2048]{1,0:T(8,128)(2,1)}, bf16[256,2048]{1,0:T(8,128)(2,1)}, u32[]{:S(2)}, u32[]{:S(2)}) collective-permute-start(bf16[256,2048]{1,0:T(8,128)(2,1)} %multiply_convert_fusion.6), channel_id=1, source_target_pairs={{0,2},{2,0},{1,3},{3,1},{4,6},{6,4},{5,7},{7,5},{8,10},{10,8},{9,1... | collective-permute-start | bytes 3145736 | tf_op jit(solution)/shard_map/ppermute | solution.py:62
  289.9 14.4 %collective-permute-start.9 = (bf16[640,2048]{1,0:T(8,128)(2,1)}, bf16[640,2048]{1,0:T(8,128)(2,1)}, u32[]{:S(2)}, u32[]{:S(2)}) collective-permute-start(bf16[640,2048]{1,0:T(8,128)(2,1)} %bitcast.17), channel_id=1, source_target_pairs={{0,4},{4,0},{8,12},{12,8},{16,20},{20,16},{24,28},{28,24},{1,5},{5... | collective-permute-start | bytes 7864328 | tf_op jit(solution)/shard_map/ppermute | solution.py:67
  296.7 56.4 %all-to-all-start.3 = ((bf16[4,256,2048]{2,1,0:T(8,128)(2,1)}), bf16[4,256,2048]{2,1,0:T(8,128)(2,1)}, u32[]{:S(2)}, u32[]{:S(2)}) async-start(bf16[4,256,2048]{2,1,0:T(8,128)(2,1)} %broadcast_in_dim.72), calls=%async_computation.3 | async-start | bytes 8388608 | tf_op jit(solution)/shard_map/all_to_all | solution.py:85
  301.6 96.5 %all-gather.13.cloned.1.call-start = ((), (), s32[]{:S(2)}) async-start(), calls=%async_computation.19 | async-start | bytes 6291456 | tf_op jit(solution)/shard_map/all_gather | solution.py:413
  304.3 48.8 %collective-permute-start.10 = (bf16[256,2048]{1,0:T(8,128)(2,1)}, bf16[256,2048]{1,0:T(8,128)(2,1)}, u32[]{:S(2)}, u32[]{:S(2)}) collective-permute-start(bf16[256,2048]{1,0:T(8,128)(2,1)} %param.22), channel_id=1, source_target_pairs={{0,2},{2,0},{1,3},{3,1},{4,6},{6,4},{5,7},{7,5},{8,10},{10,8},{9,1... | collective-permute-start | bytes 3145736 | tf_op jit(solution)/shard_map/ppermute | solution.py:62
  360.0 27.7 %collective-permute-start.11 = (bf16[640,2048]{1,0:T(8,128)(2,1)}, bf16[640,2048]{1,0:T(8,128)(2,1)}, u32[]{:S(2)}, u32[]{:S(2)}) collective-permute-start(bf16[640,2048]{1,0:T(8,128)(2,1)} %bitcast.19), channel_id=1, source_target_pairs={{0,4},{4,0},{8,12},{12,8},{16,20},{20,16},{24,28},{28,24},{1,5},{5... | collective-permute-start | bytes 7864328 | tf_op jit(solution)/shard_map/ppermute | solution.py:67
  366.4 53.6 %all-to-all-start.4 = ((bf16[4,256,2048]{2,1,0:T(8,128)(2,1)}), bf16[4,256,2048]{2,1,0:T(8,128)(2,1)}, u32[]{:S(2)}, u32[]{:S(2)}) async-start(bf16[4,256,2048]{2,1,0:T(8,128)(2,1)} %broadcast_in_dim.74), calls=%async_computation.4 | async-start | bytes 8388608 | tf_op jit(solution)/shard_map/all_to_all | solution.py:85
  383.1 44.2 %collective-permute-start.13 = (bf16[640,2048]{1,0:T(8,128)(2,1)}, bf16[640,2048]{1,0:T(8,128)(2,1)}, u32[]{:S(2)}, u32[]{:S(2)}) collective-permute-start(bf16[640,2048]{1,0:T(8,128)(2,1)} %bitcast.23), channel_id=1, source_target_pairs={{0,4},{4,0},{8,12},{12,8},{16,20},{20,16},{24,28},{28,24},{1,5},{5... | collective-permute-start | bytes 7864328 | tf_op jit(solution)/shard_map/ppermute | solution.py:67
  427.3 24.4 %collective-permute-start.12 = (bf16[640,2048]{1,0:T(8,128)(2,1)}, bf16[640,2048]{1,0:T(8,128)(2,1)}, u32[]{:S(2)}, u32[]{:S(2)}) collective-permute-start(bf16[640,2048]{1,0:T(8,128)(2,1)} %bitcast.21), channel_id=1, source_target_pairs={{0,4},{4,0},{8,12},{12,8},{16,20},{20,16},{24,28},{28,24},{1,5},{5... | collective-permute-start | bytes 7864328 | tf_op jit(solution)/shard_map/ppermute | solution.py:67
  499.0 34.1 %collective-permute-start.14 = (bf16[640,2048]{1,0:T(8,128)(2,1)}, bf16[640,2048]{1,0:T(8,128)(2,1)}, u32[]{:S(2)}, u32[]{:S(2)}) collective-permute-start(bf16[640,2048]{1,0:T(8,128)(2,1)} %get-tuple-element.310), channel_id=1, source_target_pairs={{0,4},{4,0},{8,12},{12,8},{16,20},{20,16},{24,28},{28,24},{1,5},{5... | collective-permute-start | bytes 7864328 | tf_op jit(solution)/shard_map/ppermute | solution.py:67
  512.3 20.8 %all-to-all-start.5 = ((f32[16,1,256]{2,1,0:T(1,128)}), f32[16,1,256]{2,1,0:T(1,128)S(1)}, u32[]{:S(2)}, u32[]{:S(2)}) async-start(f32[16,1,256]{2,1,0:T(1,128)} %all_to_all.64), calls=%async_computation.5 | async-start | bytes 32768 | tf_op jit(solution)/shard_map/all_to_all | solution.py:525
  515.8 173.9 %reduce-scatter.4.cloned.1.call-start = ((), (), s32[]{:S(2)}) async-start(), calls=%async_computation.20 | async-start | bytes 6291456 | tf_op jit(solution)/shard_map/reduce_scatter | solution.py:404
  546.0 78.9 %collective-permute-start.17 = (bf16[640,2048]{1,0:T(8,128)(2,1)}, bf16[640,2048]{1,0:T(8,128)(2,1)}, u32[]{:S(2)}, u32[]{:S(2)}) collective-permute-start(bf16[640,2048]{1,0:T(8,128)(2,1)} %get-tuple-element.305), channel_id=1, source_target_pairs={{0,4},{4,0},{8,12},{12,8},{16,20},{20,16},{24,28},{28,24},{1,5},{5... | collective-permute-start | bytes 7864328 | tf_op jit(solution)/shard_map/ppermute | solution.py:67
  546.3 61.1 %all-to-all-start.6 = ((bf16[4,256,2048]{2,1,0:T(8,128)(2,1)}), bf16[4,256,2048]{2,1,0:T(8,128)(2,1)}, u32[]{:S(2)}, u32[]{:S(2)}) async-start(bf16[4,256,2048]{2,1,0:T(8,128)(2,1)} %fusion.59), calls=%async_computation.6 | async-start | bytes 8388608 | tf_op jit(solution)/shard_map/all_to_all | solution.py:85
  551.2 203.6 %reduce-scatter.6.cloned.1.call-start = ((), (), s32[]{:S(2)}) async-start(), calls=%async_computation.21 | async-start | bytes 6291456 | tf_op jit(solution)/shard_map/reduce_scatter | solution.py:404
  588.0 23.7 %collective-permute-start.15 = (bf16[640,2048]{1,0:T(8,128)(2,1)}, bf16[640,2048]{1,0:T(8,128)(2,1)}, u32[]{:S(2)}, u32[]{:S(2)}) collective-permute-start(bf16[640,2048]{1,0:T(8,128)(2,1)} %slice.225), channel_id=1, source_target_pairs={{0,4},{4,0},{8,12},{12,8},{16,20},{20,16},{24,28},{28,24},{1,5},{5... | collective-permute-start | bytes 7864328 | tf_op jit(solution)/shard_map/ppermute | solution.py:67
  591.0 41.1 %collective-permute-start.18 = (bf16[640,2048]{1,0:T(8,128)(2,1)}, bf16[640,2048]{1,0:T(8,128)(2,1)}, u32[]{:S(2)}, u32[]{:S(2)}) collective-permute-start(bf16[640,2048]{1,0:T(8,128)(2,1)} %get-tuple-element.301), channel_id=1, source_target_pairs={{0,4},{4,0},{8,12},{12,8},{16,20},{20,16},{24,28},{28,24},{1,5},{5... | collective-permute-start | bytes 7864328 | tf_op jit(solution)/shard_map/ppermute | solution.py:67
  619.8 53.2 %all-to-all-start.7 = ((bf16[4,256,2048]{2,1,0:T(8,128)(2,1)}), bf16[4,256,2048]{2,1,0:T(8,128)(2,1)}, u32[]{:S(2)}, u32[]{:S(2)}) async-start(bf16[4,256,2048]{2,1,0:T(8,128)(2,1)} %fusion.56), calls=%async_computation.7 | async-start | bytes 8388608 | tf_op jit(solution)/shard_map/all_to_all | solution.py:85
  638.5 48.4 %collective-permute-start.16 = (bf16[256,2048]{1,0:T(8,128)(2,1)}, bf16[256,2048]{1,0:T(8,128)(2,1)}, u32[]{:S(2)}, u32[]{:S(2)}) collective-permute-start(bf16[256,2048]{1,0:T(8,128)(2,1)} %reduce_sum.277), channel_id=1, source_target_pairs={{0,2},{2,0},{1,3},{3,1},{4,6},{6,4},{5,7},{7,5},{8,10},{10,8},{9,1... | collective-permute-start | bytes 3145736 | tf_op jit(solution)/shard_map/ppermute | solution.py:62
  689.8 52.5 %all-to-all-start.8 = ((bf16[4,256,2048]{2,1,0:T(8,128)(2,1)}), bf16[4,256,2048]{2,1,0:T(8,128)(2,1)}, u32[]{:S(2)}, u32[]{:S(2)}) async-start(bf16[4,256,2048]{2,1,0:T(8,128)(2,1)} %fusion.50), calls=%async_computation.9 | async-start | bytes 8388608 | tf_op jit(solution)/shard_map/all_to_all | solution.py:85
  704.5 50.7 %collective-permute-start.19 = (bf16[256,2048]{1,0:T(8,128)(2,1)}, bf16[256,2048]{1,0:T(8,128)(2,1)}, u32[]{:S(2)}, u32[]{:S(2)}) collective-permute-start(bf16[256,2048]{1,0:T(8,128)(2,1)} %get-tuple-element.283), channel_id=1, source_target_pairs={{0,1},{1,0},{2,3},{3,2},{4,5},{5,4},{6,7},{7,6},{8,9},{9,8},{10,11... | collective-permute-start | bytes 3145736 | tf_op jit(solution)/shard_map/ppermute | solution.py:62
  706.9 47.9 %collective-permute-start.20 = (bf16[256,2048]{1,0:T(8,128)(2,1)}, bf16[256,2048]{1,0:T(8,128)(2,1)}, u32[]{:S(2)}, u32[]{:S(2)}) collective-permute-start(bf16[256,2048]{1,0:T(8,128)(2,1)} %get-tuple-element.283), channel_id=1, source_target_pairs={{0,2},{2,0},{1,3},{3,1},{4,6},{6,4},{5,7},{7,5},{8,10},{10,8},{9,1... | collective-permute-start | bytes 3145736 | tf_op jit(solution)/shard_map/ppermute | solution.py:62
  754.8 23.0 %collective-permute-start.21 = (bf16[256,2048]{1,0:T(8,128)(2,1)}, bf16[256,2048]{1,0:T(8,128)(2,1)S(1)}, u32[]{:S(2)}, u32[]{:S(2)}) collective-permute-start(bf16[256,2048]{1,0:T(8,128)(2,1)} %collective-permute-done.20), channel_id=1, source_target_pairs={{0,1},{1,0},{2,3},{3,2},{4,5},{5,4},{6,7},{7,6},{8,9},{9,8},{10,11... | collective-permute-start | bytes 3145736 | tf_op jit(solution)/shard_map/ppermute | solution.py:62
  777.8 40.5 %collective-permute-start.22 = (bf16[1024,512]{1,0:T(8,128)(2,1)}, bf16[1024,512]{1,0:T(8,128)(2,1)}, u32[]{:S(2)}, u32[]{:S(2)}) collective-permute-start(bf16[1024,512]{1,0:T(8,128)(2,1)} %get-tuple-element.186), channel_id=1, source_target_pairs={{0,1},{1,0},{2,3},{3,2},{4,5},{5,4},{6,7},{7,6},{8,9},{9,8},{10,11... | collective-permute-start | bytes 3145736 | tf_op jit(solution)/shard_map/ppermute | solution.py:62
  809.3 52.3 %all-to-all-start.9 = ((bf16[4,256,2048]{2,1,0:T(8,128)(2,1)}), bf16[4,256,2048]{2,1,0:T(8,128)(2,1)}, u32[]{:S(2)}, u32[]{:S(2)}) async-start(bf16[4,256,2048]{2,1,0:T(8,128)(2,1)} %fusion.53), calls=%async_computation.11 | async-start | bytes 8388608 | tf_op jit(solution)/shard_map/all_to_all | solution.py:85
  814.3 64.9 %all-gather.15.cloned.1.call-start = ((), (), s32[]{:S(2)}) async-start(), calls=%async_computation.23 | async-start | bytes 3145728 | tf_op jit(solution)/shard_map/all_gather | solution.py:787
  818.4 4.2 collective-permute-start.23
  823.3 4.6 collective-permute-start.24
  828.6 50.6 %collective-permute-start.25 = (bf16[1024,512]{1,0:T(8,128)(2,1)}, bf16[1024,512]{1,0:T(8,128)(2,1)}, u32[]{:S(2)}, u32[]{:S(2)}) collective-permute-start(bf16[1024,512]{1,0:T(8,128)(2,1)} %get-tuple-element.189), channel_id=1, source_target_pairs={{0,1},{1,0},{2,3},{3,2},{4,5},{5,4},{6,7},{7,6},{8,9},{9,8},{10,11... | collective-permute-start | bytes 3145736 | tf_op jit(solution)/shard_map/ppermute | solution.py:62
  879.2 30.8 %collective-permute-start.26 = (bf16[256,2048]{1,0:T(8,128)(2,1)}, bf16[256,2048]{1,0:T(8,128)(2,1)}, u32[]{:S(2)}, u32[]{:S(2)}) collective-permute-start(bf16[256,2048]{1,0:T(8,128)(2,1)} %convolution_convert_fusion.11), channel_id=1, source_target_pairs={{0,1},{1,0},{2,3},{3,2},{4,5},{5,4},{6,7},{7,6},{8,9},{9,8},{10,11... | collective-permute-start | bytes 3145736 | tf_op jit(solution)/shard_map/ppermute | solution.py:62
  879.2 31.1 %all-to-all-start.11 = ((bf16[8,256,512]{2,1,0:T(8,128)(2,1)}), bf16[8,256,512]{2,1,0:T(8,128)(2,1)}, u32[]{:S(2)}, u32[]{:S(2)}) async-start(bf16[8,256,512]{2,1,0:T(8,128)(2,1)} %bitcast.165), calls=%async_computation.13 | async-start | bytes 4194304 | tf_op jit(solution)/shard_map/all_to_all | solution.py:836
  883.6 109.3 %reduce-scatter.8.cloned.1.call-start = ((), (), s32[]{:S(2)}) async-start(), calls=%async_computation.22 | async-start | bytes 7077888 | tf_op jit(solution)/shard_map/reduce_scatter | solution.py:852
  913.6 48.9 %collective-permute-start.28 = (bf16[256,2048]{1,0:T(8,128)(2,1)}, bf16[256,2048]{1,0:T(8,128)(2,1)}, u32[]{:S(2)}, u32[]{:S(2)}) collective-permute-start(bf16[256,2048]{1,0:T(8,128)(2,1)} %add_convert_fusion.2), channel_id=1, source_target_pairs={{0,2},{2,0},{1,3},{3,1},{4,6},{6,4},{5,7},{7,5},{8,10},{10,8},{9,1... | collective-permute-start | bytes 3145736 | tf_op jit(solution)/shard_map/ppermute | solution.py:62
  915.4 45.5 %collective-permute-start.27 = (bf16[256,2048]{1,0:T(8,128)(2,1)}, bf16[256,2048]{1,0:T(8,128)(2,1)}, u32[]{:S(2)}, u32[]{:S(2)}) collective-permute-start(bf16[256,2048]{1,0:T(8,128)(2,1)} %convolution_convert_fusion.10), channel_id=1, source_target_pairs={{0,1},{1,0},{2,3},{3,2},{4,5},{5,4},{6,7},{7,6},{8,9},{9,8},{10,11... | collective-permute-start | bytes 3145736 | tf_op jit(solution)/shard_map/ppermute | solution.py:62
  966.2 26.3 %all-to-all-start.12 = ((f32[32,1,64]{2,1,0:T(1,128)}), f32[32,1,64]{2,1,0:T(1,128)S(1)}, u32[]{:S(2)}, u32[]{:S(2)}) async-start(f32[32,1,64]{2,1,0:T(1,128)} %all_to_all.76), calls=%async_computation.15 | async-start | bytes 32768 | tf_op jit(solution)/shard_map/all_to_all | solution.py:99
  (108 other events, 2138.3 us)
Sparse Core Ops, SparseCore 0:
  10.5 59.1 all-gather.6
  87.7 57.0 all-gather.8
  238.3 79.2 all-gather.10
  318.9 79.0 all-gather.12
  540.3 55.2 reduce-scatter.3
  611.8 77.9 reduce-scatter.5
  822.7 56.4 all-gather.14
  910.4 61.5 reduce-scatter.7

commit v4 on v3

--- a/solution.py
+++ b/solution.py
@@ -395,9 +395,8 @@
     return contract_first(left, columns_of(right, 1 - lax.axis_index("tensor"))).astype(LOW)
 
 
-def own_grad(left, right, arrived):
-    mine = contract_first(left, columns_of(right, lax.axis_index("tensor")))
-    return mine + arrived.astype(WIDE)
+def my_grad(left, right):
+    return contract_first(left, columns_of(right, lax.axis_index("tensor")))
 
 
 def owned_grad(total):
@@ -550,16 +549,17 @@
     )
     gate_grad = owned_grad(gate_total)
     near_parts = combine(near_route[:near_half], near_swapped, *picks[0][:2])
-    up_pair = (all_rows, both(near_up_act, far_up_act))
     far_arrived = swap(far_grad, "context")
-    grad, mixture_parts, rest_parts, up_theirs, down_grad = sync(
+    far_arrived, mixture_parts, rest_parts = sync(far_arrived, mixture_parts, rest_parts)
+    grad, mixture_parts, rest_parts, down_grad, far_up_act = sync(
         sum_chips(near_parts) + far_arrived.astype(WIDE),
         mixture_parts,
         rest_parts,
-        their_grad(*up_pair),
         down_grad,
-    )
-    later = (mixture_parts, rest_parts, gate_grad, down_grad, up_theirs, up_pair)
+        far_up_act,
+    )
+    up_pair = (all_rows, both(near_up_act, far_up_act))
+    later = (mixture_parts, rest_parts, gate_grad, down_grad, up_pair)
     return (grad, by_expert.T, later)
 
 
@@ -747,8 +747,7 @@
             late_down,
             capacity,
         )
-        mixture_parts, rest_parts, gate_grad, down_grad, up_theirs, up_pair = later
-        up_halves = halves(up_theirs)
+        mixture_parts, rest_parts, gate_grad, down_grad, up_pair = later
     else:
         weights = (gate_weight, whole_weight(late_up), whole_weight(late_down))
         grad_from_experts, grad_router_probs, mixture, expert_grads = experts_by_slots(
@@ -783,7 +782,10 @@
     if by_blocks:
         rest = sum_chips(rest_parts).astype(LOW)
     if by_blocks:
-        across, own_sums, rest, gate_grad = sync(across, tuple(own_sums), rest, gate_grad)
+        across, own_sums, rest, gate_grad, up_mine, up_theirs = sync(
+            across, tuple(own_sums), rest, gate_grad, my_grad(*up_pair), their_grad(*up_pair)
+        )
+        up_halves = halves(up_theirs)
         others = lax.all_gather(rest, "context", axis=0, tiled=False)
     last = swap(across, "tensor")
     near_query, near_sums = piece_back(1, near_piece, own_sums)
@@ -827,42 +829,42 @@
 
     far_part = contract_last(block_of(grad_pre, 3), qkv_cols).astype(LOW)
     if by_blocks:
-        far_part, grad_pre, up_second, others, mixture, out_total = sync(
-            far_part, grad_pre, swap(up_late, "tensor"), others, mixture, out_total
-        )
-        other = lax.dynamic_index_in_dim(others, lax.axis_index("context") ^ 1, 0, False)
-        mixture = mixture + other.astype(WIDE)
-    block_output = (middle + mixture).astype(LOW)
+        far_part, grad_pre, out_total, mixture = sync(far_part, grad_pre, out_total, mixture)
     out_dealt = lax.all_to_all(out_total, "shard", split_axis=0, concat_axis=0, tiled=True)
     far = swap(far_part, "tensor")
     head_total = contract_first(low_group, grad_pre).astype(LOW)
     parts = [contract_last(block_of(grad_pre, k), qkv_cols) for k in range(3)]
+    far, head_total, near_part, out_dealt, *parts = sync(
+        far, head_total, parts[1].astype(LOW), out_dealt, parts[0], parts[2]
+    )
+    if by_blocks:
+        other = lax.dynamic_index_in_dim(others, lax.axis_index("context") ^ 1, 0, False)
+        mixture = mixture + other.astype(WIDE)
+    block_output = (middle + mixture).astype(LOW)
+    across = swap((parts[1] + far.astype(WIDE)).astype(LOW), "context")
+    near = swap(near_part, "tensor")
+    head_grads = lax.psum_scatter(head_total, "shard", scatter_dimension=0, tiled=True).astype(WIDE)
+    if by_blocks:
+        near, across, gate_grad, down_grad, up_late = sync(
+            near, across, gate_grad, down_grad, up_late
+        )
+        up_arrived = jnp.concatenate([up_first, swap(up_late, "tensor")], axis=0)
+        expert_grads = (gate_grad, up_mine + up_arrived.astype(WIDE), down_grad)
+    out_grad = jnp.sum(
+        out_dealt.reshape((lax.axis_size("shard"),) + w_out.shape).astype(WIDE), axis=0
+    )
+    grad_first = parts[0] + near.astype(WIDE) + across.astype(WIDE)
+    grad_normed_first, grad_gain_first = rms_back(inputs, factor_first, gain_first, grad_first)
+    grad_input = grad_middle + grad_normed_first
     zero_gain = jnp.zeros((2, model_width), WIDE)
     grad_gains = lax.dynamic_update_slice(zero_gain, gain_grads, (0, group_index * column_span))
     by_device = [
         one.reshape(device_count, -1)
-        for one in (grad_router_weight, grad_gain_second, grad_gains[0], grad_gains[1])
+        for one in (grad_router_weight, grad_gain_first, grad_gain_second, grad_gains[0], grad_gains[1])
     ]
-    early = scatter_small(jnp.concatenate(by_device, axis=1))
-    far, head_total, near_part, early, out_dealt, *parts = sync(
-        far, head_total, parts[1].astype(LOW), early, out_dealt, parts[0], parts[2]
-    )
-    across = swap((parts[1] + far.astype(WIDE)).astype(LOW), "context")
-    near = swap(near_part, "tensor")
-    head_grads = lax.psum_scatter(head_total, "shard", scatter_dimension=0, tiled=True).astype(WIDE)
-    if by_blocks:
-        up_arrived = jnp.concatenate([up_first, up_second], axis=0)
-        near, gate_grad, down_grad, up_arrived = sync(near, gate_grad, down_grad, up_arrived)
-        expert_grads = (gate_grad, own_grad(*up_pair, up_arrived), down_grad)
-    out_grad = jnp.sum(
-        out_dealt.reshape((lax.axis_size("shard"),) + w_out.shape).astype(WIDE), axis=0
-    )
-    grad_first = parts[0] + near.astype(WIDE) + across.astype(WIDE)
-    grad_normed_first, grad_gain_first = rms_back(inputs, factor_first, gain_first, grad_first)
-    grad_input = grad_middle + grad_normed_first
-    late = scatter_small(grad_gain_first.reshape(device_count, -1))
-    router_grad = early[:router_size].reshape(router_rows, expert_count)
-    rest = early[router_size:].reshape(3, router_rows)
+    small_grads = scatter_small(jnp.concatenate(by_device, axis=1))
+    router_grad = small_grads[:router_size].reshape(router_rows, expert_count)
+    gain_totals = small_grads[router_size:].reshape(4, router_rows)
     return (
         block_output,
         grad_input,
@@ -871,10 +873,7 @@
         head_grads[:, 2 * column_span : 3 * column_span],
         out_grad,
         router_grad,
-        late,
-        rest[0],
-        rest[1],
-        rest[2],
+        *(gain_totals[i] for i in range(4)),
         *(grad.astype(WIDE)[None] for grad in expert_grads),
     )
 

time: 1010 us -> 985 us (0.975)
  waiting for transfers between devices: 321 us -> 299 us
  blocking collectives: 13 us -> 0 us
    all_to_all x8, waiting for transfers between devices: 67.3 us -> 29.8 us  [over_chips(): lax.all_to_all(blocks, 'shard', split_axis=0, concat_axis=0, axis_index_g...]
    ppermute x21, waiting for transfers between devices: 221 us -> 246 us  [swap(): return lax.ppermute(values, axis, SWAP)]
    all_gather x1, waiting for transfers between devices: 14.5 us -> 0.01 us  [local(): others = lax.all_gather(rest, 'context', axis=0, tiled=False)]
    all_to_all x1 -> x0, blocking collectives: 13 us -> none  [deal(): lax.all_to_all(rows, DEVICES, split_axis=0, concat_axis=0, tiled=True)]
    unnamed x223 -> x206, local copies, waits for them, and re-layouts: 21.6 us -> 28.5 us
  transfers between devices with their start and end apart: 49 -> 49, of which waited for: 23 -> 20; matrix products, arithmetic and copies ran while one was open for 42% -> 49% of each run, Pallas kernels for 6% -> 7%
where the time goes in v4:
time: 985 us; the launch traced here: 980 us
  matrix products  325 us (33%)
  waiting for transfers between devices  299 us (30%)
  local copies, waits for them, and re-layouts  96.7 us (10%)
  other arithmetic  92.6 us (9%)
  starting transfers between devices  86.7 us (9%)
  Pallas kernels  64.1 us (7%)
  between operations  16.2 us (2%)
    ppermute x21, waiting for transfers between devices, swap(): return lax.ppermute(values, axis, SWAP)  246 us
    dot_general x23, matrix products, plain(): return jnp.dot(left, right, preferred_element_type=jnp.float32)  104 us
    dot_general x15, matrix products, contract_last(): lax.dot_general(left, right, (((1,), (1,)), ((), ())), preferred_element_...  96.3 us
    dot_general x10, matrix products, contract_first(): lax.dot_general(left, right, (((0,), (0,)), ((), ())), preferred_element_...  81 us
    all_to_all x8, starting transfers between devices, over_chips(): lax.all_to_all(blocks, 'shard', split_axis=0, concat_axis=0, axis_index_g...  39.6 us
    all_to_all x8, waiting for transfers between devices, over_chips(): lax.all_to_all(blocks, 'shard', split_axis=0, concat_axis=0, axis_index_g...  29.8 us
    pallas_call x4, Pallas kernels, attend_block_back(): pl.pallas_call(lambda *refs: attend_back_kernel(which, sums is None, *ref...  29.3 us
    unnamed x206, local copies, waits for them, and re-layouts  28.5 us
  transfers between devices with their start and end apart: 49, of which 20 were waited for; matrix products, arithmetic and copies ran while one was open for 49% of the time, Pallas kernels for 7%

profile of v4, /device:TPU:0, one launch (start us, length us, event | category | flops | bytes accessed | tf_op | source)
XLA Modules:
  0.0 980.4 jit_solution(13466654565229042828)
XLA Ops:
  31.9 32.1 %collective-permute-done.1 = bf16[256,2048]{1,0:T(8,128)(2,1)S(1)} collective-permute-done((bf16[256,2048]{1,0:T(8,128)(2,1)}, bf16[256,2048]{1,0:T(8,128)(2,1)S(1)}, u32[]{:S(2)}, u32[]{:S(2)}) %collective-permute-start.1) | collective-permute-done | bytes 1048608 | tf_op jit(solution)/shard_map/ppermute | solution.py:62
  69.8 16.3 %collective-permute-done.2 = bf16[256,2048]{1,0:T(8,128)(2,1)} collective-permute-done((bf16[256,2048]{1,0:T(8,128)(2,1)S(1)}, bf16[256,2048]{1,0:T(8,128)(2,1)}, u32[]{:S(2)}, u32[]{:S(2)}) %collective-permute-start.2) | collective-permute-done | bytes 1048608 | tf_op jit(solution)/shard_map/ppermute | solution.py:62
  91.8 5.7 fusion.102
  137.1 7.7 all-gather.9.cloned.1.call-done
  159.8 10.1 %collective-permute-done.5 = bf16[256,2048]{1,0:T(8,128)(2,1)S(1)} collective-permute-done((bf16[256,2048]{1,0:T(8,128)(2,1)}, bf16[256,2048]{1,0:T(8,128)(2,1)S(1)}, u32[]{:S(2)}, u32[]{:S(2)}) %collective-permute-start.5) | collective-permute-done | bytes 1048608 | tf_op jit(solution)/shard_map/ppermute | solution.py:62
  183.3 35.7 %collective-permute-done.7 = bf16[256,2048]{1,0:T(8,128)(2,1)} collective-permute-done((bf16[256,2048]{1,0:T(8,128)(2,1)}, bf16[256,2048]{1,0:T(8,128)(2,1)}, u32[]{:S(2)}, u32[]{:S(2)}) %collective-permute-start.7) | collective-permute-done | bytes 1048608 | tf_op jit(solution)/shard_map/ppermute | solution.py:62
  239.7 44.2 %collective-permute-done.8 = bf16[256,2048]{1,0:T(8,128)(2,1)} collective-permute-done((bf16[256,2048]{1,0:T(8,128)(2,1)}, bf16[256,2048]{1,0:T(8,128)(2,1)}, u32[]{:S(2)}, u32[]{:S(2)}) %collective-permute-start.8) | collective-permute-done | bytes 1048608 | tf_op jit(solution)/shard_map/ppermute | solution.py:62
  303.3 10.5 %fusion.89 = f32[1280,1024]{1,0:T(8,128)} fusion(bf16[2048,1024]{1,0:T(8,128)(2,1)} %all-gather.9.cloned.1.call-done, bf16[640,2048]{1,0:T(8,128)(2,1)} %collective-permute-done.9, bf16[640,2048]{1,0:T(8,128)(2,1)} %bitcast.165), kind=kOutput, calls=%fused_computation.150 | convolution fusion | flops 5379194880 | bytes 14680064 | tf_op jit(solution)/shard_map/dot_general | solution.py:58
  318.4 14.5 %multiply_convert_fusion.5 = (bf16[1280,1024]{1,0:T(8,128)(2,1)}, f32[1280,1024]{1,0:T(8,128)}) fusion(f32[1280,1024]{1,0:T(8,128)} %fusion.89, bf16[2048,1024]{1,0:T(8,128)(2,1)} %all-gather.11.cloned.1.call-done, bf16[640,2048]{1,0:T(8,128)(2,1)} %collective-permute-done.9, bf16[640,2048]{1,0:T(8,128)(2,1)} %bitcast.166), kind=kOutput, calls=%fused_computation.67 | convolution fusion | flops 5387059200 | bytes 22544384 | tf_op jit(solution)/shard_map/dot_general | solution.py:58
  332.9 19.1 %collective-permute-done.10 = bf16[256,2048]{1,0:T(8,128)(2,1)} collective-permute-done((bf16[256,2048]{1,0:T(8,128)(2,1)}, bf16[256,2048]{1,0:T(8,128)(2,1)}, u32[]{:S(2)}, u32[]{:S(2)}) %collective-permute-start.10) | collective-permute-done | bytes 1048608 | tf_op jit(solution)/shard_map/ppermute | solution.py:62
  388.4 8.6 all-gather.13.cloned.1.call-done
  401.2 16.6 %all-to-all-done.4 = bf16[4,256,2048]{2,1,0:T(8,128)(2,1)} async-done(((bf16[4,256,2048]{2,1,0:T(8,128)(2,1)}), bf16[4,256,2048]{2,1,0:T(8,128)(2,1)}, u32[]{:S(2)}, u32[]{:S(2)}) %all-to-all-start.4) | async-done | bytes 4194336 | tf_op jit(solution)/shard_map/all_to_all | solution.py:85
  427.4 10.2 %fusion.3 = (bf16[1280,2048]{1,0:T(8,128)(2,1)}, f32[1280]{0:T(1024)S(1)}, bf16[1280,2048]{1,0:T(8,128)(2,1)}) fusion(f32[1280]{0:T(1024)S(1)} %get-tuple-element.259, bf16[640,2048]{1,0:T(8,128)(2,1)} %collective-permute-done.13, bf16[640,2048]{1,0:T(8,128)(2,1)S(1)} %bitcast.174, bf16[1280,1024]{1,0:T(8,128)(2,1)S(1)} %copy-done.85, ...), kind=kOutput, calls=%fused_computation.17 | convolution fusion | flops 5400165376 | bytes 22554624 | tf_op jit(solution)/shard_map/dot_general | solution.py:46
  439.1 5.9 fusion.165
  445.0 9.4 fusion.178
  457.2 10.7 %fusion.177 = f32[1280,1024]{1,0:T(8,128)} fusion(bf16[1280,2048]{1,0:T(8,128)(2,1)S(1)} %fusion, bf16[2048,1024]{1,0:T(8,128)(2,1)} %all-gather.13.cloned.1.call-done), kind=kOutput, calls=%fused_computation.337 | convolution fusion | flops 5368709120 | bytes 14680064 | tf_op jit(solution)/shard_map/dot_general | solution.py:58
  467.9 12.9 %multiply_convert_fusion.2 = (bf16[1280,1024]{1,0:T(8,128)(2,1)}, bf16[1280,1024]{1,0:T(8,128)(2,1)}, bf16[1280,1024]{1,0:T(8,128)(2,1)S(1)}) fusion(f32[1280,1024]{1,0:T(8,128)} %fusion.178, f32[1280,1024]{1,0:T(8,128)} %fusion.177, bf16[1280,2048]{1,0:T(8,128)(2,1)S(1)} %bitcast.154, bf16[2048,1024]{1,0:T(8,128)(2,1)} %all-gather.11.cloned.1.call-done), kind=kOutput, calls=%fused_computation.62 | convolution fusion | flops 5388369920 | bytes 27787264 | tf_op jit(solution)/shard_map/dot_general | solution.py:58
  480.8 10.9 %fusion.179 = f32[1280,2048]{1,0:T(8,128)} fusion(bf16[1280,1024]{1,0:T(8,128)(2,1)} %get-tuple-element.276, bf16[2048,1024]{1,0:T(8,128)(2,1)S(1)} %copy-done.79), kind=kOutput, calls=%fused_computation.339 | convolution fusion | flops 5368709120 | bytes 17301504 | tf_op jit(solution)/shard_map/dot_general | solution.py:46
  491.8 10.0 %convolution_add_fusion = bf16[1280,2048]{1,0:T(8,128)(2,1)S(1)} fusion(f32[1280,2048]{1,0:T(8,128)} %fusion.179, bf16[1280,1024]{1,0:T(8,128)(2,1)S(1)} %get-tuple-element.171, bf16[2048,1024]{1,0:T(8,128)(2,1)} %all-gather.11.cloned.1.call-done), kind=kOutput, calls=%fused_computation.26 | convolution fusion | flops 5373952000 | bytes 22544384 | tf_op jit(solution)/shard_map/dot_general | solution.py:46
  506.7 9.3 fusion.5
  521.9 16.8 %fusion.45 = bf16[2048,1024]{1,0:T(8,128)(2,1)} fusion(bf16[1280,1024]{1,0:T(8,128)(2,1)} %get-tuple-element.275, bf16[1280,1024]{1,0:T(8,128)(2,1)} %get-tuple-element.149, bf16[1280,2048]{1,0:T(8,128)(2,1)} %copy-done.37, bf16[1280,2048]{1,0:T(8,128)(2,1)} %get-tuple-element.151), kind=kOutput, calls=%fused_computation.91 | convolution fusion | flops 10770972672 | bytes 19922944 | tf_op jit(solution)/shard_map/dot_general | solution.py:52
  538.8 7.2 fusion.59
  551.4 12.8 %multiply_convert_fusion = (bf16[1280,1024]{1,0:T(8,128)(2,1)S(1)}, bf16[1280,1024]{1,0:T(8,128)(2,1)S(1)}) fusion(f32[1280,1024]{1,0:T(8,128)} %fusion.89, f32[1280,1024]{1,0:T(8,128)} %get-tuple-element.324, bf16[1280,2048]{1,0:T(8,128)(2,1)} %get-tuple-element.151, bf16[2048,1024]{1,0:T(8,128)(2,1)} %all-gather.13.cloned.1.call-done), kind=kOutput, calls=%fused_computation.60 | convolution fusion | flops 5385748480 | bytes 25165824 | tf_op jit(solution)/shard_map/dot_general | solution.py:58
  564.3 8.3 fusion.180
  572.5 10.1 %add_convert_fusion = bf16[1280,2048]{1,0:T(8,128)(2,1)} fusion(f32[1280,2048]{1,0:T(8,128)} %fusion.180, bf16[1280,1024]{1,0:T(8,128)(2,1)S(1)} %get-tuple-element.170, bf16[2048,1024]{1,0:T(8,128)(2,1)S(1)} %copy-done.81), kind=kOutput, calls=%fused_computation.25 | convolution fusion | flops 5373952000 | bytes 22544384 | tf_op jit(solution)/shard_map/dot_general | solution.py:46
  590.8 16.2 %fusion.42 = bf16[2048,1024]{1,0:T(8,128)(2,1)} fusion(bf16[1280,1024]{1,0:T(8,128)(2,1)} %get-tuple-element.276, bf16[1280,1024]{1,0:T(8,128)(2,1)} %copy-done.84, bf16[1280,2048]{1,0:T(8,128)(2,1)S(1)} %bitcast.156, bf16[640,2048]{1,0:T(8,128)(2,1)} %collective-permute-done.9, bf16[640,2048]{1,0:T(8,128)(2,1)S(1)} %bitcast.168), kind=kOutput, calls=%fused_computation.90 | convolution fusion | flops 10781458432 | bytes 19922944 | tf_op jit(solution)/shard_map/dot_general | solution.py:52
  614.8 7.1 fusion.56
  631.7 7.3 fusion.53
  639.0 6.3 fusion.50
  647.1 30.9 %collective-permute-done.16 = bf16[256,2048]{1,0:T(8,128)(2,1)} collective-permute-done((bf16[256,2048]{1,0:T(8,128)(2,1)}, bf16[256,2048]{1,0:T(8,128)(2,1)}, u32[]{:S(2)}, u32[]{:S(2)}) %collective-permute-start.16) | collective-permute-done | bytes 1048608 | tf_op jit(solution)/shard_map/ppermute | solution.py:62
  703.1 6.4 shard_map.295
  718.2 8.3 convolution_convert_fusion.7
  726.4 8.5 fusion.63
  734.9 13.2 %all-to-all-done.8 = bf16[4,256,2048]{2,1,0:T(8,128)(2,1)} async-done(((bf16[4,256,2048]{2,1,0:T(8,128)(2,1)}), bf16[4,256,2048]{2,1,0:T(8,128)(2,1)}, u32[]{:S(2)}, u32[]{:S(2)}) %all-to-all-start.8) | async-done | bytes 4194336 | tf_op jit(solution)/shard_map/all_to_all | solution.py:85
  755.3 7.5 shard_map.296
  766.3 7.7 shard_map.297
  795.0 7.7 shard_map.298
  802.8 6.0 shard_map.299
  814.8 7.3 add_convert_fusion.1
  826.9 6.5 shard_map.300
  833.4 5.9 convolution_convert_fusion.11
  847.9 11.0 %convolution_convert_fusion = bf16[2048,1536]{1,0:T(8,128)(2,1)} fusion(bf16[1024,1536]{1,0:T(8,128)(2,1)} %shard_map.300, bf16[256,2048]{1,0:T(8,128)(2,1)} %get-tuple-element.315, bf16[256,2048]{1,0:T(8,128)(2,1)} %get-tuple-element.314, bf16[256,2048]{1,0:T(8,128)(2,1)} %get-tuple-element.313, bf16[256,2048]{1,0:T(8,128)(2,1)S(1)} %copy-done.60), kind=kOutput, calls=%fused_computation.29 | convolution fusion | flops 6462373888 | bytes 13631488 | tf_op jit(solution)/shard_map/dot_general | solution.py:52
  859.0 6.3 fusion.98
  865.3 6.1 fusion.96
  892.3 27.9 %collective-permute-done.26 = bf16[256,2048]{1,0:T(8,128)(2,1)} collective-permute-done((bf16[256,2048]{1,0:T(8,128)(2,1)}, bf16[256,2048]{1,0:T(8,128)(2,1)}, u32[]{:S(2)}, u32[]{:S(2)}) %collective-permute-start.26) | collective-permute-done | bytes 1048608 | tf_op jit(solution)/shard_map/ppermute | solution.py:62
  920.3 7.3 collective-permute-done.27
  931.1 6.2 all-to-all-start.11
  950.3 15.0 %collective-permute-done.28 = bf16[1024,512]{1,0:T(8,128)(2,1)} collective-permute-done((bf16[1024,512]{1,0:T(8,128)(2,1)}, bf16[1024,512]{1,0:T(8,128)(2,1)}, u32[]{:S(2)}, u32[]{:S(2)}) %collective-permute-start.28) | collective-permute-done | bytes 1048608 | tf_op jit(solution)/shard_map/ppermute | solution.py:62
  (473 shorter events, 376.1 us)
Async XLA Ops:
  7.2 84.5 %all-gather.7.cloned.1.call-start = ((), (), s32[]{:S(2)}) async-start(), calls=%async_computation.15 | async-start | bytes 9437184 | tf_op jit(solution)/shard_map/all_gather | solution.py:658
  9.6 59.9 %collective-permute-start = (bf16[256,2048]{1,0:T(8,128)(2,1)}, bf16[256,2048]{1,0:T(8,128)(2,1)S(1)}, u32[]{:S(2)}, u32[]{:S(2)}) collective-permute-start(bf16[256,2048]{1,0:T(8,128)(2,1)} %param.21), channel_id=1, source_target_pairs={{0,1},{1,0},{2,3},{3,2},{4,5},{5,4},{6,7},{7,6},{8,9},{9,8},{10,11... | collective-permute-start | bytes 3145736 | tf_op jit(solution)/shard_map/ppermute | solution.py:62
  12.7 51.3 %collective-permute-start.1 = (bf16[256,2048]{1,0:T(8,128)(2,1)}, bf16[256,2048]{1,0:T(8,128)(2,1)S(1)}, u32[]{:S(2)}, u32[]{:S(2)}) collective-permute-start(bf16[256,2048]{1,0:T(8,128)(2,1)} %param.21), channel_id=1, source_target_pairs={{0,2},{2,0},{1,3},{3,1},{4,6},{6,4},{5,7},{7,5},{8,10},{10,8},{9,1... | collective-permute-start | bytes 3145736 | tf_op jit(solution)/shard_map/ppermute | solution.py:62
  24.8 41.6 %all-to-all-start = ((bf16[32,2,1664]{2,1,0:T(2,128)(2,1)}), bf16[32,2,1664]{2,1,0:T(2,128)(2,1)S(1)}, u32[]{:S(2)}, u32[]{:S(2)}) async-start(bf16[32,2,1664]{2,1,0:T(2,128)(2,1)} %reshape.418), calls=%async_computation | async-start | bytes 425984 | tf_op jit(solution)/shard_map/all_to_all | solution.py:99
  27.5 117.3 %all-gather.9.cloned.1.call-start = ((), (), s32[]{:S(2)}) async-start(), calls=%async_computation.16 | async-start | bytes 6291456 | tf_op jit(solution)/shard_map/all_gather | solution.py:412
  64.0 22.1 %collective-permute-start.2 = (bf16[256,2048]{1,0:T(8,128)(2,1)S(1)}, bf16[256,2048]{1,0:T(8,128)(2,1)}, u32[]{:S(2)}, u32[]{:S(2)}) collective-permute-start(bf16[256,2048]{1,0:T(8,128)(2,1)S(1)} %collective-permute-done.1), channel_id=1, source_target_pairs={{0,1},{1,0},{2,3},{3,2},{4,5},{5,4},{6,7},{7,6},{8,9},{9,8},{10,11... | collective-permute-start | bytes 3145736 | tf_op jit(solution)/shard_map/ppermute | solution.py:62
  112.9 8.7 collective-permute-start.4
  116.4 102.5 %all-to-all-start.1 = ((bf16[4,256,2048]{2,1,0:T(8,128)(2,1)}), bf16[4,256,2048]{2,1,0:T(8,128)(2,1)}, u32[]{:S(2)}, u32[]{:S(2)}) async-start(bf16[4,256,2048]{2,1,0:T(8,128)(2,1)} %broadcast_in_dim.68), calls=%async_computation.1 | async-start | bytes 8388608 | tf_op jit(solution)/shard_map/all_to_all | solution.py:85
  144.8 25.1 %collective-permute-start.5 = (bf16[256,2048]{1,0:T(8,128)(2,1)}, bf16[256,2048]{1,0:T(8,128)(2,1)S(1)}, u32[]{:S(2)}, u32[]{:S(2)}) collective-permute-start(bf16[256,2048]{1,0:T(8,128)(2,1)} %convolution_convert_fusion.9), channel_id=1, source_target_pairs={{0,1},{1,0},{2,3},{3,2},{4,5},{5,4},{6,7},{7,6},{8,9},{9,8},{10,11... | collective-permute-start | bytes 3145736 | tf_op jit(solution)/shard_map/ppermute | solution.py:62
  171.2 47.8 %collective-permute-start.7 = (bf16[256,2048]{1,0:T(8,128)(2,1)}, bf16[256,2048]{1,0:T(8,128)(2,1)}, u32[]{:S(2)}, u32[]{:S(2)}) collective-permute-start(bf16[256,2048]{1,0:T(8,128)(2,1)} %add_convert_fusion.3), channel_id=1, source_target_pairs={{0,2},{2,0},{1,3},{3,1},{4,6},{6,4},{5,7},{7,5},{8,10},{10,8},{9,1... | collective-permute-start | bytes 3145736 | tf_op jit(solution)/shard_map/ppermute | solution.py:62
  173.6 46.4 %collective-permute-start.6 = (bf16[256,2048]{1,0:T(8,128)(2,1)}, bf16[256,2048]{1,0:T(8,128)(2,1)}, u32[]{:S(2)}, u32[]{:S(2)}) collective-permute-start(bf16[256,2048]{1,0:T(8,128)(2,1)} %convolution_convert_fusion.8), channel_id=1, source_target_pairs={{0,1},{1,0},{2,3},{3,2},{4,5},{5,4},{6,7},{7,6},{8,9},{9,8},{10,11... | collective-permute-start | bytes 3145736 | tf_op jit(solution)/shard_map/ppermute | solution.py:62
  231.0 52.9 %all-to-all-start.2 = ((bf16[4,256,2048]{2,1,0:T(8,128)(2,1)}), bf16[4,256,2048]{2,1,0:T(8,128)(2,1)}, u32[]{:S(2)}, u32[]{:S(2)}) async-start(bf16[4,256,2048]{2,1,0:T(8,128)(2,1)} %broadcast_in_dim.71), calls=%async_computation.2 | async-start | bytes 8388608 | tf_op jit(solution)/shard_map/all_to_all | solution.py:85
  235.9 82.5 %all-gather.11.cloned.1.call-start = ((), (), s32[]{:S(2)}) async-start(), calls=%async_computation.17 | async-start | bytes 6291456 | tf_op jit(solution)/shard_map/all_gather | solution.py:412
  237.0 46.9 %collective-permute-start.8 = (bf16[256,2048]{1,0:T(8,128)(2,1)}, bf16[256,2048]{1,0:T(8,128)(2,1)}, u32[]{:S(2)}, u32[]{:S(2)}) collective-permute-start(bf16[256,2048]{1,0:T(8,128)(2,1)} %multiply_convert_fusion.6), channel_id=1, source_target_pairs={{0,2},{2,0},{1,3},{3,1},{4,6},{6,4},{5,7},{7,5},{8,10},{10,8},{9,1... | collective-permute-start | bytes 3145736 | tf_op jit(solution)/shard_map/ppermute | solution.py:62
  290.8 12.4 %collective-permute-start.9 = (bf16[640,2048]{1,0:T(8,128)(2,1)}, bf16[640,2048]{1,0:T(8,128)(2,1)}, u32[]{:S(2)}, u32[]{:S(2)}) collective-permute-start(bf16[640,2048]{1,0:T(8,128)(2,1)} %bitcast.17), channel_id=1, source_target_pairs={{0,4},{4,0},{8,12},{12,8},{16,20},{20,16},{24,28},{28,24},{1,5},{5... | collective-permute-start | bytes 7864328 | tf_op jit(solution)/shard_map/ppermute | solution.py:67
  296.3 55.7 %all-to-all-start.3 = ((bf16[4,256,2048]{2,1,0:T(8,128)(2,1)}), bf16[4,256,2048]{2,1,0:T(8,128)(2,1)}, u32[]{:S(2)}, u32[]{:S(2)}) async-start(bf16[4,256,2048]{2,1,0:T(8,128)(2,1)} %broadcast_in_dim.72), calls=%async_computation.3 | async-start | bytes 8388608 | tf_op jit(solution)/shard_map/all_to_all | solution.py:85
  301.2 95.8 %all-gather.13.cloned.1.call-start = ((), (), s32[]{:S(2)}) async-start(), calls=%async_computation.18 | async-start | bytes 6291456 | tf_op jit(solution)/shard_map/all_gather | solution.py:412
  303.2 48.8 %collective-permute-start.10 = (bf16[256,2048]{1,0:T(8,128)(2,1)}, bf16[256,2048]{1,0:T(8,128)(2,1)}, u32[]{:S(2)}, u32[]{:S(2)}) collective-permute-start(bf16[256,2048]{1,0:T(8,128)(2,1)} %param.22), channel_id=1, source_target_pairs={{0,2},{2,0},{1,3},{3,1},{4,6},{6,4},{5,7},{7,5},{8,10},{10,8},{9,1... | collective-permute-start | bytes 3145736 | tf_op jit(solution)/shard_map/ppermute | solution.py:62
  359.0 24.5 %collective-permute-start.11 = (bf16[640,2048]{1,0:T(8,128)(2,1)}, bf16[640,2048]{1,0:T(8,128)(2,1)}, u32[]{:S(2)}, u32[]{:S(2)}) collective-permute-start(bf16[640,2048]{1,0:T(8,128)(2,1)} %bitcast.19), channel_id=1, source_target_pairs={{0,4},{4,0},{8,12},{12,8},{16,20},{20,16},{24,28},{28,24},{1,5},{5... | collective-permute-start | bytes 7864328 | tf_op jit(solution)/shard_map/ppermute | solution.py:67
  364.5 53.4 %all-to-all-start.4 = ((bf16[4,256,2048]{2,1,0:T(8,128)(2,1)}), bf16[4,256,2048]{2,1,0:T(8,128)(2,1)}, u32[]{:S(2)}, u32[]{:S(2)}) async-start(bf16[4,256,2048]{2,1,0:T(8,128)(2,1)} %broadcast_in_dim.74), calls=%async_computation.4 | async-start | bytes 8388608 | tf_op jit(solution)/shard_map/all_to_all | solution.py:85
  379.4 45.7 %collective-permute-start.13 = (bf16[640,2048]{1,0:T(8,128)(2,1)}, bf16[640,2048]{1,0:T(8,128)(2,1)}, u32[]{:S(2)}, u32[]{:S(2)}) collective-permute-start(bf16[640,2048]{1,0:T(8,128)(2,1)} %bitcast.23), channel_id=1, source_target_pairs={{0,4},{4,0},{8,12},{12,8},{16,20},{20,16},{24,28},{28,24},{1,5},{5... | collective-permute-start | bytes 7864328 | tf_op jit(solution)/shard_map/ppermute | solution.py:67
  425.1 29.3 %collective-permute-start.12 = (bf16[640,2048]{1,0:T(8,128)(2,1)}, bf16[640,2048]{1,0:T(8,128)(2,1)}, u32[]{:S(2)}, u32[]{:S(2)}) collective-permute-start(bf16[640,2048]{1,0:T(8,128)(2,1)} %bitcast.21), channel_id=1, source_target_pairs={{0,4},{4,0},{8,12},{12,8},{16,20},{20,16},{24,28},{28,24},{1,5},{5... | collective-permute-start | bytes 7864328 | tf_op jit(solution)/shard_map/ppermute | solution.py:67
  445.0 186.7 %collective-permute-start.17 = (bf16[640,2048]{1,0:T(8,128)(2,1)}, bf16[640,2048]{1,0:T(8,128)(2,1)}, u32[]{:S(2)}, u32[]{:S(2)}) collective-permute-start(bf16[640,2048]{1,0:T(8,128)(2,1)} %get-tuple-element.283), channel_id=1, source_target_pairs={{0,4},{4,0},{8,12},{12,8},{16,20},{20,16},{24,28},{28,24},{1,5},{5... | collective-permute-start | bytes 7864328 | tf_op jit(solution)/shard_map/ppermute | solution.py:67
  504.9 33.8 %collective-permute-start.14 = (bf16[640,2048]{1,0:T(8,128)(2,1)}, bf16[640,2048]{1,0:T(8,128)(2,1)}, u32[]{:S(2)}, u32[]{:S(2)}) collective-permute-start(bf16[640,2048]{1,0:T(8,128)(2,1)} %get-tuple-element.288), channel_id=1, source_target_pairs={{0,4},{4,0},{8,12},{12,8},{16,20},{20,16},{24,28},{28,24},{1,5},{5... | collective-permute-start | bytes 7864328 | tf_op jit(solution)/shard_map/ppermute | solution.py:67
  518.3 20.4 %all-to-all-start.5 = ((f32[16,1,256]{2,1,0:T(1,128)}), f32[16,1,256]{2,1,0:T(1,128)S(1)}, u32[]{:S(2)}, u32[]{:S(2)}) async-start(f32[16,1,256]{2,1,0:T(1,128)} %all_to_all.58), calls=%async_computation.5 | async-start | bytes 32768 | tf_op jit(solution)/shard_map/all_to_all | solution.py:524
  545.9 64.6 %all-to-all-start.6 = ((bf16[4,256,2048]{2,1,0:T(8,128)(2,1)}), bf16[4,256,2048]{2,1,0:T(8,128)(2,1)}, u32[]{:S(2)}, u32[]{:S(2)}) async-start(bf16[4,256,2048]{2,1,0:T(8,128)(2,1)} %fusion.59), calls=%async_computation.6 | async-start | bytes 8388608 | tf_op jit(solution)/shard_map/all_to_all | solution.py:85
  550.8 133.4 %reduce-scatter.4.cloned.1.call-start = ((), (), s32[]{:S(2)}) async-start(), calls=%async_computation.19 | async-start | bytes 6291456 | tf_op jit(solution)/shard_map/reduce_scatter | solution.py:403
  586.3 28.4 %collective-permute-start.15 = (bf16[640,2048]{1,0:T(8,128)(2,1)}, bf16[640,2048]{1,0:T(8,128)(2,1)}, u32[]{:S(2)}, u32[]{:S(2)}) collective-permute-start(bf16[640,2048]{1,0:T(8,128)(2,1)} %slice.231), channel_id=1, source_target_pairs={{0,4},{4,0},{8,12},{12,8},{16,20},{20,16},{24,28},{28,24},{1,5},{5... | collective-permute-start | bytes 7864328 | tf_op jit(solution)/shard_map/ppermute | solution.py:67
  589.9 49.2 %collective-permute-start.18 = (bf16[640,2048]{1,0:T(8,128)(2,1)}, bf16[640,2048]{1,0:T(8,128)(2,1)}, u32[]{:S(2)}, u32[]{:S(2)}) collective-permute-start(bf16[640,2048]{1,0:T(8,128)(2,1)} %get-tuple-element.279), channel_id=1, source_target_pairs={{0,4},{4,0},{8,12},{12,8},{16,20},{20,16},{24,28},{28,24},{1,5},{5... | collective-permute-start | bytes 7864328 | tf_op jit(solution)/shard_map/ppermute | solution.py:67
  621.9 56.1 %all-to-all-start.7 = ((bf16[4,256,2048]{2,1,0:T(8,128)(2,1)}), bf16[4,256,2048]{2,1,0:T(8,128)(2,1)}, u32[]{:S(2)}, u32[]{:S(2)}) async-start(bf16[4,256,2048]{2,1,0:T(8,128)(2,1)} %fusion.56), calls=%async_computation.7 | async-start | bytes 8388608 | tf_op jit(solution)/shard_map/all_to_all | solution.py:85
  626.8 125.6 %reduce-scatter.6.cloned.1.call-start = ((), (), s32[]{:S(2)}) async-start(), calls=%async_computation.20 | async-start | bytes 6291456 | tf_op jit(solution)/shard_map/reduce_scatter | solution.py:403
  629.1 48.8 %collective-permute-start.16 = (bf16[256,2048]{1,0:T(8,128)(2,1)}, bf16[256,2048]{1,0:T(8,128)(2,1)}, u32[]{:S(2)}, u32[]{:S(2)}) collective-permute-start(bf16[256,2048]{1,0:T(8,128)(2,1)} %reduce_sum.268), channel_id=1, source_target_pairs={{0,2},{2,0},{1,3},{3,1},{4,6},{6,4},{5,7},{7,5},{8,10},{10,8},{9,1... | collective-permute-start | bytes 3145736 | tf_op jit(solution)/shard_map/ppermute | solution.py:62
  691.6 61.1 %collective-permute-start.19 = (bf16[256,2048]{1,0:T(8,128)(2,1)}, bf16[256,2048]{1,0:T(8,128)(2,1)}, u32[]{:S(2)}, u32[]{:S(2)}) collective-permute-start(bf16[256,2048]{1,0:T(8,128)(2,1)} %get-tuple-element.261), channel_id=1, source_target_pairs={{0,1},{1,0},{2,3},{3,2},{4,5},{5,4},{6,7},{7,6},{8,9},{9,8},{10,11... | collective-permute-start | bytes 3145736 | tf_op jit(solution)/shard_map/ppermute | solution.py:62
  691.9 60.5 %collective-permute-start.20 = (bf16[256,2048]{1,0:T(8,128)(2,1)}, bf16[256,2048]{1,0:T(8,128)(2,1)}, u32[]{:S(2)}, u32[]{:S(2)}) collective-permute-start(bf16[256,2048]{1,0:T(8,128)(2,1)} %get-tuple-element.261), channel_id=1, source_target_pairs={{0,2},{2,0},{1,3},{3,1},{4,6},{6,4},{5,7},{7,5},{8,10},{10,8},{9,1... | collective-permute-start | bytes 3145736 | tf_op jit(solution)/shard_map/ppermute | solution.py:62
  695.3 52.8 %all-to-all-start.8 = ((bf16[4,256,2048]{2,1,0:T(8,128)(2,1)}), bf16[4,256,2048]{2,1,0:T(8,128)(2,1)}, u32[]{:S(2)}, u32[]{:S(2)}) async-start(bf16[4,256,2048]{2,1,0:T(8,128)(2,1)} %fusion.50), calls=%async_computation.9 | async-start | bytes 8388608 | tf_op jit(solution)/shard_map/all_to_all | solution.py:85
  752.4 24.4 %collective-permute-start.21 = (bf16[256,2048]{1,0:T(8,128)(2,1)}, bf16[256,2048]{1,0:T(8,128)(2,1)S(1)}, u32[]{:S(2)}, u32[]{:S(2)}) collective-permute-start(bf16[256,2048]{1,0:T(8,128)(2,1)} %collective-permute-done.20), channel_id=1, source_target_pairs={{0,1},{1,0},{2,3},{3,2},{4,5},{5,4},{6,7},{7,6},{8,9},{9,8},{10,11... | collective-permute-start | bytes 3145736 | tf_op jit(solution)/shard_map/ppermute | solution.py:62
  777.8 31.1 %collective-permute-start.22 = (bf16[1024,512]{1,0:T(8,128)(2,1)}, bf16[1024,512]{1,0:T(8,128)(2,1)}, u32[]{:S(2)}, u32[]{:S(2)}) collective-permute-start(bf16[1024,512]{1,0:T(8,128)(2,1)} %get-tuple-element.193), channel_id=1, source_target_pairs={{0,1},{1,0},{2,3},{3,2},{4,5},{5,4},{6,7},{7,6},{8,9},{9,8},{10,11... | collective-permute-start | bytes 3145736 | tf_op jit(solution)/shard_map/ppermute | solution.py:62
  779.5 59.7 %all-to-all-start.9 = ((bf16[4,256,2048]{2,1,0:T(8,128)(2,1)}), bf16[4,256,2048]{2,1,0:T(8,128)(2,1)}, u32[]{:S(2)}, u32[]{:S(2)}) async-start(bf16[4,256,2048]{2,1,0:T(8,128)(2,1)} %fusion.53), calls=%async_computation.11 | async-start | bytes 8388608 | tf_op jit(solution)/shard_map/all_to_all | solution.py:85
  784.6 100.8 %all-gather.15.cloned.1.call-start = ((), (), s32[]{:S(2)}) async-start(), calls=%async_computation.22 | async-start | bytes 3145728 | tf_op jit(solution)/shard_map/all_gather | solution.py:789
  808.9 5.1 collective-permute-start.23
  814.7 10.2 %collective-permute-start.24 = (f32[2,4,256]{2,0,1:T(2,128)S(1)}, f32[2,4,256]{2,0,1:T(2,128)S(1)}, u32[]{:S(2)}, u32[]{:S(2)}) collective-permute-start(f32[2,4,256]{2,0,1:T(2,128)S(1)} %bitcast_add_fusion), channel_id=1, source_target_pairs={{0,2},{2,0},{1,3},{3,1},{4,6},{6,4},{5,7},{7,5},{8,10},{10,8},{9,1... | collective-permute-start | bytes 24584 | tf_op jit(solution)/shard_map/ppermute | solution.py:62
  842.5 31.6 %collective-permute-start.25 = (bf16[256,2048]{1,0:T(8,128)(2,1)}, bf16[256,2048]{1,0:T(8,128)(2,1)}, u32[]{:S(2)}, u32[]{:S(2)}) collective-permute-start(bf16[256,2048]{1,0:T(8,128)(2,1)} %convolution_convert_fusion.11), channel_id=1, source_target_pairs={{0,1},{1,0},{2,3},{3,2},{4,5},{5,4},{6,7},{7,6},{8,9},{9,8},{10,11... | collective-permute-start | bytes 3145736 | tf_op jit(solution)/shard_map/ppermute | solution.py:62
  843.3 31.0 %all-to-all-start.10 = ((bf16[8,256,512]{2,1,0:T(8,128)(2,1)}), bf16[8,256,512]{2,1,0:T(8,128)(2,1)}, u32[]{:S(2)}, u32[]{:S(2)}) async-start(bf16[8,256,512]{2,1,0:T(8,128)(2,1)} %bitcast.162), calls=%async_computation.12 | async-start | bytes 4194304 | tf_op jit(solution)/shard_map/all_to_all | solution.py:833
  847.6 123.2 %reduce-scatter.8.cloned.1.call-start = ((), (), s32[]{:S(2)}) async-start(), calls=%async_computation.21 | async-start | bytes 7077888 | tf_op jit(solution)/shard_map/reduce_scatter | solution.py:846
  874.3 45.9 %collective-permute-start.26 = (bf16[256,2048]{1,0:T(8,128)(2,1)}, bf16[256,2048]{1,0:T(8,128)(2,1)}, u32[]{:S(2)}, u32[]{:S(2)}) collective-permute-start(bf16[256,2048]{1,0:T(8,128)(2,1)} %convolution_convert_fusion.10), channel_id=1, source_target_pairs={{0,1},{1,0},{2,3},{3,2},{4,5},{5,4},{6,7},{7,6},{8,9},{9,8},{10,11... | collective-permute-start | bytes 3145736 | tf_op jit(solution)/shard_map/ppermute | solution.py:62
  878.8 48.8 %collective-permute-start.27 = (bf16[256,2048]{1,0:T(8,128)(2,1)}, bf16[256,2048]{1,0:T(8,128)(2,1)}, u32[]{:S(2)}, u32[]{:S(2)}) collective-permute-start(bf16[256,2048]{1,0:T(8,128)(2,1)} %add_convert_fusion.2), channel_id=1, source_target_pairs={{0,2},{2,0},{1,3},{3,1},{4,6},{6,4},{5,7},{7,5},{8,10},{10,8},{9,1... | collective-permute-start | bytes 3145736 | tf_op jit(solution)/shard_map/ppermute | solution.py:62
  931.1 17.8 %all-to-all-start.11 = ((f32[32,1,1280]{2,1,0:T(1,128)}), f32[32,1,1280]{2,1,0:T(1,128)S(1)}, u32[]{:S(2)}, u32[]{:S(2)}) async-start(f32[32,1,1280]{2,1,0:T(1,128)} %copy.49), calls=%async_computation.14 | async-start | bytes 327680 | tf_op jit(solution)/shard_map/all_to_all | solution.py:99
  937.3 28.1 %collective-permute-start.28 = (bf16[1024,512]{1,0:T(8,128)(2,1)}, bf16[1024,512]{1,0:T(8,128)(2,1)}, u32[]{:S(2)}, u32[]{:S(2)}) collective-permute-start(bf16[1024,512]{1,0:T(8,128)(2,1)} %get-tuple-element.217), channel_id=1, source_target_pairs={{0,1},{1,0},{2,3},{3,2},{4,5},{5,4},{6,7},{7,6},{8,9},{9,8},{10,11... | collective-permute-start | bytes 3145736 | tf_op jit(solution)/shard_map/ppermute | solution.py:62
  (98 other events, 1191.7 us)
Sparse Core Ops, SparseCore 0:
  10.5 59.1 all-gather.6
  87.7 57.0 all-gather.8
  238.2 80.1 all-gather.10
  319.8 77.1 all-gather.12
  553.6 55.8 reduce-scatter.3
  629.7 111.1 reduce-scatter.5
  788.8 55.4 all-gather.14
  874.4 63.0 reduce-scatter.7

commit v5 on v4

--- a/solution.py
+++ b/solution.py
@@ -499,13 +499,14 @@
     down_weight = whole_weight(w_down)
     weights = (gate_weight, up_weight, down_weight)
     near_kept = expert_hidden(near_rows, weights)
-    near_hidden, far_chunk, cot_across = sync(near_kept[2], gather_chips(across), cot_across)
+    near_hidden, far_chunk = sync(near_kept[2], gather_chips(across))
     near_kept = near_kept[:2] + (near_hidden,)
-    cot_far = gather_chips(cot_across)
     far_rows = pick_rows(*picks[1][:2], far_chunk)
-    far_rows, down_weight = sync(far_rows, down_weight)
+    far_rows, cot_across = sync(far_rows, cot_across)
+    far_kept = expert_hidden(far_rows, weights)
+    far_hidden, cot_far, down_weight = sync(far_kept[2], gather_chips(cot_across), down_weight)
+    far_kept = far_kept[:2] + (far_hidden,)
     weights = (gate_weight, up_weight, down_weight)
-    far_kept = expert_hidden(far_rows, weights)
     near_cot, far_cot = pick_rows(*picks[0][:2], cot_near), pick_rows(*picks[1][:2], cot_far)
     gate = arrive(0, near_rows)
     produced = expert_produce(near_hidden, weights)

time: 985 us -> 1010 us (1.025)
  waiting for transfers between devices: 299 us -> 333 us
    all_to_all x8, waiting for transfers between devices: 29.8 us -> 52.5 us  [over_chips(): lax.all_to_all(blocks, 'shard', split_axis=0, concat_axis=0, axis_index_g...]
    ppermute x21, waiting for transfers between devices: 246 us -> 262 us  [swap(): return lax.ppermute(values, axis, SWAP)]
    unnamed x206 -> x208, local copies, waits for them, and re-layouts: 28.5 us -> 28.7 us
  transfers between devices with their start and end apart: 49 -> 49, of which waited for: 20 -> 20; matrix products, arithmetic and copies ran while one was open for 49% -> 46% of each run, Pallas kernels for 7% -> 6%
where the time goes in v5:
time: 1010 us
  waiting for transfers between devices  333 us (33%)
  matrix products  319 us (32%)
  local copies, waits for them, and re-layouts  96.8 us (10%)
  other arithmetic  90.2 us (9%)
  starting transfers between devices  86.8 us (9%)
  Pallas kernels  64 us (6%)
  between operations  16 us (2%)
    ppermute x21, waiting for transfers between devices, swap(): return lax.ppermute(values, axis, SWAP)  262 us
    dot_general x23, matrix products, plain(): return jnp.dot(left, right, preferred_element_type=jnp.float32)  101 us
    dot_general x15, matrix products, contract_last(): lax.dot_general(left, right, (((1,), (1,)), ((), ())), preferred_element_...  93.3 us
    dot_general x10, matrix products, contract_first(): lax.dot_general(left, right, (((0,), (0,)), ((), ())), preferred_element_...  80.9 us
    all_to_all x8, waiting for transfers between devices, over_chips(): lax.all_to_all(blocks, 'shard', split_axis=0, concat_axis=0, axis_index_g...  52.5 us
    all_to_all x8, starting transfers between devices, over_chips(): lax.all_to_all(blocks, 'shard', split_axis=0, concat_axis=0, axis_index_g...  40 us
    pallas_call x4, Pallas kernels, attend_block_back(): pl.pallas_call(lambda *refs: attend_back_kernel(which, sums is None, *ref...  29.3 us
    unnamed x208, local copies, waits for them, and re-layouts  28.7 us
  transfers between devices with their start and end apart: 49, of which 20 were waited for; matrix products, arithmetic and copies ran while one was open for 46% of the time, Pallas kernels for 6%

profile of v5, /device:TPU:0, one launch (start us, length us, event | category | flops | bytes accessed | tf_op | source)
XLA Modules:
  0.0 1005.1 jit_solution(13581139350371063813)
XLA Ops:
  32.3 31.7 %collective-permute-done.1 = bf16[256,2048]{1,0:T(8,128)(2,1)S(1)} collective-permute-done((bf16[256,2048]{1,0:T(8,128)(2,1)}, bf16[256,2048]{1,0:T(8,128)(2,1)S(1)}, u32[]{:S(2)}, u32[]{:S(2)}) %collective-permute-start.1) | collective-permute-done | bytes 1048608 | tf_op jit(solution)/shard_map/ppermute | solution.py:62
  69.8 16.3 %collective-permute-done.2 = bf16[256,2048]{1,0:T(8,128)(2,1)} collective-permute-done((bf16[256,2048]{1,0:T(8,128)(2,1)S(1)}, bf16[256,2048]{1,0:T(8,128)(2,1)}, u32[]{:S(2)}, u32[]{:S(2)}) %collective-permute-start.2) | collective-permute-done | bytes 1048608 | tf_op jit(solution)/shard_map/ppermute | solution.py:62
  137.0 7.8 all-gather.9.cloned.1.call-done
  159.8 10.1 %collective-permute-done.5 = bf16[256,2048]{1,0:T(8,128)(2,1)S(1)} collective-permute-done((bf16[256,2048]{1,0:T(8,128)(2,1)}, bf16[256,2048]{1,0:T(8,128)(2,1)S(1)}, u32[]{:S(2)}, u32[]{:S(2)}) %collective-permute-start.5) | collective-permute-done | bytes 1048608 | tf_op jit(solution)/shard_map/ppermute | solution.py:62
  183.3 35.7 %collective-permute-done.7 = bf16[256,2048]{1,0:T(8,128)(2,1)} collective-permute-done((bf16[256,2048]{1,0:T(8,128)(2,1)}, bf16[256,2048]{1,0:T(8,128)(2,1)}, u32[]{:S(2)}, u32[]{:S(2)}) %collective-permute-start.7) | collective-permute-done | bytes 1048608 | tf_op jit(solution)/shard_map/ppermute | solution.py:62
  239.7 44.2 %collective-permute-done.8 = bf16[256,2048]{1,0:T(8,128)(2,1)} collective-permute-done((bf16[256,2048]{1,0:T(8,128)(2,1)}, bf16[256,2048]{1,0:T(8,128)(2,1)}, u32[]{:S(2)}, u32[]{:S(2)}) %collective-permute-start.8) | collective-permute-done | bytes 1048608 | tf_op jit(solution)/shard_map/ppermute | solution.py:62
  302.3 10.5 %fusion.89 = f32[1280,1024]{1,0:T(8,128)} fusion(bf16[2048,1024]{1,0:T(8,128)(2,1)} %all-gather.9.cloned.1.call-done, bf16[640,2048]{1,0:T(8,128)(2,1)} %collective-permute-done.9, bf16[640,2048]{1,0:T(8,128)(2,1)} %bitcast.161), kind=kOutput, calls=%fused_computation.150 | convolution fusion | flops 5379194880 | bytes 14680064 | tf_op jit(solution)/shard_map/dot_general | solution.py:58
  312.8 7.0 all-gather.11.cloned.1.call-done
  319.9 14.5 %multiply_convert_fusion.5 = (bf16[1280,1024]{1,0:T(8,128)(2,1)}, f32[1280,1024]{1,0:T(8,128)}) fusion(f32[1280,1024]{1,0:T(8,128)} %fusion.89, bf16[2048,1024]{1,0:T(8,128)(2,1)} %all-gather.11.cloned.1.call-done, bf16[640,2048]{1,0:T(8,128)(2,1)} %collective-permute-done.9, bf16[640,2048]{1,0:T(8,128)(2,1)} %bitcast.162), kind=kOutput, calls=%fused_computation.67 | convolution fusion | flops 5387059200 | bytes 22544384 | tf_op jit(solution)/shard_map/dot_general | solution.py:58
  334.3 15.1 %all-to-all-done.3 = bf16[4,256,2048]{2,1,0:T(8,128)(2,1)} async-done(((bf16[4,256,2048]{2,1,0:T(8,128)(2,1)}), bf16[4,256,2048]{2,1,0:T(8,128)(2,1)}, u32[]{:S(2)}, u32[]{:S(2)}) %all-to-all-start.3) | async-done | bytes 4194336 | tf_op jit(solution)/shard_map/all_to_all | solution.py:85
  374.7 35.8 %collective-permute-done.11 = bf16[256,2048]{1,0:T(8,128)(2,1)} collective-permute-done((bf16[256,2048]{1,0:T(8,128)(2,1)}, bf16[256,2048]{1,0:T(8,128)(2,1)}, u32[]{:S(2)}, u32[]{:S(2)}) %collective-permute-start.11) | collective-permute-done | bytes 1048608 | tf_op jit(solution)/shard_map/ppermute | solution.py:62
  423.8 8.8 fusion.177
  434.9 8.1 multiply_convert_fusion.4
  443.0 24.3 %all-to-all-done.4 = bf16[4,256,2048]{2,1,0:T(8,128)(2,1)} async-done(((bf16[4,256,2048]{2,1,0:T(8,128)(2,1)}), bf16[4,256,2048]{2,1,0:T(8,128)(2,1)}, u32[]{:S(2)}, u32[]{:S(2)}) %all-to-all-start.4) | async-done | bytes 4194336 | tf_op jit(solution)/shard_map/all_to_all | solution.py:85
  479.6 10.4 %fusion.3 = (bf16[1280,2048]{1,0:T(8,128)(2,1)}, f32[1280]{0:T(1024)S(1)}, bf16[1280,2048]{1,0:T(8,128)(2,1)}) fusion(f32[1280]{0:T(1024)S(1)} %get-tuple-element.263, bf16[640,2048]{1,0:T(8,128)(2,1)} %collective-permute-done.13, bf16[640,2048]{1,0:T(8,128)(2,1)S(1)} %bitcast.169, bf16[1280,1024]{1,0:T(8,128)(2,1)S(1)} %copy-done.88, ...), kind=kOutput, calls=%fused_computation.17 | convolution fusion | flops 5400165376 | bytes 22554624 | tf_op jit(solution)/shard_map/dot_general | solution.py:46
  491.5 6.1 fusion.165
  498.5 10.2 %fusion.5 = (bf16[1280,2048]{1,0:T(8,128)(2,1)}, f32[1280]{0:T(1024)S(1)}, bf16[1280,2048]{1,0:T(8,128)(2,1)}) fusion(f32[1280]{0:T(1024)S(1)} %get-tuple-element.264, bf16[640,2048]{1,0:T(8,128)(2,1)} %collective-permute-done.12, bf16[640,2048]{1,0:T(8,128)(2,1)S(1)} %bitcast.170, bf16[1280,1024]{1,0:T(8,128)(2,1)S(1)} %copy-done.89, ...), kind=kOutput, calls=%fused_computation.19 | convolution fusion | flops 5400165376 | bytes 22554624 | tf_op jit(solution)/shard_map/dot_general | solution.py:46
  508.7 11.8 %multiply_convert_fusion.2 = (bf16[1280,1024]{1,0:T(8,128)(2,1)S(1)}, bf16[1280,1024]{1,0:T(8,128)(2,1)S(1)}) fusion(f32[1280,1024]{1,0:T(8,128)} %copy-done.85, f32[1280,1024]{1,0:T(8,128)} %get-tuple-element.330, bf16[1280,2048]{1,0:T(8,128)(2,1)} %get-tuple-element.154, bf16[2048,1024]{1,0:T(8,128)(2,1)S(1)} %copy-done.84), kind=kOutput, calls=%fused_computation.62 | convolution fusion | flops 5385748480 | bytes 25165824 | tf_op jit(solution)/shard_map/dot_general | solution.py:58
  520.6 8.5 fusion.178
  529.1 8.5 convolution_add_fusion
  546.4 16.8 %fusion.45 = bf16[2048,1024]{1,0:T(8,128)(2,1)} fusion(bf16[1280,1024]{1,0:T(8,128)(2,1)} %get-tuple-element.153, bf16[1280,1024]{1,0:T(8,128)(2,1)} %get-tuple-element.152, bf16[1280,2048]{1,0:T(8,128)(2,1)} %get-tuple-element.154, bf16[1280,2048]{1,0:T(8,128)(2,1)} %get-tuple-element.155), kind=kOutput, calls=%fused_computation.91 | convolution fusion | flops 10770972672 | bytes 19922944 | tf_op jit(solution)/shard_map/dot_general | solution.py:52
  563.2 7.2 fusion.59
  575.8 13.2 %multiply_convert_fusion = (bf16[1280,1024]{1,0:T(8,128)(2,1)S(1)}, bf16[1280,1024]{1,0:T(8,128)(2,1)S(1)}) fusion(f32[1280,1024]{1,0:T(8,128)} %fusion.89, f32[1280,1024]{1,0:T(8,128)} %get-tuple-element.328, bf16[1280,2048]{1,0:T(8,128)(2,1)} %get-tuple-element.155, bf16[2048,1024]{1,0:T(8,128)(2,1)} %all-gather.13.cloned.1.call-done), kind=kOutput, calls=%fused_computation.60 | convolution fusion | flops 5385748480 | bytes 25165824 | tf_op jit(solution)/shard_map/dot_general | solution.py:58
  589.1 8.3 fusion.179
  597.3 10.1 %add_convert_fusion = bf16[1280,2048]{1,0:T(8,128)(2,1)} fusion(f32[1280,2048]{1,0:T(8,128)} %fusion.179, bf16[1280,1024]{1,0:T(8,128)(2,1)S(1)} %get-tuple-element.174, bf16[2048,1024]{1,0:T(8,128)(2,1)S(1)} %copy-done.82), kind=kOutput, calls=%fused_computation.25 | convolution fusion | flops 5373952000 | bytes 22544384 | tf_op jit(solution)/shard_map/dot_general | solution.py:46
  615.4 16.1 %fusion.42 = bf16[2048,1024]{1,0:T(8,128)(2,1)} fusion(bf16[1280,1024]{1,0:T(8,128)(2,1)} %copy-done.86, bf16[1280,1024]{1,0:T(8,128)(2,1)} %copy-done.87, bf16[1280,2048]{1,0:T(8,128)(2,1)S(1)} %bitcast.154, bf16[640,2048]{1,0:T(8,128)(2,1)} %collective-permute-done.9, bf16[640,2048]{1,0:T(8,128)(2,1)S(1)} %bitcast.164), kind=kOutput, calls=%fused_computation.90 | convolution fusion | flops 10781458432 | bytes 19922944 | tf_op jit(solution)/shard_map/dot_general | solution.py:52
  639.4 7.1 fusion.56
  656.4 7.3 fusion.53
  663.7 6.3 fusion.50
  671.7 30.9 %collective-permute-done.16 = bf16[256,2048]{1,0:T(8,128)(2,1)} collective-permute-done((bf16[256,2048]{1,0:T(8,128)(2,1)}, bf16[256,2048]{1,0:T(8,128)(2,1)}, u32[]{:S(2)}, u32[]{:S(2)}) %collective-permute-start.16) | collective-permute-done | bytes 1048608 | tf_op jit(solution)/shard_map/ppermute | solution.py:62
  728.3 6.4 shard_map.295
  743.3 8.3 convolution_convert_fusion.7
  751.6 8.5 fusion.63
  760.1 13.1 %all-to-all-done.8 = bf16[4,256,2048]{2,1,0:T(8,128)(2,1)} async-done(((bf16[4,256,2048]{2,1,0:T(8,128)(2,1)}), bf16[4,256,2048]{2,1,0:T(8,128)(2,1)}, u32[]{:S(2)}, u32[]{:S(2)}) %all-to-all-start.8) | async-done | bytes 4194336 | tf_op jit(solution)/shard_map/all_to_all | solution.py:85
  780.4 7.5 shard_map.296
  791.3 7.7 shard_map.297
  819.9 7.7 shard_map.298
  827.7 6.0 shard_map.299
  839.8 7.3 add_convert_fusion.1
  851.9 6.5 shard_map.300
  858.4 5.9 convolution_convert_fusion.11
  872.3 11.0 %convolution_convert_fusion = bf16[2048,1536]{1,0:T(8,128)(2,1)} fusion(bf16[1024,1536]{1,0:T(8,128)(2,1)} %shard_map.300, bf16[256,2048]{1,0:T(8,128)(2,1)} %get-tuple-element.319, bf16[256,2048]{1,0:T(8,128)(2,1)} %get-tuple-element.318, bf16[256,2048]{1,0:T(8,128)(2,1)} %get-tuple-element.317, bf16[256,2048]{1,0:T(8,128)(2,1)S(1)} %copy-done.59), kind=kOutput, calls=%fused_computation.29 | convolution fusion | flops 6462373888 | bytes 13631488 | tf_op jit(solution)/shard_map/dot_general | solution.py:52
  883.3 6.3 fusion.98
  889.6 6.1 fusion.96
  917.2 27.5 %collective-permute-done.26 = bf16[256,2048]{1,0:T(8,128)(2,1)} collective-permute-done((bf16[256,2048]{1,0:T(8,128)(2,1)}, bf16[256,2048]{1,0:T(8,128)(2,1)}, u32[]{:S(2)}, u32[]{:S(2)}) %collective-permute-start.26) | collective-permute-done | bytes 1048608 | tf_op jit(solution)/shard_map/ppermute | solution.py:62
  944.8 7.8 collective-permute-done.27
  956.1 6.0 all-to-all-start.11
  975.2 15.0 %collective-permute-done.28 = bf16[1024,512]{1,0:T(8,128)(2,1)} collective-permute-done((bf16[1024,512]{1,0:T(8,128)(2,1)}, bf16[1024,512]{1,0:T(8,128)(2,1)}, u32[]{:S(2)}, u32[]{:S(2)}) %collective-permute-start.28) | collective-permute-done | bytes 1048608 | tf_op jit(solution)/shard_map/ppermute | solution.py:62
  (473 shorter events, 375.9 us)
Async XLA Ops:
  7.2 84.5 %all-gather.7.cloned.1.call-start = ((), (), s32[]{:S(2)}) async-start(), calls=%async_computation.15 | async-start | bytes 9437184 | tf_op jit(solution)/shard_map/all_gather | solution.py:659
  9.6 59.9 %collective-permute-start = (bf16[256,2048]{1,0:T(8,128)(2,1)}, bf16[256,2048]{1,0:T(8,128)(2,1)S(1)}, u32[]{:S(2)}, u32[]{:S(2)}) collective-permute-start(bf16[256,2048]{1,0:T(8,128)(2,1)} %param.21), channel_id=1, source_target_pairs={{0,1},{1,0},{2,3},{3,2},{4,5},{5,4},{6,7},{7,6},{8,9},{9,8},{10,11... | collective-permute-start | bytes 3145736 | tf_op jit(solution)/shard_map/ppermute | solution.py:62
  12.7 51.3 %collective-permute-start.1 = (bf16[256,2048]{1,0:T(8,128)(2,1)}, bf16[256,2048]{1,0:T(8,128)(2,1)S(1)}, u32[]{:S(2)}, u32[]{:S(2)}) collective-permute-start(bf16[256,2048]{1,0:T(8,128)(2,1)} %param.21), channel_id=1, source_target_pairs={{0,2},{2,0},{1,3},{3,1},{4,6},{6,4},{5,7},{7,5},{8,10},{10,8},{9,1... | collective-permute-start | bytes 3145736 | tf_op jit(solution)/shard_map/ppermute | solution.py:62
  24.8 41.6 %all-to-all-start = ((bf16[32,2,1664]{2,1,0:T(2,128)(2,1)}), bf16[32,2,1664]{2,1,0:T(2,128)(2,1)S(1)}, u32[]{:S(2)}, u32[]{:S(2)}) async-start(bf16[32,2,1664]{2,1,0:T(2,128)(2,1)} %reshape.418), calls=%async_computation | async-start | bytes 425984 | tf_op jit(solution)/shard_map/all_to_all | solution.py:99
  27.5 117.3 %all-gather.9.cloned.1.call-start = ((), (), s32[]{:S(2)}) async-start(), calls=%async_computation.16 | async-start | bytes 6291456 | tf_op jit(solution)/shard_map/all_gather | solution.py:412
  64.0 22.1 %collective-permute-start.2 = (bf16[256,2048]{1,0:T(8,128)(2,1)S(1)}, bf16[256,2048]{1,0:T(8,128)(2,1)}, u32[]{:S(2)}, u32[]{:S(2)}) collective-permute-start(bf16[256,2048]{1,0:T(8,128)(2,1)S(1)} %collective-permute-done.1), channel_id=1, source_target_pairs={{0,1},{1,0},{2,3},{3,2},{4,5},{5,4},{6,7},{7,6},{8,9},{9,8},{10,11... | collective-permute-start | bytes 3145736 | tf_op jit(solution)/shard_map/ppermute | solution.py:62
  112.9 8.6 collective-permute-start.4
  116.4 102.6 %all-to-all-start.1 = ((bf16[4,256,2048]{2,1,0:T(8,128)(2,1)}), bf16[4,256,2048]{2,1,0:T(8,128)(2,1)}, u32[]{:S(2)}, u32[]{:S(2)}) async-start(bf16[4,256,2048]{2,1,0:T(8,128)(2,1)} %broadcast_in_dim.68), calls=%async_computation.1 | async-start | bytes 8388608 | tf_op jit(solution)/shard_map/all_to_all | solution.py:85
  144.8 25.1 %collective-permute-start.5 = (bf16[256,2048]{1,0:T(8,128)(2,1)}, bf16[256,2048]{1,0:T(8,128)(2,1)S(1)}, u32[]{:S(2)}, u32[]{:S(2)}) collective-permute-start(bf16[256,2048]{1,0:T(8,128)(2,1)} %convolution_convert_fusion.9), channel_id=1, source_target_pairs={{0,1},{1,0},{2,3},{3,2},{4,5},{5,4},{6,7},{7,6},{8,9},{9,8},{10,11... | collective-permute-start | bytes 3145736 | tf_op jit(solution)/shard_map/ppermute | solution.py:62
  171.2 47.8 %collective-permute-start.7 = (bf16[256,2048]{1,0:T(8,128)(2,1)}, bf16[256,2048]{1,0:T(8,128)(2,1)}, u32[]{:S(2)}, u32[]{:S(2)}) collective-permute-start(bf16[256,2048]{1,0:T(8,128)(2,1)} %add_convert_fusion.3), channel_id=1, source_target_pairs={{0,2},{2,0},{1,3},{3,1},{4,6},{6,4},{5,7},{7,5},{8,10},{10,8},{9,1... | collective-permute-start | bytes 3145736 | tf_op jit(solution)/shard_map/ppermute | solution.py:62
  173.6 46.4 %collective-permute-start.6 = (bf16[256,2048]{1,0:T(8,128)(2,1)}, bf16[256,2048]{1,0:T(8,128)(2,1)}, u32[]{:S(2)}, u32[]{:S(2)}) collective-permute-start(bf16[256,2048]{1,0:T(8,128)(2,1)} %convolution_convert_fusion.8), channel_id=1, source_target_pairs={{0,1},{1,0},{2,3},{3,2},{4,5},{5,4},{6,7},{7,6},{8,9},{9,8},{10,11... | collective-permute-start | bytes 3145736 | tf_op jit(solution)/shard_map/ppermute | solution.py:62
  230.9 52.9 %all-to-all-start.2 = ((bf16[4,256,2048]{2,1,0:T(8,128)(2,1)}), bf16[4,256,2048]{2,1,0:T(8,128)(2,1)}, u32[]{:S(2)}, u32[]{:S(2)}) async-start(bf16[4,256,2048]{2,1,0:T(8,128)(2,1)} %broadcast_in_dim.71), calls=%async_computation.2 | async-start | bytes 8388608 | tf_op jit(solution)/shard_map/all_to_all | solution.py:85
  235.8 84.1 %all-gather.11.cloned.1.call-start = ((), (), s32[]{:S(2)}) async-start(), calls=%async_computation.17 | async-start | bytes 6291456 | tf_op jit(solution)/shard_map/all_gather | solution.py:412
  236.9 46.9 %collective-permute-start.8 = (bf16[256,2048]{1,0:T(8,128)(2,1)}, bf16[256,2048]{1,0:T(8,128)(2,1)}, u32[]{:S(2)}, u32[]{:S(2)}) collective-permute-start(bf16[256,2048]{1,0:T(8,128)(2,1)} %multiply_convert_fusion.6), channel_id=1, source_target_pairs={{0,2},{2,0},{1,3},{3,1},{4,6},{6,4},{5,7},{7,5},{8,10},{10,8},{9,1... | collective-permute-start | bytes 3145736 | tf_op jit(solution)/shard_map/ppermute | solution.py:62
  290.8 11.6 %collective-permute-start.9 = (bf16[640,2048]{1,0:T(8,128)(2,1)}, bf16[640,2048]{1,0:T(8,128)(2,1)}, u32[]{:S(2)}, u32[]{:S(2)}) collective-permute-start(bf16[640,2048]{1,0:T(8,128)(2,1)} %bitcast.17), channel_id=1, source_target_pairs={{0,4},{4,0},{8,12},{12,8},{16,20},{20,16},{24,28},{28,24},{1,5},{5... | collective-permute-start | bytes 7864328 | tf_op jit(solution)/shard_map/ppermute | solution.py:67
  296.2 53.2 %all-to-all-start.3 = ((bf16[4,256,2048]{2,1,0:T(8,128)(2,1)}), bf16[4,256,2048]{2,1,0:T(8,128)(2,1)}, u32[]{:S(2)}, u32[]{:S(2)}) async-start(bf16[4,256,2048]{2,1,0:T(8,128)(2,1)} %broadcast_in_dim.72), calls=%async_computation.3 | async-start | bytes 8388608 | tf_op jit(solution)/shard_map/all_to_all | solution.py:85
  301.1 141.9 %all-gather.13.cloned.1.call-start = ((), (), s32[]{:S(2)}) async-start(), calls=%async_computation.18 | async-start | bytes 6291456 | tf_op jit(solution)/shard_map/all_gather | solution.py:412
  356.4 13.0 %collective-permute-start.10 = (bf16[640,2048]{1,0:T(8,128)(2,1)}, bf16[640,2048]{1,0:T(8,128)(2,1)}, u32[]{:S(2)}, u32[]{:S(2)}) collective-permute-start(bf16[640,2048]{1,0:T(8,128)(2,1)} %bitcast.19), channel_id=1, source_target_pairs={{0,4},{4,0},{8,12},{12,8},{16,20},{20,16},{24,28},{28,24},{1,5},{5... | collective-permute-start | bytes 7864328 | tf_op jit(solution)/shard_map/ppermute | solution.py:67
  361.7 48.8 %collective-permute-start.11 = (bf16[256,2048]{1,0:T(8,128)(2,1)}, bf16[256,2048]{1,0:T(8,128)(2,1)}, u32[]{:S(2)}, u32[]{:S(2)}) collective-permute-start(bf16[256,2048]{1,0:T(8,128)(2,1)} %param.22), channel_id=1, source_target_pairs={{0,2},{2,0},{1,3},{3,1},{4,6},{6,4},{5,7},{7,5},{8,10},{10,8},{9,1... | collective-permute-start | bytes 3145736 | tf_op jit(solution)/shard_map/ppermute | solution.py:62
  368.9 109.8 %collective-permute-start.13 = (bf16[640,2048]{1,0:T(8,128)(2,1)}, bf16[640,2048]{1,0:T(8,128)(2,1)}, u32[]{:S(2)}, u32[]{:S(2)}) collective-permute-start(bf16[640,2048]{1,0:T(8,128)(2,1)} %bitcast.23), channel_id=1, source_target_pairs={{0,4},{4,0},{8,12},{12,8},{16,20},{20,16},{24,28},{28,24},{1,5},{5... | collective-permute-start | bytes 7864328 | tf_op jit(solution)/shard_map/ppermute | solution.py:67
  414.2 53.1 %all-to-all-start.4 = ((bf16[4,256,2048]{2,1,0:T(8,128)(2,1)}), bf16[4,256,2048]{2,1,0:T(8,128)(2,1)}, u32[]{:S(2)}, u32[]{:S(2)}) async-start(bf16[4,256,2048]{2,1,0:T(8,128)(2,1)} %broadcast_in_dim.74), calls=%async_computation.4 | async-start | bytes 8388608 | tf_op jit(solution)/shard_map/all_to_all | solution.py:85
  474.3 23.3 %collective-permute-start.12 = (bf16[640,2048]{1,0:T(8,128)(2,1)}, bf16[640,2048]{1,0:T(8,128)(2,1)}, u32[]{:S(2)}, u32[]{:S(2)}) collective-permute-start(bf16[640,2048]{1,0:T(8,128)(2,1)} %bitcast.21), channel_id=1, source_target_pairs={{0,4},{4,0},{8,12},{12,8},{16,20},{20,16},{24,28},{28,24},{1,5},{5... | collective-permute-start | bytes 7864328 | tf_op jit(solution)/shard_map/ppermute | solution.py:67
  497.6 158.7 %collective-permute-start.17 = (bf16[640,2048]{1,0:T(8,128)(2,1)}, bf16[640,2048]{1,0:T(8,128)(2,1)}, u32[]{:S(2)}, u32[]{:S(2)}) collective-permute-start(bf16[640,2048]{1,0:T(8,128)(2,1)} %get-tuple-element.287), channel_id=1, source_target_pairs={{0,4},{4,0},{8,12},{12,8},{16,20},{20,16},{24,28},{28,24},{1,5},{5... | collective-permute-start | bytes 7864328 | tf_op jit(solution)/shard_map/ppermute | solution.py:67
  540.3 22.9 %collective-permute-start.14 = (bf16[640,2048]{1,0:T(8,128)(2,1)}, bf16[640,2048]{1,0:T(8,128)(2,1)}, u32[]{:S(2)}, u32[]{:S(2)}) collective-permute-start(bf16[640,2048]{1,0:T(8,128)(2,1)} %get-tuple-element.292), channel_id=1, source_target_pairs={{0,4},{4,0},{8,12},{12,8},{16,20},{20,16},{24,28},{28,24},{1,5},{5... | collective-permute-start | bytes 7864328 | tf_op jit(solution)/shard_map/ppermute | solution.py:67
  542.6 20.6 %all-to-all-start.5 = ((f32[16,1,256]{2,1,0:T(1,128)}), f32[16,1,256]{2,1,0:T(1,128)S(1)}, u32[]{:S(2)}, u32[]{:S(2)}) async-start(f32[16,1,256]{2,1,0:T(1,128)} %all_to_all.58), calls=%async_computation.5 | async-start | bytes 32768 | tf_op jit(solution)/shard_map/all_to_all | solution.py:525
  570.4 64.8 %all-to-all-start.6 = ((bf16[4,256,2048]{2,1,0:T(8,128)(2,1)}), bf16[4,256,2048]{2,1,0:T(8,128)(2,1)}, u32[]{:S(2)}, u32[]{:S(2)}) async-start(bf16[4,256,2048]{2,1,0:T(8,128)(2,1)} %fusion.59), calls=%async_computation.6 | async-start | bytes 8388608 | tf_op jit(solution)/shard_map/all_to_all | solution.py:85
  575.2 133.6 %reduce-scatter.4.cloned.1.call-start = ((), (), s32[]{:S(2)}) async-start(), calls=%async_computation.19 | async-start | bytes 6291456 | tf_op jit(solution)/shard_map/reduce_scatter | solution.py:403
  611.1 28.3 %collective-permute-start.15 = (bf16[640,2048]{1,0:T(8,128)(2,1)}, bf16[640,2048]{1,0:T(8,128)(2,1)}, u32[]{:S(2)}, u32[]{:S(2)}) collective-permute-start(bf16[640,2048]{1,0:T(8,128)(2,1)} %slice.231), channel_id=1, source_target_pairs={{0,4},{4,0},{8,12},{12,8},{16,20},{20,16},{24,28},{28,24},{1,5},{5... | collective-permute-start | bytes 7864328 | tf_op jit(solution)/shard_map/ppermute | solution.py:67
  614.6 49.1 %collective-permute-start.18 = (bf16[640,2048]{1,0:T(8,128)(2,1)}, bf16[640,2048]{1,0:T(8,128)(2,1)}, u32[]{:S(2)}, u32[]{:S(2)}) collective-permute-start(bf16[640,2048]{1,0:T(8,128)(2,1)} %get-tuple-element.282), channel_id=1, source_target_pairs={{0,4},{4,0},{8,12},{12,8},{16,20},{20,16},{24,28},{28,24},{1,5},{5... | collective-permute-start | bytes 7864328 | tf_op jit(solution)/shard_map/ppermute | solution.py:67
  646.5 56.2 %all-to-all-start.7 = ((bf16[4,256,2048]{2,1,0:T(8,128)(2,1)}), bf16[4,256,2048]{2,1,0:T(8,128)(2,1)}, u32[]{:S(2)}, u32[]{:S(2)}) async-start(bf16[4,256,2048]{2,1,0:T(8,128)(2,1)} %fusion.56), calls=%async_computation.7 | async-start | bytes 8388608 | tf_op jit(solution)/shard_map/all_to_all | solution.py:85
  651.4 126.1 %reduce-scatter.6.cloned.1.call-start = ((), (), s32[]{:S(2)}) async-start(), calls=%async_computation.20 | async-start | bytes 6291456 | tf_op jit(solution)/shard_map/reduce_scatter | solution.py:403
  653.8 48.9 %collective-permute-start.16 = (bf16[256,2048]{1,0:T(8,128)(2,1)}, bf16[256,2048]{1,0:T(8,128)(2,1)}, u32[]{:S(2)}, u32[]{:S(2)}) collective-permute-start(bf16[256,2048]{1,0:T(8,128)(2,1)} %reduce_sum.268), channel_id=1, source_target_pairs={{0,2},{2,0},{1,3},{3,1},{4,6},{6,4},{5,7},{7,5},{8,10},{10,8},{9,1... | collective-permute-start | bytes 3145736 | tf_op jit(solution)/shard_map/ppermute | solution.py:62
  716.2 61.5 %collective-permute-start.19 = (bf16[256,2048]{1,0:T(8,128)(2,1)}, bf16[256,2048]{1,0:T(8,128)(2,1)}, u32[]{:S(2)}, u32[]{:S(2)}) collective-permute-start(bf16[256,2048]{1,0:T(8,128)(2,1)} %get-tuple-element.265), channel_id=1, source_target_pairs={{0,1},{1,0},{2,3},{3,2},{4,5},{5,4},{6,7},{7,6},{8,9},{9,8},{10,11... | collective-permute-start | bytes 3145736 | tf_op jit(solution)/shard_map/ppermute | solution.py:62
  716.8 60.6 %collective-permute-start.20 = (bf16[256,2048]{1,0:T(8,128)(2,1)}, bf16[256,2048]{1,0:T(8,128)(2,1)}, u32[]{:S(2)}, u32[]{:S(2)}) collective-permute-start(bf16[256,2048]{1,0:T(8,128)(2,1)} %get-tuple-element.265), channel_id=1, source_target_pairs={{0,2},{2,0},{1,3},{3,1},{4,6},{6,4},{5,7},{7,5},{8,10},{10,8},{9,1... | collective-permute-start | bytes 3145736 | tf_op jit(solution)/shard_map/ppermute | solution.py:62
  720.2 52.9 %all-to-all-start.8 = ((bf16[4,256,2048]{2,1,0:T(8,128)(2,1)}), bf16[4,256,2048]{2,1,0:T(8,128)(2,1)}, u32[]{:S(2)}, u32[]{:S(2)}) async-start(bf16[4,256,2048]{2,1,0:T(8,128)(2,1)} %fusion.50), calls=%async_computation.9 | async-start | bytes 8388608 | tf_op jit(solution)/shard_map/all_to_all | solution.py:85
  777.4 24.3 %collective-permute-start.21 = (bf16[256,2048]{1,0:T(8,128)(2,1)}, bf16[256,2048]{1,0:T(8,128)(2,1)S(1)}, u32[]{:S(2)}, u32[]{:S(2)}) collective-permute-start(bf16[256,2048]{1,0:T(8,128)(2,1)} %collective-permute-done.20), channel_id=1, source_target_pairs={{0,1},{1,0},{2,3},{3,2},{4,5},{5,4},{6,7},{7,6},{8,9},{9,8},{10,11... | collective-permute-start | bytes 3145736 | tf_op jit(solution)/shard_map/ppermute | solution.py:62
  802.8 31.0 %collective-permute-start.22 = (bf16[1024,512]{1,0:T(8,128)(2,1)}, bf16[1024,512]{1,0:T(8,128)(2,1)}, u32[]{:S(2)}, u32[]{:S(2)}) collective-permute-start(bf16[1024,512]{1,0:T(8,128)(2,1)} %get-tuple-element.197), channel_id=1, source_target_pairs={{0,1},{1,0},{2,3},{3,2},{4,5},{5,4},{6,7},{7,6},{8,9},{9,8},{10,11... | collective-permute-start | bytes 3145736 | tf_op jit(solution)/shard_map/ppermute | solution.py:62
  804.5 59.8 %all-to-all-start.9 = ((bf16[4,256,2048]{2,1,0:T(8,128)(2,1)}), bf16[4,256,2048]{2,1,0:T(8,128)(2,1)}, u32[]{:S(2)}, u32[]{:S(2)}) async-start(bf16[4,256,2048]{2,1,0:T(8,128)(2,1)} %fusion.53), calls=%async_computation.11 | async-start | bytes 8388608 | tf_op jit(solution)/shard_map/all_to_all | solution.py:85
  809.5 100.7 %all-gather.15.cloned.1.call-start = ((), (), s32[]{:S(2)}) async-start(), calls=%async_computation.22 | async-start | bytes 3145728 | tf_op jit(solution)/shard_map/all_gather | solution.py:790
  833.8 5.1 collective-permute-start.23
  839.7 10.3 %collective-permute-start.24 = (f32[2,4,256]{2,0,1:T(2,128)S(1)}, f32[2,4,256]{2,0,1:T(2,128)S(1)}, u32[]{:S(2)}, u32[]{:S(2)}) collective-permute-start(f32[2,4,256]{2,0,1:T(2,128)S(1)} %bitcast_add_fusion), channel_id=1, source_target_pairs={{0,2},{2,0},{1,3},{3,1},{4,6},{6,4},{5,7},{7,5},{8,10},{10,8},{9,1... | collective-permute-start | bytes 24584 | tf_op jit(solution)/shard_map/ppermute | solution.py:62
  867.5 31.0 %collective-permute-start.25 = (bf16[256,2048]{1,0:T(8,128)(2,1)}, bf16[256,2048]{1,0:T(8,128)(2,1)}, u32[]{:S(2)}, u32[]{:S(2)}) collective-permute-start(bf16[256,2048]{1,0:T(8,128)(2,1)} %convolution_convert_fusion.11), channel_id=1, source_target_pairs={{0,1},{1,0},{2,3},{3,2},{4,5},{5,4},{6,7},{7,6},{8,9},{9,8},{10,11... | collective-permute-start | bytes 3145736 | tf_op jit(solution)/shard_map/ppermute | solution.py:62
  867.6 31.0 %all-to-all-start.10 = ((bf16[8,256,512]{2,1,0:T(8,128)(2,1)}), bf16[8,256,512]{2,1,0:T(8,128)(2,1)}, u32[]{:S(2)}, u32[]{:S(2)}) async-start(bf16[8,256,512]{2,1,0:T(8,128)(2,1)} %bitcast.158), calls=%async_computation.12 | async-start | bytes 4194304 | tf_op jit(solution)/shard_map/all_to_all | solution.py:834
  872.0 123.7 %reduce-scatter.8.cloned.1.call-start = ((), (), s32[]{:S(2)}) async-start(), calls=%async_computation.21 | async-start | bytes 7077888 | tf_op jit(solution)/shard_map/reduce_scatter | solution.py:847
  898.7 46.1 %collective-permute-start.26 = (bf16[256,2048]{1,0:T(8,128)(2,1)}, bf16[256,2048]{1,0:T(8,128)(2,1)}, u32[]{:S(2)}, u32[]{:S(2)}) collective-permute-start(bf16[256,2048]{1,0:T(8,128)(2,1)} %convolution_convert_fusion.10), channel_id=1, source_target_pairs={{0,1},{1,0},{2,3},{3,2},{4,5},{5,4},{6,7},{7,6},{8,9},{9,8},{10,11... | collective-permute-start | bytes 3145736 | tf_op jit(solution)/shard_map/ppermute | solution.py:62
  903.9 48.8 %collective-permute-start.27 = (bf16[256,2048]{1,0:T(8,128)(2,1)}, bf16[256,2048]{1,0:T(8,128)(2,1)}, u32[]{:S(2)}, u32[]{:S(2)}) collective-permute-start(bf16[256,2048]{1,0:T(8,128)(2,1)} %add_convert_fusion.2), channel_id=1, source_target_pairs={{0,2},{2,0},{1,3},{3,1},{4,6},{6,4},{5,7},{7,5},{8,10},{10,8},{9,1... | collective-permute-start | bytes 3145736 | tf_op jit(solution)/shard_map/ppermute | solution.py:62
  956.1 17.6 %all-to-all-start.11 = ((f32[32,1,1280]{2,1,0:T(1,128)}), f32[32,1,1280]{2,1,0:T(1,128)S(1)}, u32[]{:S(2)}, u32[]{:S(2)}) async-start(f32[32,1,1280]{2,1,0:T(1,128)} %copy.49), calls=%async_computation.14 | async-start | bytes 327680 | tf_op jit(solution)/shard_map/all_to_all | solution.py:99
  962.1 28.1 %collective-permute-start.28 = (bf16[1024,512]{1,0:T(8,128)(2,1)}, bf16[1024,512]{1,0:T(8,128)(2,1)}, u32[]{:S(2)}, u32[]{:S(2)}) collective-permute-start(bf16[1024,512]{1,0:T(8,128)(2,1)} %get-tuple-element.221), channel_id=1, source_target_pairs={{0,1},{1,0},{2,3},{3,2},{4,5},{5,4},{6,7},{7,6},{8,9},{9,8},{10,11... | collective-permute-start | bytes 3145736 | tf_op jit(solution)/shard_map/ppermute | solution.py:62
  (99 other events, 1192.4 us)
Sparse Core Ops, SparseCore 0:
  10.5 59.1 all-gather.6
  87.7 57.0 all-gather.8
  239.8 80.0 all-gather.10
  361.8 78.7 all-gather.12
  578.0 55.9 reduce-scatter.3
  654.3 111.1 reduce-scatter.5
  813.8 55.4 all-gather.14
  898.8 63.5 reduce-scatter.7

commit v6 on v4

--- a/solution.py
+++ b/solution.py
@@ -845,11 +845,8 @@
     near = swap(near_part, "tensor")
     head_grads = lax.psum_scatter(head_total, "shard", scatter_dimension=0, tiled=True).astype(WIDE)
     if by_blocks:
-        near, across, gate_grad, down_grad, up_late = sync(
-            near, across, gate_grad, down_grad, up_late
-        )
-        up_arrived = jnp.concatenate([up_first, swap(up_late, "tensor")], axis=0)
-        expert_grads = (gate_grad, up_mine + up_arrived.astype(WIDE), down_grad)
+        near, gate_grad, down_grad, up_late = sync(near, gate_grad, down_grad, up_late)
+        up_second = swap(up_late, "tensor")
     out_grad = jnp.sum(
         out_dealt.reshape((lax.axis_size("shard"),) + w_out.shape).astype(WIDE), axis=0
     )
@@ -862,7 +859,12 @@
         one.reshape(device_count, -1)
         for one in (grad_router_weight, grad_gain_first, grad_gain_second, grad_gains[0], grad_gains[1])
     ]
-    small_grads = scatter_small(jnp.concatenate(by_device, axis=1))
+    small_rows = jnp.concatenate(by_device, axis=1)
+    if by_blocks:
+        small_rows, up_second = sync(small_rows, up_second)
+        up_arrived = jnp.concatenate([up_first, up_second], axis=0)
+        expert_grads = (gate_grad, up_mine + up_arrived.astype(WIDE), down_grad)
+    small_grads = scatter_small(small_rows)
     router_grad = small_grads[:router_size].reshape(router_rows, expert_count)
     gain_totals = small_grads[router_size:].reshape(4, router_rows)
     return (

time: 985 us -> 984 us (level)
    unnamed x206 -> x212, local copies, waits for them, and re-layouts: 28.5 us -> 30.6 us
  transfers between devices with their start and end apart: 49 -> 49, of which waited for: 20 -> 21; matrix products, arithmetic and copies ran while one was open for 49% -> 49% of each run, Pallas kernels for 7% -> 7%
where the time goes in v6:
time: 984 us; the launch traced here: 979 us
  matrix products  325 us (33%)
  waiting for transfers between devices  301 us (31%)
  local copies, waits for them, and re-layouts  98.6 us (10%)
  other arithmetic  89.4 us (9%)
  starting transfers between devices  83.9 us (9%)
  Pallas kernels  64 us (7%)
  between operations  16.2 us (2%)
    ppermute x21, waiting for transfers between devices, swap(): return lax.ppermute(values, axis, SWAP)  244 us
    dot_general x23, matrix products, plain(): return jnp.dot(left, right, preferred_element_type=jnp.float32)  104 us
    dot_general x15, matrix products, contract_last(): lax.dot_general(left, right, (((1,), (1,)), ((), ())), preferred_element_...  96.2 us
    dot_general x10, matrix products, contract_first(): lax.dot_general(left, right, (((0,), (0,)), ((), ())), preferred_element_...  81.2 us
    all_to_all x8, starting transfers between devices, over_chips(): lax.all_to_all(blocks, 'shard', split_axis=0, concat_axis=0, axis_index_g...  39.7 us
    unnamed x212, local copies, waits for them, and re-layouts  30.6 us
    all_to_all x8, waiting for transfers between devices, over_chips(): lax.all_to_all(blocks, 'shard', split_axis=0, concat_axis=0, axis_index_g...  29.7 us
    pallas_call x4, Pallas kernels, attend_block_back(): pl.pallas_call(lambda *refs: attend_back_kernel(which, sums is None, *ref...  29.3 us
  transfers between devices with their start and end apart: 49, of which 21 were waited for; matrix products, arithmetic and copies ran while one was open for 49% of the time, Pallas kernels for 7%

profile of v6, /device:TPU:0, one launch (start us, length us, event | category | flops | bytes accessed | tf_op | source)
XLA Modules:
  0.0 978.6 jit_solution(355138773386533603)
XLA Ops:
  31.9 32.0 %collective-permute-done.1 = bf16[256,2048]{1,0:T(8,128)(2,1)S(1)} collective-permute-done((bf16[256,2048]{1,0:T(8,128)(2,1)}, bf16[256,2048]{1,0:T(8,128)(2,1)S(1)}, u32[]{:S(2)}, u32[]{:S(2)}) %collective-permute-start.1) | collective-permute-done | bytes 1048608 | tf_op jit(solution)/shard_map/ppermute | solution.py:62
  69.8 16.3 %collective-permute-done.2 = bf16[256,2048]{1,0:T(8,128)(2,1)} collective-permute-done((bf16[256,2048]{1,0:T(8,128)(2,1)S(1)}, bf16[256,2048]{1,0:T(8,128)(2,1)}, u32[]{:S(2)}, u32[]{:S(2)}) %collective-permute-start.2) | collective-permute-done | bytes 1048608 | tf_op jit(solution)/shard_map/ppermute | solution.py:62
  91.8 5.7 fusion.102
  137.1 7.7 all-gather.9.cloned.1.call-done
  159.8 10.1 %collective-permute-done.5 = bf16[256,2048]{1,0:T(8,128)(2,1)S(1)} collective-permute-done((bf16[256,2048]{1,0:T(8,128)(2,1)}, bf16[256,2048]{1,0:T(8,128)(2,1)S(1)}, u32[]{:S(2)}, u32[]{:S(2)}) %collective-permute-start.5) | collective-permute-done | bytes 1048608 | tf_op jit(solution)/shard_map/ppermute | solution.py:62
  183.3 35.7 %collective-permute-done.7 = bf16[256,2048]{1,0:T(8,128)(2,1)} collective-permute-done((bf16[256,2048]{1,0:T(8,128)(2,1)}, bf16[256,2048]{1,0:T(8,128)(2,1)}, u32[]{:S(2)}, u32[]{:S(2)}) %collective-permute-start.7) | collective-permute-done | bytes 1048608 | tf_op jit(solution)/shard_map/ppermute | solution.py:62
  239.7 44.2 %collective-permute-done.8 = bf16[256,2048]{1,0:T(8,128)(2,1)} collective-permute-done((bf16[256,2048]{1,0:T(8,128)(2,1)}, bf16[256,2048]{1,0:T(8,128)(2,1)}, u32[]{:S(2)}, u32[]{:S(2)}) %collective-permute-start.8) | collective-permute-done | bytes 1048608 | tf_op jit(solution)/shard_map/ppermute | solution.py:62
  303.2 10.5 %fusion.89 = f32[1280,1024]{1,0:T(8,128)} fusion(bf16[2048,1024]{1,0:T(8,128)(2,1)} %all-gather.9.cloned.1.call-done, bf16[640,2048]{1,0:T(8,128)(2,1)} %collective-permute-done.9, bf16[640,2048]{1,0:T(8,128)(2,1)} %bitcast.165), kind=kOutput, calls=%fused_computation.150 | convolution fusion | flops 5379194880 | bytes 14680064 | tf_op jit(solution)/shard_map/dot_general | solution.py:58
  318.4 14.5 %multiply_convert_fusion.5 = (bf16[1280,1024]{1,0:T(8,128)(2,1)}, f32[1280,1024]{1,0:T(8,128)}) fusion(f32[1280,1024]{1,0:T(8,128)} %fusion.89, bf16[2048,1024]{1,0:T(8,128)(2,1)} %all-gather.11.cloned.1.call-done, bf16[640,2048]{1,0:T(8,128)(2,1)} %collective-permute-done.9, bf16[640,2048]{1,0:T(8,128)(2,1)} %bitcast.166), kind=kOutput, calls=%fused_computation.67 | convolution fusion | flops 5387059200 | bytes 22544384 | tf_op jit(solution)/shard_map/dot_general | solution.py:58
  332.9 19.1 %collective-permute-done.10 = bf16[256,2048]{1,0:T(8,128)(2,1)} collective-permute-done((bf16[256,2048]{1,0:T(8,128)(2,1)}, bf16[256,2048]{1,0:T(8,128)(2,1)}, u32[]{:S(2)}, u32[]{:S(2)}) %collective-permute-start.10) | collective-permute-done | bytes 1048608 | tf_op jit(solution)/shard_map/ppermute | solution.py:62
  388.3 8.6 all-gather.13.cloned.1.call-done
  401.2 16.6 %all-to-all-done.4 = bf16[4,256,2048]{2,1,0:T(8,128)(2,1)} async-done(((bf16[4,256,2048]{2,1,0:T(8,128)(2,1)}), bf16[4,256,2048]{2,1,0:T(8,128)(2,1)}, u32[]{:S(2)}, u32[]{:S(2)}) %all-to-all-start.4) | async-done | bytes 4194336 | tf_op jit(solution)/shard_map/all_to_all | solution.py:85
  427.4 10.3 %fusion.3 = (bf16[1280,2048]{1,0:T(8,128)(2,1)}, f32[1280]{0:T(1024)S(1)}, bf16[1280,2048]{1,0:T(8,128)(2,1)}) fusion(f32[1280]{0:T(1024)S(1)} %get-tuple-element.261, bf16[640,2048]{1,0:T(8,128)(2,1)} %collective-permute-done.13, bf16[640,2048]{1,0:T(8,128)(2,1)S(1)} %bitcast.174, bf16[1280,1024]{1,0:T(8,128)(2,1)S(1)} %copy-done.88, ...), kind=kOutput, calls=%fused_computation.17 | convolution fusion | flops 5400165376 | bytes 22554624 | tf_op jit(solution)/shard_map/dot_general | solution.py:46
  439.1 5.9 fusion.165
  445.0 9.4 fusion.178
  457.2 10.7 %fusion.177 = f32[1280,1024]{1,0:T(8,128)} fusion(bf16[1280,2048]{1,0:T(8,128)(2,1)S(1)} %fusion, bf16[2048,1024]{1,0:T(8,128)(2,1)} %all-gather.13.cloned.1.call-done), kind=kOutput, calls=%fused_computation.337 | convolution fusion | flops 5368709120 | bytes 14680064 | tf_op jit(solution)/shard_map/dot_general | solution.py:58
  467.9 12.9 %multiply_convert_fusion.2 = (bf16[1280,1024]{1,0:T(8,128)(2,1)}, bf16[1280,1024]{1,0:T(8,128)(2,1)}, bf16[1280,1024]{1,0:T(8,128)(2,1)S(1)}) fusion(f32[1280,1024]{1,0:T(8,128)} %fusion.178, f32[1280,1024]{1,0:T(8,128)} %fusion.177, bf16[1280,2048]{1,0:T(8,128)(2,1)S(1)} %bitcast.154, bf16[2048,1024]{1,0:T(8,128)(2,1)} %all-gather.11.cloned.1.call-done), kind=kOutput, calls=%fused_computation.62 | convolution fusion | flops 5388369920 | bytes 27787264 | tf_op jit(solution)/shard_map/dot_general | solution.py:58
  480.9 10.9 %fusion.179 = f32[1280,2048]{1,0:T(8,128)} fusion(bf16[1280,1024]{1,0:T(8,128)(2,1)} %get-tuple-element.278, bf16[2048,1024]{1,0:T(8,128)(2,1)S(1)} %copy-done.82), kind=kOutput, calls=%fused_computation.339 | convolution fusion | flops 5368709120 | bytes 17301504 | tf_op jit(solution)/shard_map/dot_general | solution.py:46
  491.7 10.0 %convolution_add_fusion = bf16[1280,2048]{1,0:T(8,128)(2,1)S(1)} fusion(f32[1280,2048]{1,0:T(8,128)} %fusion.179, bf16[1280,1024]{1,0:T(8,128)(2,1)S(1)} %get-tuple-element.172, bf16[2048,1024]{1,0:T(8,128)(2,1)} %all-gather.11.cloned.1.call-done), kind=kOutput, calls=%fused_computation.26 | convolution fusion | flops 5373952000 | bytes 22544384 | tf_op jit(solution)/shard_map/dot_general | solution.py:46
  506.7 9.3 fusion.5
  521.9 16.8 %fusion.45 = bf16[2048,1024]{1,0:T(8,128)(2,1)} fusion(bf16[1280,1024]{1,0:T(8,128)(2,1)} %get-tuple-element.277, bf16[1280,1024]{1,0:T(8,128)(2,1)} %get-tuple-element.150, bf16[1280,2048]{1,0:T(8,128)(2,1)} %copy-done.36, bf16[1280,2048]{1,0:T(8,128)(2,1)} %get-tuple-element.152), kind=kOutput, calls=%fused_computation.91 | convolution fusion | flops 10770972672 | bytes 19922944 | tf_op jit(solution)/shard_map/dot_general | solution.py:52
  538.8 7.2 fusion.59
  551.4 12.8 %multiply_convert_fusion = (bf16[1280,1024]{1,0:T(8,128)(2,1)S(1)}, bf16[1280,1024]{1,0:T(8,128)(2,1)S(1)}) fusion(f32[1280,1024]{1,0:T(8,128)} %fusion.89, f32[1280,1024]{1,0:T(8,128)} %get-tuple-element.326, bf16[1280,2048]{1,0:T(8,128)(2,1)} %get-tuple-element.152, bf16[2048,1024]{1,0:T(8,128)(2,1)} %all-gather.13.cloned.1.call-done), kind=kOutput, calls=%fused_computation.60 | convolution fusion | flops 5385748480 | bytes 25165824 | tf_op jit(solution)/shard_map/dot_general | solution.py:58
  564.3 8.2 fusion.180
  572.5 10.1 %add_convert_fusion = bf16[1280,2048]{1,0:T(8,128)(2,1)} fusion(f32[1280,2048]{1,0:T(8,128)} %fusion.180, bf16[1280,1024]{1,0:T(8,128)(2,1)S(1)} %get-tuple-element.171, bf16[2048,1024]{1,0:T(8,128)(2,1)S(1)} %copy-done.84), kind=kOutput, calls=%fused_computation.25 | convolution fusion | flops 5373952000 | bytes 22544384 | tf_op jit(solution)/shard_map/dot_general | solution.py:46
  590.7 16.2 %fusion.42 = bf16[2048,1024]{1,0:T(8,128)(2,1)} fusion(bf16[1280,1024]{1,0:T(8,128)(2,1)} %get-tuple-element.278, bf16[1280,1024]{1,0:T(8,128)(2,1)} %copy-done.87, bf16[1280,2048]{1,0:T(8,128)(2,1)S(1)} %bitcast.156, bf16[640,2048]{1,0:T(8,128)(2,1)} %collective-permute-done.9, bf16[640,2048]{1,0:T(8,128)(2,1)S(1)} %bitcast.168), kind=kOutput, calls=%fused_computation.90 | convolution fusion | flops 10781458432 | bytes 19922944 | tf_op jit(solution)/shard_map/dot_general | solution.py:52
  614.8 7.1 fusion.56
  631.7 7.3 fusion.53
  639.1 6.3 fusion.50
  647.1 30.9 %collective-permute-done.16 = bf16[256,2048]{1,0:T(8,128)(2,1)} collective-permute-done((bf16[256,2048]{1,0:T(8,128)(2,1)}, bf16[256,2048]{1,0:T(8,128)(2,1)}, u32[]{:S(2)}, u32[]{:S(2)}) %collective-permute-start.16) | collective-permute-done | bytes 1048608 | tf_op jit(solution)/shard_map/ppermute | solution.py:62
  703.1 6.4 shard_map.295
  718.1 8.3 convolution_convert_fusion.7
  726.3 8.5 fusion.63
  734.8 13.1 %all-to-all-done.8 = bf16[4,256,2048]{2,1,0:T(8,128)(2,1)} async-done(((bf16[4,256,2048]{2,1,0:T(8,128)(2,1)}), bf16[4,256,2048]{2,1,0:T(8,128)(2,1)}, u32[]{:S(2)}, u32[]{:S(2)}) %all-to-all-start.8) | async-done | bytes 4194336 | tf_op jit(solution)/shard_map/all_to_all | solution.py:85
  755.1 7.5 shard_map.296
  766.1 7.7 shard_map.297
  794.7 7.7 shard_map.298
  802.5 6.0 shard_map.299
  814.6 7.3 add_convert_fusion.1
  826.7 6.5 shard_map.300
  833.2 5.8 convolution_convert_fusion.11
  846.9 11.2 %convolution_convert_fusion = bf16[2048,1536]{1,0:T(8,128)(2,1)} fusion(bf16[1024,1536]{1,0:T(8,128)(2,1)} %shard_map.300, bf16[256,2048]{1,0:T(8,128)(2,1)} %get-tuple-element.317, bf16[256,2048]{1,0:T(8,128)(2,1)} %get-tuple-element.316, bf16[256,2048]{1,0:T(8,128)(2,1)} %get-tuple-element.315, bf16[256,2048]{1,0:T(8,128)(2,1)S(1)} %copy-done.63), kind=kOutput, calls=%fused_computation.29 | convolution fusion | flops 6462373888 | bytes 13631488 | tf_op jit(solution)/shard_map/dot_general | solution.py:52
  858.1 6.3 fusion.98
  864.4 6.1 fusion.96
  891.6 31.1 %collective-permute-done.26 = bf16[256,2048]{1,0:T(8,128)(2,1)S(1)} collective-permute-done((bf16[256,2048]{1,0:T(8,128)(2,1)}, bf16[256,2048]{1,0:T(8,128)(2,1)S(1)}, u32[]{:S(2)}, u32[]{:S(2)}) %collective-permute-start.26) | collective-permute-done | bytes 1048608 | tf_op jit(solution)/shard_map/ppermute | solution.py:62
  929.0 5.9 collective-permute-done.27
  940.4 11.9 %collective-permute-done.28 = bf16[1024,512]{1,0:T(8,128)(2,1)} collective-permute-done((bf16[1024,512]{1,0:T(8,128)(2,1)}, bf16[1024,512]{1,0:T(8,128)(2,1)}, u32[]{:S(2)}, u32[]{:S(2)}) %collective-permute-start.28) | collective-permute-done | bytes 1048608 | tf_op jit(solution)/shard_map/ppermute | solution.py:62
  953.1 5.6 all-to-all-start.11
  (479 shorter events, 376.2 us)
Async XLA Ops:
  7.2 84.5 %all-gather.7.cloned.1.call-start = ((), (), s32[]{:S(2)}) async-start(), calls=%async_computation.15 | async-start | bytes 9437184 | tf_op jit(solution)/shard_map/all_gather | solution.py:658
  9.6 59.9 %collective-permute-start = (bf16[256,2048]{1,0:T(8,128)(2,1)}, bf16[256,2048]{1,0:T(8,128)(2,1)S(1)}, u32[]{:S(2)}, u32[]{:S(2)}) collective-permute-start(bf16[256,2048]{1,0:T(8,128)(2,1)} %param.21), channel_id=1, source_target_pairs={{0,1},{1,0},{2,3},{3,2},{4,5},{5,4},{6,7},{7,6},{8,9},{9,8},{10,11... | collective-permute-start | bytes 3145736 | tf_op jit(solution)/shard_map/ppermute | solution.py:62
  12.7 51.3 %collective-permute-start.1 = (bf16[256,2048]{1,0:T(8,128)(2,1)}, bf16[256,2048]{1,0:T(8,128)(2,1)S(1)}, u32[]{:S(2)}, u32[]{:S(2)}) collective-permute-start(bf16[256,2048]{1,0:T(8,128)(2,1)} %param.21), channel_id=1, source_target_pairs={{0,2},{2,0},{1,3},{3,1},{4,6},{6,4},{5,7},{7,5},{8,10},{10,8},{9,1... | collective-permute-start | bytes 3145736 | tf_op jit(solution)/shard_map/ppermute | solution.py:62
  24.8 41.6 %all-to-all-start = ((bf16[32,2,1664]{2,1,0:T(2,128)(2,1)}), bf16[32,2,1664]{2,1,0:T(2,128)(2,1)S(1)}, u32[]{:S(2)}, u32[]{:S(2)}) async-start(bf16[32,2,1664]{2,1,0:T(2,128)(2,1)} %reshape.418), calls=%async_computation | async-start | bytes 425984 | tf_op jit(solution)/shard_map/all_to_all | solution.py:99
  27.5 117.3 %all-gather.9.cloned.1.call-start = ((), (), s32[]{:S(2)}) async-start(), calls=%async_computation.16 | async-start | bytes 6291456 | tf_op jit(solution)/shard_map/all_gather | solution.py:412
  64.0 22.1 %collective-permute-start.2 = (bf16[256,2048]{1,0:T(8,128)(2,1)S(1)}, bf16[256,2048]{1,0:T(8,128)(2,1)}, u32[]{:S(2)}, u32[]{:S(2)}) collective-permute-start(bf16[256,2048]{1,0:T(8,128)(2,1)S(1)} %collective-permute-done.1), channel_id=1, source_target_pairs={{0,1},{1,0},{2,3},{3,2},{4,5},{5,4},{6,7},{7,6},{8,9},{9,8},{10,11... | collective-permute-start | bytes 3145736 | tf_op jit(solution)/shard_map/ppermute | solution.py:62
  112.9 8.7 collective-permute-start.4
  116.5 102.5 %all-to-all-start.1 = ((bf16[4,256,2048]{2,1,0:T(8,128)(2,1)}), bf16[4,256,2048]{2,1,0:T(8,128)(2,1)}, u32[]{:S(2)}, u32[]{:S(2)}) async-start(bf16[4,256,2048]{2,1,0:T(8,128)(2,1)} %broadcast_in_dim.68), calls=%async_computation.1 | async-start | bytes 8388608 | tf_op jit(solution)/shard_map/all_to_all | solution.py:85
  144.8 25.1 %collective-permute-start.5 = (bf16[256,2048]{1,0:T(8,128)(2,1)}, bf16[256,2048]{1,0:T(8,128)(2,1)S(1)}, u32[]{:S(2)}, u32[]{:S(2)}) collective-permute-start(bf16[256,2048]{1,0:T(8,128)(2,1)} %convolution_convert_fusion.9), channel_id=1, source_target_pairs={{0,1},{1,0},{2,3},{3,2},{4,5},{5,4},{6,7},{7,6},{8,9},{9,8},{10,11... | collective-permute-start | bytes 3145736 | tf_op jit(solution)/shard_map/ppermute | solution.py:62
  171.2 47.8 %collective-permute-start.7 = (bf16[256,2048]{1,0:T(8,128)(2,1)}, bf16[256,2048]{1,0:T(8,128)(2,1)}, u32[]{:S(2)}, u32[]{:S(2)}) collective-permute-start(bf16[256,2048]{1,0:T(8,128)(2,1)} %add_convert_fusion.3), channel_id=1, source_target_pairs={{0,2},{2,0},{1,3},{3,1},{4,6},{6,4},{5,7},{7,5},{8,10},{10,8},{9,1... | collective-permute-start | bytes 3145736 | tf_op jit(solution)/shard_map/ppermute | solution.py:62
  173.6 46.4 %collective-permute-start.6 = (bf16[256,2048]{1,0:T(8,128)(2,1)}, bf16[256,2048]{1,0:T(8,128)(2,1)}, u32[]{:S(2)}, u32[]{:S(2)}) collective-permute-start(bf16[256,2048]{1,0:T(8,128)(2,1)} %convolution_convert_fusion.8), channel_id=1, source_target_pairs={{0,1},{1,0},{2,3},{3,2},{4,5},{5,4},{6,7},{7,6},{8,9},{9,8},{10,11... | collective-permute-start | bytes 3145736 | tf_op jit(solution)/shard_map/ppermute | solution.py:62
  231.0 52.9 %all-to-all-start.2 = ((bf16[4,256,2048]{2,1,0:T(8,128)(2,1)}), bf16[4,256,2048]{2,1,0:T(8,128)(2,1)}, u32[]{:S(2)}, u32[]{:S(2)}) async-start(bf16[4,256,2048]{2,1,0:T(8,128)(2,1)} %broadcast_in_dim.71), calls=%async_computation.2 | async-start | bytes 8388608 | tf_op jit(solution)/shard_map/all_to_all | solution.py:85
  235.8 82.5 %all-gather.11.cloned.1.call-start = ((), (), s32[]{:S(2)}) async-start(), calls=%async_computation.17 | async-start | bytes 6291456 | tf_op jit(solution)/shard_map/all_gather | solution.py:412
  237.0 46.9 %collective-permute-start.8 = (bf16[256,2048]{1,0:T(8,128)(2,1)}, bf16[256,2048]{1,0:T(8,128)(2,1)}, u32[]{:S(2)}, u32[]{:S(2)}) collective-permute-start(bf16[256,2048]{1,0:T(8,128)(2,1)} %multiply_convert_fusion.6), channel_id=1, source_target_pairs={{0,2},{2,0},{1,3},{3,1},{4,6},{6,4},{5,7},{7,5},{8,10},{10,8},{9,1... | collective-permute-start | bytes 3145736 | tf_op jit(solution)/shard_map/ppermute | solution.py:62
  290.8 12.4 %collective-permute-start.9 = (bf16[640,2048]{1,0:T(8,128)(2,1)}, bf16[640,2048]{1,0:T(8,128)(2,1)}, u32[]{:S(2)}, u32[]{:S(2)}) collective-permute-start(bf16[640,2048]{1,0:T(8,128)(2,1)} %bitcast.17), channel_id=1, source_target_pairs={{0,4},{4,0},{8,12},{12,8},{16,20},{20,16},{24,28},{28,24},{1,5},{5... | collective-permute-start | bytes 7864328 | tf_op jit(solution)/shard_map/ppermute | solution.py:67
  296.3 55.7 %all-to-all-start.3 = ((bf16[4,256,2048]{2,1,0:T(8,128)(2,1)}), bf16[4,256,2048]{2,1,0:T(8,128)(2,1)}, u32[]{:S(2)}, u32[]{:S(2)}) async-start(bf16[4,256,2048]{2,1,0:T(8,128)(2,1)} %broadcast_in_dim.72), calls=%async_computation.3 | async-start | bytes 8388608 | tf_op jit(solution)/shard_map/all_to_all | solution.py:85
  301.1 95.8 %all-gather.13.cloned.1.call-start = ((), (), s32[]{:S(2)}) async-start(), calls=%async_computation.18 | async-start | bytes 6291456 | tf_op jit(solution)/shard_map/all_gather | solution.py:412
  303.2 48.8 %collective-permute-start.10 = (bf16[256,2048]{1,0:T(8,128)(2,1)}, bf16[256,2048]{1,0:T(8,128)(2,1)}, u32[]{:S(2)}, u32[]{:S(2)}) collective-permute-start(bf16[256,2048]{1,0:T(8,128)(2,1)} %param.22), channel_id=1, source_target_pairs={{0,2},{2,0},{1,3},{3,1},{4,6},{6,4},{5,7},{7,5},{8,10},{10,8},{9,1... | collective-permute-start | bytes 3145736 | tf_op jit(solution)/shard_map/ppermute | solution.py:62
  358.9 24.5 %collective-permute-start.11 = (bf16[640,2048]{1,0:T(8,128)(2,1)}, bf16[640,2048]{1,0:T(8,128)(2,1)}, u32[]{:S(2)}, u32[]{:S(2)}) collective-permute-start(bf16[640,2048]{1,0:T(8,128)(2,1)} %bitcast.19), channel_id=1, source_target_pairs={{0,4},{4,0},{8,12},{12,8},{16,20},{20,16},{24,28},{28,24},{1,5},{5... | collective-permute-start | bytes 7864328 | tf_op jit(solution)/shard_map/ppermute | solution.py:67
  364.4 53.4 %all-to-all-start.4 = ((bf16[4,256,2048]{2,1,0:T(8,128)(2,1)}), bf16[4,256,2048]{2,1,0:T(8,128)(2,1)}, u32[]{:S(2)}, u32[]{:S(2)}) async-start(bf16[4,256,2048]{2,1,0:T(8,128)(2,1)} %broadcast_in_dim.74), calls=%async_computation.4 | async-start | bytes 8388608 | tf_op jit(solution)/shard_map/all_to_all | solution.py:85
  379.4 45.7 %collective-permute-start.13 = (bf16[640,2048]{1,0:T(8,128)(2,1)}, bf16[640,2048]{1,0:T(8,128)(2,1)}, u32[]{:S(2)}, u32[]{:S(2)}) collective-permute-start(bf16[640,2048]{1,0:T(8,128)(2,1)} %bitcast.23), channel_id=1, source_target_pairs={{0,4},{4,0},{8,12},{12,8},{16,20},{20,16},{24,28},{28,24},{1,5},{5... | collective-permute-start | bytes 7864328 | tf_op jit(solution)/shard_map/ppermute | solution.py:67
  425.1 29.4 %collective-permute-start.12 = (bf16[640,2048]{1,0:T(8,128)(2,1)}, bf16[640,2048]{1,0:T(8,128)(2,1)}, u32[]{:S(2)}, u32[]{:S(2)}) collective-permute-start(bf16[640,2048]{1,0:T(8,128)(2,1)} %bitcast.21), channel_id=1, source_target_pairs={{0,4},{4,0},{8,12},{12,8},{16,20},{20,16},{24,28},{28,24},{1,5},{5... | collective-permute-start | bytes 7864328 | tf_op jit(solution)/shard_map/ppermute | solution.py:67
  445.0 186.7 %collective-permute-start.17 = (bf16[640,2048]{1,0:T(8,128)(2,1)}, bf16[640,2048]{1,0:T(8,128)(2,1)}, u32[]{:S(2)}, u32[]{:S(2)}) collective-permute-start(bf16[640,2048]{1,0:T(8,128)(2,1)} %get-tuple-element.285), channel_id=1, source_target_pairs={{0,4},{4,0},{8,12},{12,8},{16,20},{20,16},{24,28},{28,24},{1,5},{5... | collective-permute-start | bytes 7864328 | tf_op jit(solution)/shard_map/ppermute | solution.py:67
  504.9 33.9 %collective-permute-start.14 = (bf16[640,2048]{1,0:T(8,128)(2,1)}, bf16[640,2048]{1,0:T(8,128)(2,1)}, u32[]{:S(2)}, u32[]{:S(2)}) collective-permute-start(bf16[640,2048]{1,0:T(8,128)(2,1)} %get-tuple-element.290), channel_id=1, source_target_pairs={{0,4},{4,0},{8,12},{12,8},{16,20},{20,16},{24,28},{28,24},{1,5},{5... | collective-permute-start | bytes 7864328 | tf_op jit(solution)/shard_map/ppermute | solution.py:67
  518.3 20.5 %all-to-all-start.5 = ((f32[16,1,256]{2,1,0:T(1,128)}), f32[16,1,256]{2,1,0:T(1,128)S(1)}, u32[]{:S(2)}, u32[]{:S(2)}) async-start(f32[16,1,256]{2,1,0:T(1,128)} %all_to_all.58), calls=%async_computation.5 | async-start | bytes 32768 | tf_op jit(solution)/shard_map/all_to_all | solution.py:524
  545.9 64.6 %all-to-all-start.6 = ((bf16[4,256,2048]{2,1,0:T(8,128)(2,1)}), bf16[4,256,2048]{2,1,0:T(8,128)(2,1)}, u32[]{:S(2)}, u32[]{:S(2)}) async-start(bf16[4,256,2048]{2,1,0:T(8,128)(2,1)} %fusion.59), calls=%async_computation.6 | async-start | bytes 8388608 | tf_op jit(solution)/shard_map/all_to_all | solution.py:85
  550.8 133.3 %reduce-scatter.4.cloned.1.call-start = ((), (), s32[]{:S(2)}) async-start(), calls=%async_computation.19 | async-start | bytes 6291456 | tf_op jit(solution)/shard_map/reduce_scatter | solution.py:403
  586.3 28.5 %collective-permute-start.15 = (bf16[640,2048]{1,0:T(8,128)(2,1)}, bf16[640,2048]{1,0:T(8,128)(2,1)}, u32[]{:S(2)}, u32[]{:S(2)}) collective-permute-start(bf16[640,2048]{1,0:T(8,128)(2,1)} %slice.231), channel_id=1, source_target_pairs={{0,4},{4,0},{8,12},{12,8},{16,20},{20,16},{24,28},{28,24},{1,5},{5... | collective-permute-start | bytes 7864328 | tf_op jit(solution)/shard_map/ppermute | solution.py:67
  589.8 49.2 %collective-permute-start.18 = (bf16[640,2048]{1,0:T(8,128)(2,1)}, bf16[640,2048]{1,0:T(8,128)(2,1)}, u32[]{:S(2)}, u32[]{:S(2)}) collective-permute-start(bf16[640,2048]{1,0:T(8,128)(2,1)} %get-tuple-element.281), channel_id=1, source_target_pairs={{0,4},{4,0},{8,12},{12,8},{16,20},{20,16},{24,28},{28,24},{1,5},{5... | collective-permute-start | bytes 7864328 | tf_op jit(solution)/shard_map/ppermute | solution.py:67
  621.9 56.1 %all-to-all-start.7 = ((bf16[4,256,2048]{2,1,0:T(8,128)(2,1)}), bf16[4,256,2048]{2,1,0:T(8,128)(2,1)}, u32[]{:S(2)}, u32[]{:S(2)}) async-start(bf16[4,256,2048]{2,1,0:T(8,128)(2,1)} %fusion.56), calls=%async_computation.7 | async-start | bytes 8388608 | tf_op jit(solution)/shard_map/all_to_all | solution.py:85
  626.8 125.4 %reduce-scatter.6.cloned.1.call-start = ((), (), s32[]{:S(2)}) async-start(), calls=%async_computation.20 | async-start | bytes 6291456 | tf_op jit(solution)/shard_map/reduce_scatter | solution.py:403
  629.2 48.8 %collective-permute-start.16 = (bf16[256,2048]{1,0:T(8,128)(2,1)}, bf16[256,2048]{1,0:T(8,128)(2,1)}, u32[]{:S(2)}, u32[]{:S(2)}) collective-permute-start(bf16[256,2048]{1,0:T(8,128)(2,1)} %reduce_sum.268), channel_id=1, source_target_pairs={{0,2},{2,0},{1,3},{3,1},{4,6},{6,4},{5,7},{7,5},{8,10},{10,8},{9,1... | collective-permute-start | bytes 3145736 | tf_op jit(solution)/shard_map/ppermute | solution.py:62
  691.5 60.9 %collective-permute-start.19 = (bf16[256,2048]{1,0:T(8,128)(2,1)}, bf16[256,2048]{1,0:T(8,128)(2,1)}, u32[]{:S(2)}, u32[]{:S(2)}) collective-permute-start(bf16[256,2048]{1,0:T(8,128)(2,1)} %get-tuple-element.263), channel_id=1, source_target_pairs={{0,1},{1,0},{2,3},{3,2},{4,5},{5,4},{6,7},{7,6},{8,9},{9,8},{10,11... | collective-permute-start | bytes 3145736 | tf_op jit(solution)/shard_map/ppermute | solution.py:62
  691.8 60.4 %collective-permute-start.20 = (bf16[256,2048]{1,0:T(8,128)(2,1)}, bf16[256,2048]{1,0:T(8,128)(2,1)}, u32[]{:S(2)}, u32[]{:S(2)}) collective-permute-start(bf16[256,2048]{1,0:T(8,128)(2,1)} %get-tuple-element.263), channel_id=1, source_target_pairs={{0,2},{2,0},{1,3},{3,1},{4,6},{6,4},{5,7},{7,5},{8,10},{10,8},{9,1... | collective-permute-start | bytes 3145736 | tf_op jit(solution)/shard_map/ppermute | solution.py:62
  695.2 52.7 %all-to-all-start.8 = ((bf16[4,256,2048]{2,1,0:T(8,128)(2,1)}), bf16[4,256,2048]{2,1,0:T(8,128)(2,1)}, u32[]{:S(2)}, u32[]{:S(2)}) async-start(bf16[4,256,2048]{2,1,0:T(8,128)(2,1)} %fusion.50), calls=%async_computation.9 | async-start | bytes 8388608 | tf_op jit(solution)/shard_map/all_to_all | solution.py:85
  752.2 24.4 %collective-permute-start.21 = (bf16[256,2048]{1,0:T(8,128)(2,1)}, bf16[256,2048]{1,0:T(8,128)(2,1)S(1)}, u32[]{:S(2)}, u32[]{:S(2)}) collective-permute-start(bf16[256,2048]{1,0:T(8,128)(2,1)} %collective-permute-done.20), channel_id=1, source_target_pairs={{0,1},{1,0},{2,3},{3,2},{4,5},{5,4},{6,7},{7,6},{8,9},{9,8},{10,11... | collective-permute-start | bytes 3145736 | tf_op jit(solution)/shard_map/ppermute | solution.py:62
  777.5 31.1 %collective-permute-start.22 = (bf16[1024,512]{1,0:T(8,128)(2,1)}, bf16[1024,512]{1,0:T(8,128)(2,1)}, u32[]{:S(2)}, u32[]{:S(2)}) collective-permute-start(bf16[1024,512]{1,0:T(8,128)(2,1)} %get-tuple-element.194), channel_id=1, source_target_pairs={{0,1},{1,0},{2,3},{3,2},{4,5},{5,4},{6,7},{7,6},{8,9},{9,8},{10,11... | collective-permute-start | bytes 3145736 | tf_op jit(solution)/shard_map/ppermute | solution.py:62
  779.3 59.8 %all-to-all-start.9 = ((bf16[4,256,2048]{2,1,0:T(8,128)(2,1)}), bf16[4,256,2048]{2,1,0:T(8,128)(2,1)}, u32[]{:S(2)}, u32[]{:S(2)}) async-start(bf16[4,256,2048]{2,1,0:T(8,128)(2,1)} %fusion.53), calls=%async_computation.11 | async-start | bytes 8388608 | tf_op jit(solution)/shard_map/all_to_all | solution.py:85
  784.3 96.4 %all-gather.15.cloned.1.call-start = ((), (), s32[]{:S(2)}) async-start(), calls=%async_computation.22 | async-start | bytes 3145728 | tf_op jit(solution)/shard_map/all_gather | solution.py:789
  808.6 5.1 collective-permute-start.23
  814.5 10.3 %collective-permute-start.24 = (f32[2,4,256]{2,0,1:T(2,128)S(1)}, f32[2,4,256]{2,0,1:T(2,128)S(1)}, u32[]{:S(2)}, u32[]{:S(2)}) collective-permute-start(f32[2,4,256]{2,0,1:T(2,128)S(1)} %bitcast_add_fusion), channel_id=1, source_target_pairs={{0,2},{2,0},{1,3},{3,1},{4,6},{6,4},{5,7},{7,5},{8,10},{10,8},{9,1... | collective-permute-start | bytes 24584 | tf_op jit(solution)/shard_map/ppermute | solution.py:62
  842.3 31.0 %collective-permute-start.25 = (bf16[256,2048]{1,0:T(8,128)(2,1)}, bf16[256,2048]{1,0:T(8,128)(2,1)}, u32[]{:S(2)}, u32[]{:S(2)}) collective-permute-start(bf16[256,2048]{1,0:T(8,128)(2,1)} %convolution_convert_fusion.11), channel_id=1, source_target_pairs={{0,1},{1,0},{2,3},{3,2},{4,5},{5,4},{6,7},{7,6},{8,9},{9,8},{10,11... | collective-permute-start | bytes 3145736 | tf_op jit(solution)/shard_map/ppermute | solution.py:62
  842.4 31.0 %all-to-all-start.10 = ((bf16[8,256,512]{2,1,0:T(8,128)(2,1)}), bf16[8,256,512]{2,1,0:T(8,128)(2,1)}, u32[]{:S(2)}, u32[]{:S(2)}) async-start(bf16[8,256,512]{2,1,0:T(8,128)(2,1)} %bitcast.162), calls=%async_computation.12 | async-start | bytes 4194304 | tf_op jit(solution)/shard_map/all_to_all | solution.py:833
  846.8 122.2 %reduce-scatter.8.cloned.1.call-start = ((), (), s32[]{:S(2)}) async-start(), calls=%async_computation.21 | async-start | bytes 7077888 | tf_op jit(solution)/shard_map/reduce_scatter | solution.py:846
  878.8 43.9 %collective-permute-start.26 = (bf16[256,2048]{1,0:T(8,128)(2,1)}, bf16[256,2048]{1,0:T(8,128)(2,1)S(1)}, u32[]{:S(2)}, u32[]{:S(2)}) collective-permute-start(bf16[256,2048]{1,0:T(8,128)(2,1)} %convolution_convert_fusion.10), channel_id=1, source_target_pairs={{0,1},{1,0},{2,3},{3,2},{4,5},{5,4},{6,7},{7,6},{8,9},{9,8},{10,11... | collective-permute-start | bytes 3145736 | tf_op jit(solution)/shard_map/ppermute | solution.py:62
  886.2 48.7 %collective-permute-start.27 = (bf16[256,2048]{1,0:T(8,128)(2,1)S(1)}, bf16[256,2048]{1,0:T(8,128)(2,1)S(1)}, u32[]{:S(2)}, u32[]{:S(2)}) collective-permute-start(bf16[256,2048]{1,0:T(8,128)(2,1)S(1)} %add_convert_fusion.2), channel_id=1, source_target_pairs={{0,2},{2,0},{1,3},{3,1},{4,6},{6,4},{5,7},{7,5},{8,10},{10,8},{9,1... | collective-permute-start | bytes 3145736 | tf_op jit(solution)/shard_map/ppermute | solution.py:62
  922.6 29.6 %collective-permute-start.28 = (bf16[1024,512]{1,0:T(8,128)(2,1)}, bf16[1024,512]{1,0:T(8,128)(2,1)}, u32[]{:S(2)}, u32[]{:S(2)}) collective-permute-start(bf16[1024,512]{1,0:T(8,128)(2,1)} %get-tuple-element.214), channel_id=1, source_target_pairs={{0,1},{1,0},{2,3},{3,2},{4,5},{5,4},{6,7},{7,6},{8,9},{9,8},{10,11... | collective-permute-start | bytes 3145736 | tf_op jit(solution)/shard_map/ppermute | solution.py:62
  953.1 14.4 %all-to-all-start.11 = ((f32[32,1,1280]{2,1,0:T(1,128)}), f32[32,1,1280]{2,1,0:T(1,128)S(1)}, u32[]{:S(2)}, u32[]{:S(2)}) async-start(f32[32,1,1280]{2,1,0:T(1,128)} %copy.49), calls=%async_computation.14 | async-start | bytes 327680 | tf_op jit(solution)/shard_map/all_to_all | solution.py:99
  (101 other events, 1008.6 us)
Sparse Core Ops, SparseCore 0:
  10.5 59.1 all-gather.6
  87.7 57.0 all-gather.8
  238.2 80.1 all-gather.10
  319.8 77.1 all-gather.12
  553.6 55.8 reduce-scatter.3
  629.7 111.1 reduce-scatter.5
  788.6 55.4 all-gather.14
  873.6 63.4 reduce-scatter.7
